TPU v7x, 32 devices: a whole 2x2x4 slice. The times are simulated.
32 devices in a mesh: dp: 8 (over y, x, core), expert: 4 (over z).
Axes of the slice: x: 2, y: 2, z: 4, core: 2. Of those that a mesh axis runs over, the one named last changes fastest.
Arguments:
- hidden_input: bfloat16 [40960, 768], P(('dp', 'expert')), may hold values from -6 to 6
- gate_carryover: float32 [40960, 8], P(('dp', 'expert')), may hold values from -2.5 to 2.5
- sequence_length: int32 [32, 5], P(('dp', 'expert')), may hold values from 1 to 1024, 1280 in all within a row
- token_stream_place: int32 [32, 1280], P(('dp', 'expert')), may hold values from 0 to 1279, each once within a row
- expert_choice_index: int32 [40960, 2], P(('dp', 'expert')), may hold values from 0 to 7, as said below
- sequence_adapter: int32 [32, 5], P(('dp', 'expert')), may hold values from 0 to 7
- attention_gain: bfloat16 [768], replicated, may hold values from 0.25 to 1.75
- query_key_weight: bfloat16 [768, 2304], P(('dp', 'expert')), may hold values from -0.21875 to 0.21875
- output_weight: bfloat16 [768, 768], P(('dp', 'expert')), may hold values from -0.625 to 0.625
- adapter_in_query: bfloat16 [768, 128], P(('dp', 'expert')), may hold values from -0.21875 to 0.21875
- adapter_out_query: bfloat16 [128, 2304], P(('dp', 'expert')), may hold values from -0.5 to 0.5
- adapter_in_output: bfloat16 [768, 128], P(('dp', 'expert')), may hold values from -0.21875 to 0.21875
- adapter_out_output: bfloat16 [128, 768], P(('dp', 'expert')), may hold values from -1.5 to 1.5
- feedfwd_gain: bfloat16 [768], replicated, may hold values from 0.25 to 1.75
- router_weight: bfloat16 [768, 8], replicated, may hold values from -0.15625 to 0.15625
- constant_gate: bfloat16 [768, 4], replicated, may hold values from -0.21875 to 0.21875
- constant_value: bfloat16 [2, 768], replicated, may hold values from -6 to 6
- gate_upward_weight: bfloat16 [4, 768, 4096], P('expert', 'dp'), may hold values from -0.21875 to 0.21875
- down_weight: bfloat16 [4, 2048, 768], P('expert', 'dp'), may hold values from -1.5 to 1.5
- adapter_in_gate: bfloat16 [4, 768, 128], P('expert', 'dp'), may hold values from -0.21875 to 0.21875
- adapter_out_gate: bfloat16 [4, 128, 4096], P('expert', 'dp'), may hold values from -0.5 to 0.5
- adapter_in_down: bfloat16 [4, 2048, 128], P('expert', 'dp'), may hold values from -0.125 to 0.125
- adapter_out_down: bfloat16 [4, 128, 768], P('expert', 'dp'), may hold values from -6 to 6
- output_gradient: bfloat16 [40960, 768], P(('dp', 'expert')), may hold values from -6 to 6
Outputs:
- out_hidden: bfloat16 [40960, 768], P(('dp', 'expert'))
- grad_hidden: float32 [40960, 768], P(('dp', 'expert'))
- grad_gate_res: float32 [40960, 8], P(('dp', 'expert'))
- grad_a_qkv: float32 [768, 128], P(('dp', 'expert'))
- grad_b_qkv: float32 [128, 2304], P(('dp', 'expert'))
- grad_a_out: float32 [768, 128], P(('dp', 'expert'))
- grad_b_out: float32 [128, 768], P(('dp', 'expert'))
- grad_a_gu: float32 [4, 768, 128], P('expert', 'dp')
- grad_b_gu: float32 [4, 128, 4096], P('expert', 'dp')
- grad_a_down: float32 [4, 2048, 128], P('expert', 'dp')
- grad_b_down: float32 [4, 128, 768], P('expert', 'dp')
Inputs may be any that keep to these rules, and one draw needn't show every extreme that they name: `expert_choice_index`: each row names two different experts. Ids under 4 are feed-forward experts, 4 is the zero expert, 5 the copy expert, 6 and 7 the constant experts. Among the rows of one device no id under 4 appears more than 408 times; on every device of one index of dp some such id appears exactly 408 times.
All inputs are finite; a program needn't handle non-finite values.
Results may differ from a plain program's by a relative error of at most 0.019.
Values may be sent and summed in bfloat16 or wider, within the bound.
A program may use at most 384 MiB of HBM per device.

v0:
```python
import math

import jax
import jax.numpy as jnp
from jax import lax
from jax.sharding import PartitionSpec as P

MODEL_WIDTH = 768
HEAD_COUNT = 12
HEAD_DIM = 64
FEEDFWD_WIDTH = 2048
ADAPTER_RANK = 16
QUERY_BLOCK = 640


EPSILON = 1e-06


def rms_scale(values):
    return lax.rsqrt(jnp.mean(values * values, axis=-1, keepdims=True) + EPSILON)


def norm_back(values, scaling, gain_vec, upstream):
    weighted = upstream * gain_vec
    return scaling * weighted - values * (scaling * scaling * scaling) * jnp.mean(
        values * weighted, axis=-1, keepdims=True
    )


def plain_product(left_arr, right_arr):
    return jnp.dot(left_arr, right_arr, preferred_element_type=jnp.float32)


def product_right_flipped(left_arr, right_arr):
    return lax.dot_general(
        left_arr, right_arr, (((1,), (1,)), ((), ())), preferred_element_type=jnp.float32
    )


def dot_left_t(left_arr, right_arr):
    return lax.dot_general(
        left_arr, right_arr, (((0,), (0,)), ((), ())), preferred_element_type=jnp.float32
    )


def grouped(values):
    return values.reshape((2, values.shape[0] // 2 * values.shape[1]) + values.shape[2:])


def token_layout(order_row, lengths_row, adapter_row):
    row_count = order_row.shape[0]
    seq_count = lengths_row.shape[0]
    seq_ends = jnp.cumsum(lengths_row)
    seq_starts = seq_ends - lengths_row
    stream = jnp.arange(row_count, dtype=jnp.int32)
    seg_stream = jnp.sum((stream[:, None] >= seq_ends[None, :]).astype(jnp.int32), axis=1)
    seg_hot = seg_stream[:, None] == jnp.arange(seq_count, dtype=jnp.int32)[None, :]
    pos_stream = stream - jnp.sum(jnp.where(seg_hot, seq_starts[None, :], 0), axis=1)
    adapt_stream = jnp.sum(jnp.where(seg_hot, adapter_row[None, :], 0), axis=1)
    inverse = jnp.zeros((row_count,), jnp.int32).at[order_row].set(stream)
    return (seg_stream, inverse, pos_stream[order_row], adapt_stream[order_row])


def rope_tables(positions, half_dim):
    freq_vals = jnp.exp(jnp.arange(half_dim, dtype=jnp.float32) * (-math.log(10000.0) / half_dim))
    angles = positions.astype(jnp.float32)[:, None] * freq_vals[None, :]
    return (jnp.cos(angles)[:, None, :], jnp.sin(angles)[:, None, :])


def rotate(values, cosine, sine_vals):
    half_dim = values.shape[-1] // 2
    first_half = values[..., :half_dim]
    second = values[..., half_dim:]
    return jnp.concatenate(
        [first_half * cosine - second * sine_vals, second * cosine + first_half * sine_vals],
        axis=-1,
    )


def rotate_back(grad_vals, cosine, sine_vals):
    half_dim = grad_vals.shape[-1] // 2
    upper_half = grad_vals[..., :half_dim]
    lower_half = grad_vals[..., half_dim:]
    return jnp.concatenate(
        [
            upper_half * cosine + lower_half * sine_vals,
            lower_half * cosine - upper_half * sine_vals,
        ],
        axis=-1,
    )


def adapter_mask_full(adapter_values, adapter_columns):
    return (
        jnp.arange(adapter_columns)[None, :] // ADAPTER_RANK
        == adapter_values.astype(jnp.int32)[:, None]
    ).astype(jnp.float32)


def block_mask(seg_stream, row_start):
    row_count = seg_stream.shape[0]
    query_index = row_start + jnp.arange(QUERY_BLOCK)
    seg_query = lax.dynamic_slice_in_dim(seg_stream, row_start, QUERY_BLOCK, 0)
    key_index = jnp.arange(row_count)
    return (seg_query[:, None] == seg_stream[None, :]) & (
        key_index[None, :] <= query_index[:, None]
    )


def attention_forward(query_rows, key_rows, value_rows, seg_stream, scaling):
    row_count = query_rows.shape[0]

    def one_block(block_num):
        row_start = block_num * QUERY_BLOCK
        query_blk = lax.dynamic_slice_in_dim(query_rows, row_start, QUERY_BLOCK, 0)
        scores = (
            jnp.einsum("qhd,khd->hqk", query_blk, key_rows, preferred_element_type=jnp.float32)
            * scaling
        )
        masked = jnp.where(block_mask(seg_stream, row_start)[None], scores, -1000000000.0)
        row_top = jnp.max(masked, axis=-1, keepdims=True)
        expo_vals = jnp.exp(masked - row_top)
        row_total = jnp.sum(expo_vals, axis=-1, keepdims=True)
        prob_low = (expo_vals / row_total).astype(jnp.bfloat16)
        block_out = jnp.einsum(
            "hqk,khd->qhd", prob_low, value_rows, preferred_element_type=jnp.float32
        )
        return (block_out, (row_top + jnp.log(row_total))[:, :, 0])

    block_outs, block_lse = lax.map(one_block, jnp.arange(row_count // QUERY_BLOCK))
    return (block_outs.reshape(query_rows.shape), block_lse)


def attention_backward(
    query_rows, key_rows, value_rows, dout_rows, lse_blocks, seg_stream, scaling
):
    row_count = query_rows.shape[0]

    def one_block(carried, block_num):
        key_grad, value_grad = carried
        row_start = block_num * QUERY_BLOCK
        query_blk = lax.dynamic_slice_in_dim(query_rows, row_start, QUERY_BLOCK, 0)
        dout_blk = lax.dynamic_slice_in_dim(dout_rows, row_start, QUERY_BLOCK, 0)
        scores = (
            jnp.einsum("qhd,khd->hqk", query_blk, key_rows, preferred_element_type=jnp.float32)
            * scaling
        )
        masked = jnp.where(block_mask(seg_stream, row_start)[None], scores, -1000000000.0)
        prob_vals = jnp.exp(masked - lse_blocks[block_num][:, :, None])
        dprob = jnp.einsum("qhd,khd->hqk", dout_blk, value_rows, preferred_element_type=jnp.float32)
        dscore = (prob_vals * (dprob - jnp.sum(prob_vals * dprob, axis=-1, keepdims=True))).astype(
            jnp.bfloat16
        )
        query_grad = (
            jnp.einsum("hqk,khd->qhd", dscore, key_rows, preferred_element_type=jnp.float32)
            * scaling
        )
        key_grad = (
            key_grad
            + jnp.einsum("hqk,qhd->khd", dscore, query_blk, preferred_element_type=jnp.float32)
            * scaling
        )
        value_grad = value_grad + jnp.einsum(
            "hqk,qhd->khd",
            prob_vals.astype(jnp.bfloat16),
            dout_blk,
            preferred_element_type=jnp.float32,
        )
        return ((key_grad, value_grad), query_grad)

    zero_start = jnp.zeros(key_rows.shape, jnp.float32)
    (key_grad, value_grad), query_blocks = lax.scan(
        one_block, (zero_start, zero_start), jnp.arange(row_count // QUERY_BLOCK)
    )
    return (query_blocks.reshape(query_rows.shape), key_grad, value_grad)


def expert_apply(weight_tuple, row_values, adapter_values):
    (
        gate_weight_local,
        down_weight_local,
        gate_adapter_in,
        gate_adapter_out,
        down_adapter_in,
        down_adapter_out,
    ) = weight_tuple
    row_mask_full = adapter_mask_full(adapter_values, gate_adapter_in.shape[1])
    lowrank_gate = (plain_product(row_values, gate_adapter_in) * row_mask_full).astype(jnp.bfloat16)
    gate_upward = plain_product(row_values, gate_weight_local) + plain_product(
        lowrank_gate, gate_adapter_out
    )
    middle_state = (
        jax.nn.silu(gate_upward[:, :FEEDFWD_WIDTH]) * gate_upward[:, FEEDFWD_WIDTH:]
    ).astype(jnp.bfloat16)
    lowrank_down = (plain_product(middle_state, down_adapter_in) * row_mask_full).astype(
        jnp.bfloat16
    )
    return (
        plain_product(middle_state, down_weight_local)
        + plain_product(lowrank_down, down_adapter_out)
    ).astype(jnp.bfloat16)


def expert_grads(weight_tuple, row_values, adapter_values, grad_result):
    (
        gate_weight_local,
        down_weight_local,
        gate_adapter_in,
        gate_adapter_out,
        down_adapter_in,
        down_adapter_out,
    ) = weight_tuple
    row_mask_full = adapter_mask_full(adapter_values, gate_adapter_in.shape[1])
    lowrank_gate = (plain_product(row_values, gate_adapter_in) * row_mask_full).astype(jnp.bfloat16)
    gate_upward = plain_product(row_values, gate_weight_local) + plain_product(
        lowrank_gate, gate_adapter_out
    )
    gate_part = gate_upward[:, :FEEDFWD_WIDTH]
    up_part = gate_upward[:, FEEDFWD_WIDTH:]
    gate_sig = jax.nn.sigmoid(gate_part)
    silu_vals = gate_part * gate_sig
    middle_state = (silu_vals * up_part).astype(jnp.bfloat16)
    lowrank_down = (plain_product(middle_state, down_adapter_in) * row_mask_full).astype(
        jnp.bfloat16
    )
    grad_lowrank_down = (
        product_right_flipped(grad_result, down_adapter_out) * row_mask_full
    ).astype(jnp.bfloat16)
    d_middle = (
        (
            product_right_flipped(grad_result, down_weight_local)
            + product_right_flipped(grad_lowrank_down, down_adapter_in)
        )
        .astype(jnp.bfloat16)
        .astype(jnp.float32)
    )
    d_gate = d_middle * up_part * gate_sig * (1.0 + gate_part * (1.0 - gate_sig))
    d_up = d_middle * silu_vals
    grad_gate_upward = jnp.concatenate([d_gate, d_up], axis=-1).astype(jnp.bfloat16)
    grad_lowrank_gate = (
        product_right_flipped(grad_gate_upward, gate_adapter_out) * row_mask_full
    ).astype(jnp.bfloat16)
    grad_rows = (
        product_right_flipped(grad_gate_upward, gate_weight_local)
        + product_right_flipped(grad_lowrank_gate, gate_adapter_in)
    ).astype(jnp.bfloat16)
    grad_terms = (
        dot_left_t(row_values, grad_lowrank_gate),
        dot_left_t(lowrank_gate, grad_gate_upward),
        dot_left_t(middle_state, grad_lowrank_down),
        dot_left_t(lowrank_down, grad_result),
    )
    return (grad_rows, grad_terms)


def shards(
    hidden_input,
    gate_carryover,
    sequence_length,
    token_stream_place,
    expert_choice_index,
    sequence_adapter,
    attention_gain,
    query_key_weight,
    output_weight,
    adapter_in_query,
    adapter_out_query,
    adapter_in_output,
    adapter_out_output,
    feedfwd_gain,
    router_weight,
    constant_gate,
    constant_value,
    gate_upward_weight,
    down_weight,
    adapter_in_gate,
    adapter_out_gate,
    adapter_in_down,
    adapter_out_down,
    output_gradient,
):
    tok_rows = hidden_input.shape[0]
    expert_count = lax.axis_size("expert")
    kind_count = expert_count + 4
    capacity = 5 * tok_rows // (2 * kind_count) // 8 * 8 + 8
    buffer_rows = expert_count * capacity
    adapter_columns = adapter_in_query.shape[1]
    scaling = 1.0 / math.sqrt(HEAD_DIM)
    order_row = token_stream_place[0]
    seg_stream, inverse, positions, token_adapter_index = token_layout(
        order_row, sequence_length[0], sequence_adapter[0]
    )
    cosine, sine_vals = rope_tables(positions, HEAD_DIM // 2)
    adapter_col_mask = adapter_mask_full(token_adapter_index, adapter_columns)

    def attention_weights():
        return (
            lax.all_gather(query_key_weight, ("dp", "expert"), axis=0, tiled=True),
            lax.all_gather(output_weight, ("dp", "expert"), axis=0, tiled=True),
            lax.all_gather(adapter_in_query, ("dp", "expert"), axis=0, tiled=True),
            lax.all_gather(adapter_out_query, ("dp", "expert"), axis=0, tiled=True),
            lax.all_gather(adapter_in_output, ("dp", "expert"), axis=0, tiled=True),
            lax.all_gather(adapter_out_output, ("dp", "expert"), axis=0, tiled=True),
        )

    def own_expert():
        return (
            lax.all_gather(gate_upward_weight, "dp", axis=1, tiled=True),
            lax.all_gather(down_weight, "dp", axis=1, tiled=True),
            lax.all_gather(adapter_in_gate, "dp", axis=1, tiled=True),
            lax.all_gather(adapter_out_gate, "dp", axis=1, tiled=True),
            lax.all_gather(adapter_in_down, "dp", axis=1, tiled=True),
            lax.all_gather(adapter_out_down, "dp", axis=1, tiled=True),
        )

    w_qkv_full, w_out_full, qkv_down, qkv_up, out_down, out_up = attention_weights()
    hidden = hidden_input.astype(jnp.float32)
    scale_one = rms_scale(hidden)
    gain_one = attention_gain.astype(jnp.float32)
    act_one = (hidden * scale_one * gain_one).astype(jnp.bfloat16)
    low_qkv = (plain_product(act_one, qkv_down) * adapter_col_mask).astype(jnp.bfloat16)
    qkv_split = (plain_product(act_one, w_qkv_full) + plain_product(low_qkv, qkv_up)).reshape(
        tok_rows, 3, HEAD_COUNT, HEAD_DIM
    )
    query_rows = rotate(qkv_split[:, 0], cosine, sine_vals).astype(jnp.bfloat16)[inverse]
    key_rows = rotate(qkv_split[:, 1], cosine, sine_vals).astype(jnp.bfloat16)[inverse]
    value_rows = qkv_split[:, 2].astype(jnp.bfloat16)[inverse]
    attended, attn_lse = attention_forward(query_rows, key_rows, value_rows, seg_stream, scaling)
    attn_low = attended[order_row].reshape(tok_rows, MODEL_WIDTH).astype(jnp.bfloat16)
    low_out = (plain_product(attn_low, out_down) * adapter_col_mask).astype(jnp.bfloat16)
    residual = hidden + (plain_product(attn_low, w_out_full) + plain_product(low_out, out_up))
    scale_two = rms_scale(residual)
    gain_two = feedfwd_gain.astype(jnp.float32)
    act_two = (residual * scale_two * gain_two).astype(jnp.bfloat16)
    act_two_f = act_two.astype(jnp.float32)
    gate_prob = jax.nn.softmax(plain_product(act_two, router_weight) + gate_carryover, axis=-1)
    choice_hot = (expert_choice_index[:, :, None] == jnp.arange(kind_count)[None, None, :]).astype(
        jnp.float32
    )
    gate_vals = jnp.sum(choice_hot * gate_prob[:, None, :], axis=-1)
    flat_ids = expert_choice_index.reshape(-1)
    expert_hot = (flat_ids[:, None] == jnp.arange(expert_count)[None, :]).astype(jnp.int32)
    slot_rank = jnp.sum((jnp.cumsum(expert_hot, axis=0) - 1) * expert_hot, axis=1)
    slot_dest = jnp.where(flat_ids < expert_count, flat_ids * capacity + slot_rank, buffer_rows)
    choice_index = jnp.arange(2 * tok_rows, dtype=jnp.int32)
    slot_source = (
        jnp.zeros((buffer_rows + 1,), jnp.int32).at[slot_dest].set(choice_index)[:buffer_rows]
    )
    slot_flag = jnp.zeros((buffer_rows + 1,), jnp.int32).at[slot_dest].set(1)[:buffer_rows] == 1
    source_token = slot_source // 2
    send_rows = jnp.where(
        slot_flag[:, None], act_two[source_token], jnp.zeros((), jnp.bfloat16)
    ).reshape(expert_count, capacity, MODEL_WIDTH)
    send_adapt = (
        jnp.where(slot_flag, token_adapter_index[source_token], 0)
        .astype(jnp.bfloat16)
        .reshape(expert_count, capacity)
    )
    own_forward = own_expert()
    own_weights = tuple((stacked_rows[0] for stacked_rows in own_forward))
    rows_in = lax.all_to_all(send_rows, "expert", split_axis=0, concat_axis=0, tiled=True)
    adapt_in = lax.all_to_all(send_adapt, "expert", split_axis=0, concat_axis=0, tiled=True)
    result = lax.map(
        lambda items: expert_apply(own_weights, items[0], items[1]),
        (grouped(rows_in), grouped(adapt_in)),
    )
    result = result.reshape(rows_in.shape)
    returned = lax.all_to_all(result, "expert", split_axis=0, concat_axis=0, tiled=True)
    zero_row = jnp.zeros((1, MODEL_WIDTH), jnp.bfloat16)
    returned_flat = jnp.concatenate([returned.reshape(buffer_rows, MODEL_WIDTH), zero_row], axis=0)
    ffn_vals = returned_flat[slot_dest].astype(jnp.float32).reshape(tok_rows, 2, MODEL_WIDTH)
    const_logits = plain_product(act_two, constant_gate)
    alpha_zero = jax.nn.softmax(const_logits[:, 0:2], axis=-1)
    alpha_one = jax.nn.softmax(const_logits[:, 2:4], axis=-1)
    value_f = constant_value.astype(jnp.float32)
    const_zero = alpha_zero[:, 0:1] * act_two_f + alpha_zero[:, 1:2] * value_f[0][None, :]
    const_one = alpha_one[:, 0:1] * act_two_f + alpha_one[:, 1:2] * value_f[1][None, :]
    is_copy = (expert_choice_index == expert_count + 1).astype(jnp.float32)[:, :, None]
    is_first = (expert_choice_index == expert_count + 2).astype(jnp.float32)[:, :, None]
    is_second = (expert_choice_index == expert_count + 3).astype(jnp.float32)[:, :, None]
    choice_out = (
        ffn_vals
        + is_copy * act_two_f[:, None, :]
        + is_first * const_zero[:, None, :]
        + is_second * const_one[:, None, :]
    )
    output = residual + jnp.sum(gate_vals[:, :, None] * choice_out, axis=1)
    upstream = output_gradient.astype(jnp.float32)
    d_gate_vals = jnp.sum(upstream[:, None, :] * choice_out, axis=-1)
    scaled_up = gate_vals[:, :, None] * upstream[:, None, :]
    grad_send = (
        jnp.where(
            slot_flag[:, None], scaled_up.reshape(2 * tok_rows, MODEL_WIDTH)[slot_source], 0.0
        )
        .astype(jnp.bfloat16)
        .reshape(expert_count, capacity, MODEL_WIDTH)
    )
    own_backward = own_expert()
    own_weights_back = tuple((stacked_rows[0] for stacked_rows in own_backward))
    grad_recv = lax.all_to_all(grad_send, "expert", split_axis=0, concat_axis=0, tiled=True)

    def source_step(carried, items):
        grad_rows, grad_terms = expert_grads(own_weights_back, items[0], items[1], items[2])
        return (jax.tree.map(jnp.add, carried, grad_terms), grad_rows)

    zero_grads = (
        jnp.zeros((MODEL_WIDTH, adapter_columns), jnp.float32),
        jnp.zeros((adapter_columns, 2 * FEEDFWD_WIDTH), jnp.float32),
        jnp.zeros((FEEDFWD_WIDTH, adapter_columns), jnp.float32),
        jnp.zeros((adapter_columns, MODEL_WIDTH), jnp.float32),
    )
    summed, d_rows_all = lax.scan(
        source_step, zero_grads, (grouped(rows_in), grouped(adapt_in), grouped(grad_recv))
    )
    back_grads = lax.all_to_all(
        d_rows_all.reshape(rows_in.shape), "expert", split_axis=0, concat_axis=0, tiled=True
    )
    expert_sums = (summed[0][None], summed[1][None], summed[2][None], summed[3][None])
    expert_owned = (
        lax.psum_scatter(
            expert_sums[0].astype(jnp.bfloat16), "dp", scatter_dimension=1, tiled=True
        ).astype(jnp.float32),
        lax.psum_scatter(
            expert_sums[1].astype(jnp.bfloat16), "dp", scatter_dimension=1, tiled=True
        ).astype(jnp.float32),
        lax.psum_scatter(
            expert_sums[2].astype(jnp.bfloat16), "dp", scatter_dimension=1, tiled=True
        ).astype(jnp.float32),
        lax.psum_scatter(
            expert_sums[3].astype(jnp.bfloat16), "dp", scatter_dimension=1, tiled=True
        ).astype(jnp.float32),
    )
    back_flat = jnp.concatenate([back_grads.reshape(buffer_rows, MODEL_WIDTH), zero_row], axis=0)
    ffn_input_grad = jnp.sum(
        back_flat[slot_dest].astype(jnp.float32).reshape(tok_rows, 2, MODEL_WIDTH), axis=1
    )
    copy_grad = jnp.sum(is_copy * scaled_up, axis=1)
    dout_zero = jnp.sum(is_first * scaled_up, axis=1)
    dout_one = jnp.sum(is_second * scaled_up, axis=1)
    dalpha_zero = jnp.stack(
        [
            jnp.sum(dout_zero * act_two_f, axis=-1),
            jnp.sum(dout_zero * value_f[0][None, :], axis=-1),
        ],
        axis=-1,
    )
    dalpha_one = jnp.stack(
        [jnp.sum(dout_one * act_two_f, axis=-1), jnp.sum(dout_one * value_f[1][None, :], axis=-1)],
        axis=-1,
    )
    dlogit_zero = alpha_zero * (
        dalpha_zero - jnp.sum(alpha_zero * dalpha_zero, axis=-1, keepdims=True)
    )
    dlogit_one = alpha_one * (dalpha_one - jnp.sum(alpha_one * dalpha_one, axis=-1, keepdims=True))
    d_prob = jnp.sum(choice_hot * d_gate_vals[:, :, None], axis=1)
    d_logits = gate_prob * (d_prob - jnp.sum(gate_prob * d_prob, axis=-1, keepdims=True))
    const_term = jnp.dot(
        jnp.concatenate([dlogit_zero, dlogit_one], axis=-1),
        constant_gate.astype(jnp.float32).T,
        precision=lax.Precision.HIGHEST,
    )
    router_term = jnp.dot(
        d_logits, router_weight.astype(jnp.float32).T, precision=lax.Precision.HIGHEST
    )
    d_act_two = (
        ffn_input_grad
        + copy_grad
        + alpha_zero[:, 0:1] * dout_zero
        + alpha_one[:, 0:1] * dout_one
        + const_term
        + router_term
    )
    d_resid = upstream + norm_back(residual, scale_two, gain_two, d_act_two)
    qkv_w_back, out_w_back, qkv_down_back, qkv_up_back, out_down_back, out_up_back = (
        attention_weights()
    )
    d_attn = d_resid.astype(jnp.bfloat16)
    dlow_out = (product_right_flipped(d_attn, out_up_back) * adapter_col_mask).astype(jnp.bfloat16)
    grad_b_out = dot_left_t(low_out, d_attn)
    grad_a_out = dot_left_t(attn_low, dlow_out)
    d_attn_low = (
        product_right_flipped(d_attn, out_w_back) + product_right_flipped(dlow_out, out_down_back)
    ).astype(jnp.bfloat16)
    dout_rows = d_attn_low.reshape(tok_rows, HEAD_COUNT, HEAD_DIM)[inverse]
    query_grad, key_grad, value_grad = attention_backward(
        query_rows, key_rows, value_rows, dout_rows, attn_lse, seg_stream, scaling
    )
    d_qkv = jnp.stack(
        [
            rotate_back(query_grad[order_row], cosine, sine_vals),
            rotate_back(key_grad[order_row], cosine, sine_vals),
            value_grad[order_row],
        ],
        axis=1,
    )
    d_qkv = d_qkv.reshape(tok_rows, 3 * MODEL_WIDTH).astype(jnp.bfloat16)
    dlow_qkv = (product_right_flipped(d_qkv, qkv_up_back) * adapter_col_mask).astype(jnp.bfloat16)
    grad_b_qkv = dot_left_t(low_qkv, d_qkv)
    grad_a_qkv = dot_left_t(act_one, dlow_qkv)
    d_act_one = product_right_flipped(d_qkv, qkv_w_back) + product_right_flipped(
        dlow_qkv, qkv_down_back
    )
    grad_hidden = d_resid + norm_back(hidden, scale_one, gain_one, d_act_one)
    attn_owned = (
        lax.psum_scatter(grad_a_qkv, ("dp", "expert"), scatter_dimension=0, tiled=True),
        lax.psum_scatter(grad_b_qkv, ("dp", "expert"), scatter_dimension=0, tiled=True),
        lax.psum_scatter(grad_a_out, ("dp", "expert"), scatter_dimension=0, tiled=True),
        lax.psum_scatter(grad_b_out, ("dp", "expert"), scatter_dimension=0, tiled=True),
    )
    return (
        output.astype(jnp.bfloat16),
        grad_hidden,
        d_logits,
        attn_owned[0],
        attn_owned[1],
        attn_owned[2],
        attn_owned[3],
        expert_owned[0],
        expert_owned[1],
        expert_owned[2],
        expert_owned[3],
    )


def solution(mesh):
    in_specs = (
        P(("dp", "expert"), None),
        P(("dp", "expert"), None),
        P(("dp", "expert"), None),
        P(("dp", "expert"), None),
        P(("dp", "expert"), None),
        P(("dp", "expert"), None),
        P(),
        P(("dp", "expert"), None),
        P(("dp", "expert"), None),
        P(("dp", "expert"), None),
        P(("dp", "expert"), None),
        P(("dp", "expert"), None),
        P(("dp", "expert"), None),
        P(),
        P(),
        P(),
        P(),
        P("expert", "dp", None),
        P("expert", "dp", None),
        P("expert", "dp", None),
        P("expert", "dp", None),
        P("expert", "dp", None),
        P("expert", "dp", None),
        P(("dp", "expert"), None),
    )
    out_specs = (
        P(("dp", "expert"), None),
        P(("dp", "expert"), None),
        P(("dp", "expert"), None),
        P(("dp", "expert"), None),
        P(("dp", "expert"), None),
        P(("dp", "expert"), None),
        P(("dp", "expert"), None),
        P("expert", "dp", None),
        P("expert", "dp", None),
        P("expert", "dp", None),
        P("expert", "dp", None),
    )
    return jax.shard_map(shards, mesh=mesh, in_specs=in_specs, out_specs=out_specs, check_vma=False)
```

profile of v0, /device:TPU:1, one launch (start us, length us, event | category | flops | bytes accessed | tf_op | source)
XLA Modules:
  0.0 1953.9 jit_solution(11526851656952281423)
XLA Ops:
  76.7 70.1 %all_gather.49 = bf16[768,128]{1,0:T(8,128)(2,1)} all-gather(bf16[24,128]{1,0:T(8,128)(2,1)S(1)} %copy-done.130), channel_id=1, replica_groups=mesh['dp'=8,'expert'=4] {'dp','expert'}, dimensions={0}, use_global_device_ids=true | all-gather | bytes 202752 | tf_op jit(solution)/shard_map/all_gather | solution.py:300
  146.8 70.3 %all_gather.52 = bf16[768,128]{1,0:T(8,128)(2,1)} all-gather(bf16[24,128]{1,0:T(8,128)(2,1)S(1)} %copy-done.131), channel_id=1, replica_groups=mesh['dp'=8,'expert'=4] {'dp','expert'}, dimensions={0}, use_global_device_ids=true | all-gather | bytes 202752 | tf_op jit(solution)/shard_map/all_gather | solution.py:302
  217.2 67.5 %all-gather.1 = bf16[32,4,768]{2,1,0:T(4,128)(2,1)S(1)} all-gather(bf16[1,4,768]{2,1,0:T(4,128)(2,1)S(1)} %bitcast.376), channel_id=1, replica_groups=mesh['dp'=8,'expert'=4] {'dp','expert'}, dimensions={0}, use_global_device_ids=true | all-gather | bytes 202752 | tf_op jit(solution)/shard_map/all_gather | solution.py:303
  285.4 68.5 %all-gather = bf16[32,4,2304]{2,1,0:T(4,128)(2,1)S(1)} all-gather(bf16[1,4,2304]{2,1,0:T(4,128)(2,1)S(1)} %bitcast.374), channel_id=1, replica_groups=mesh['dp'=8,'expert'=4] {'dp','expert'}, dimensions={0}, use_global_device_ids=true | all-gather | bytes 608256 | tf_op jit(solution)/shard_map/all_gather | solution.py:301
  466.2 25.3 %subtract_convert_fusion.2 = (bf16[1280,12,32]{2,1,0:T(8,128)(2,1)S(1)}, bf16[1280,12,32]{2,1,0:T(8,128)(2,1)}, bf16[1280,12,32]{2,1,0:T(8,128)(2,1)}, bf16[1280,12,32]{2,1,0:T(8,128)(2,1)}) fusion(f32[1280,12,64]{2,1,0:T(8,128)} %bitcast.353, f32[1280,32]{1,0:T(8,128)S(1)} %get-tuple-element.892, f32[1280,32]{1,0:T(8,128)S(1)} %get-tuple-element.891, ...), kind=kLoop, calls=%fused_computation.164 | loop fusion | flops 7864320 | bytes 12124160 | tf_op jit(solution)/shard_map/convert.17
  534.6 113.9 %while.64 = (s32[]{:T(128)}, bf16[2,640,12,64]{1,3,2,0:T(8,128)(2,1)}, f32[2,12,640]{2,1,0:T(8,128)S(1)}, s32[2]{0:T(128)S(1)}, s32[1280]{0:T(1024)S(1)}, /*inde...) while((s32[]{:T(128)}, ...), condition=%wide.region_9.10_spmd.clone, body=%wide.region_6.9_spmd.sunk.clone | while | flops 2636997632 | bytes 152030960 | solution.py:130
  536.8 18.3 fusion.372
  555.1 17.9 fusion.373
  593.7 18.3 fusion.372
  780.6 73.0 %while.65 = (s32[]{:T(128)}, bf16[2,816,768]{2,1,0:T(8,128)(2,1)}, bf16[2,816,768]{2,1,0:T(8,128)(2,1)}, bf16[768,4096]{1,0:T(8,128)(2,1)}, bf16[2,816]{1,0:T(2,...) while((s32[]{:T(128)}, bf16[2,816,768]{2,1,0:T(8,128)(2,1)}, ...), condition=%wide.region_20.21_spmd.clone, body=%wide.region_19.20_spmd.sunk.clone | while | flops 9320314880 | bytes 100473720 | solution.py:363
  859.9 127.8 %while.66 = (s32[]{:T(128)}, f32[768,128]{1,0:T(8,128)}, f32[128,4096]{1,0:T(8,128)}, f32[2048,128]{1,0:T(8,128)}, f32[128,768]{1,0:T(8,128)}, /*index=5*/bf16[2...) while((s32[]{:T(128)}, f32[768,128]{1,0:T(8,128)}, ...), condition=%wide.region_27.28_spmd.clone.clone, body=%wide.region_26.27_spmd.clone.sunk.clone | while | flops 17565108224 | bytes 274885472 | solution.py:412
  1018.0 31.0 %all-to-all-done.4 = bf16[4,408,768]{2,1,0:T(8,128)(2,1)} async-done(((bf16[4,408,768]{2,1,0:T(8,128)(2,1)}), bf16[4,408,768]{2,1,0:T(8,128)(2,1)}, u32[]{:S(2)}, u32[]{:S(2)}) %all-to-all-start.4) | async-done | bytes 2506784 | tf_op jit(solution)/shard_map/all_to_all | solution.py:415
  1110.5 60.4 %multiply_reduce_fusion.1 = (f32[1280,2]{1,0:T(8,128)S(1)}, f32[1280,768]{1,0:T(8,128)}, f32[1280,768]{1,0:T(8,128)}, f32[1280,768]{1,0:T(8,128)}, f32[1280,768]{1,0:T(8,128)}) fusion(f32[1280,768]{1,0:T(8,128)} %copy.371, f32[1280,2]{1,0:T(8,128)S(1)} %copy-done.47, f32[1280,2]{1,0:T(8,128)S(1)} %copy-done.53, f32[1280,2]{1,0:T(8,128)S(1)} %copy-done.54, ...), kind=kLoop, calls=%fused_computation.170 | loop fusion | flops 29488640 | bytes 39372800 | tf_op jit(solution)/shard_map/reduce_sum | solution.py:389
  1238.4 253.0 %while.67 = (s32[]{:T(128)}, f32[1280,12,64]{0,2,1:T(8,128)}, f32[1280,12,64]{0,2,1:T(8,128)}, f32[2,640,12,64]{1,3,2,0:T(8,128)}, s32[2]{0:T(128)S(1)}, /*index...) while((s32[]{:T(128)}, f32[1280,12,64]{0,2,1:T(8,128)}, ...), condition=%wide.region_44.45_spmd.clone.clone, body=%wide.region_42.44_spmd.clone.sunk.clone | while | flops 6387786752 | bytes 363579232 | solution.py:172
  1242.9 20.2 %fusion.431 = f32[12,640,1280]{2,1,0:T(8,128)} fusion(bf16[1280,12,64]{0,2,1:T(8,128)(2,1)} %get-tuple-element.1442, bf16[1280,12,64]{0,2,1:T(8,128)(2,1)} %get-tuple-element.1441, s32[]{:T(128)S(6)} %select_n.212), kind=kOutput, calls=%fused_computation.46.clone.1.clone | convolution fusion | flops 1258291200 | bytes 42270724 | tf_op jit(solution)/shard_map/while/body/eval_jaxpr/qhd,khd->hqk/dot_general | solution.py:150
  1263.2 28.5 %multiply_reduce_fusion.14 = (f32[12,640]{1,0:T(8,128)S(1)}, f32[12,640,1280]{2,1,0:T(8,128)}) fusion(f32[12,640,1280]{2,1,0:T(8,128)} %fusion.431, f32[12,640]{1,0:T(8,128)S(1)} %dynamic-slice_bitcast_fusion.3, bf16[1280,12,64]{0,2,1:T(8,128)(2,1)S(1)} %get-tuple-element.1439, bf16[1280,12,64]{0,2,1:T(8,128)(2,1)S(1)} %copy-done.8, ...), kind=kOutput, calls=%fused_computation.35.clone.1.clone | convolution fusion | flops 1307435520 | bytes 82483200 | tf_op jit(solution)/shard_map/while/body/eval_jaxpr/qhd,khd->hqk/dot_general | solution.py:145
  1291.7 31.8 %multiply_convert_fusion.5 = bf16[12,640,1280]{2,1,0:T(8,128)(2,1)} fusion(f32[12,640,1280]{2,1,0:T(8,128)} %get-tuple-element.1290, f32[12,640,1280]{2,1,0:T(8,128)} %fusion.431, f32[12,640]{1,0:T(8,128)S(1)} %get-tuple-element.1291), kind=kLoop, calls=%fused_computation.34.clone.1.clone | loop fusion | flops 29491200 | bytes 98334720 | tf_op jit(solution)/shard_map/while/body/eval_jaxpr/convert_element_type | solution.py:151
  1368.0 20.2 %fusion.431 = f32[12,640,1280]{2,1,0:T(8,128)} fusion(bf16[1280,12,64]{0,2,1:T(8,128)(2,1)} %get-tuple-element.1442, bf16[1280,12,64]{0,2,1:T(8,128)(2,1)} %get-tuple-element.1441, s32[]{:T(128)S(6)} %select_n.212), kind=kOutput, calls=%fused_computation.46.clone.1.clone | convolution fusion | flops 1258291200 | bytes 42270724 | tf_op jit(solution)/shard_map/while/body/eval_jaxpr/qhd,khd->hqk/dot_general | solution.py:150
  1388.3 28.5 %multiply_reduce_fusion.14 = (f32[12,640]{1,0:T(8,128)S(1)}, f32[12,640,1280]{2,1,0:T(8,128)}) fusion(f32[12,640,1280]{2,1,0:T(8,128)} %fusion.431, f32[12,640]{1,0:T(8,128)S(1)} %dynamic-slice_bitcast_fusion.3, bf16[1280,12,64]{0,2,1:T(8,128)(2,1)S(1)} %get-tuple-element.1439, bf16[1280,12,64]{0,2,1:T(8,128)(2,1)S(1)} %copy-done.8, ...), kind=kOutput, calls=%fused_computation.35.clone.1.clone | convolution fusion | flops 1307435520 | bytes 82483200 | tf_op jit(solution)/shard_map/while/body/eval_jaxpr/qhd,khd->hqk/dot_general | solution.py:145
  1416.8 31.8 %multiply_convert_fusion.5 = bf16[12,640,1280]{2,1,0:T(8,128)(2,1)} fusion(f32[12,640,1280]{2,1,0:T(8,128)} %get-tuple-element.1290, f32[12,640,1280]{2,1,0:T(8,128)} %fusion.431, f32[12,640]{1,0:T(8,128)S(1)} %get-tuple-element.1291), kind=kLoop, calls=%fused_computation.34.clone.1.clone | loop fusion | flops 29491200 | bytes 98334720 | tf_op jit(solution)/shard_map/while/body/eval_jaxpr/convert_element_type | solution.py:151
  1556.0 26.9 %add_convert_fusion.4 = (bf16[1280,12,32]{2,1,0:T(8,128)(2,1)}, bf16[1280,12,32]{2,1,0:T(8,128)(2,1)}, bf16[1280,12,32]{2,1,0:T(8,128)(2,1)}, bf16[1280,12,32]{2,1,0:T(8,128)(2,1)}) fusion(f32[1280,12,64]{2,1,0:T(8,128)} %gather_fusion.12, f32[1280,32]{1,0:T(8,128)S(1)} %copy-done.45, f32[1280,32]{1,0:T(8,128)S(1)} %copy-done.43, ...), kind=kLoop, calls=%fused_computation.162 | loop fusion | flops 7864320 | bytes 12124160 | tf_op jit(solution)/shard_map/convert.14
  1660.0 88.4 %all-reduce.9.cloned.1.call-done = (f32[128,2304]{1,0:T(8,128)}, f32[128,768]{1,0:T(8,128)}) async-done(((f32[128,2304]{1,0:T(8,128)}, f32[128,768]{1,0:T(8,128)}), (f32[128,2304]{1,0:T(8,128)}, f32[128,768]{1,0:T(8,128)})) %all-reduce.9.cloned.1.call-update) | async-done | bytes 1572880
  1751.3 96.2 %reduce-scatter.21.cloned.1.call-done = f32[24,128]{1,0:T(8,128)} async-done(((f32[768,128]{1,0:T(8,128)}), f32[24,128]{1,0:T(8,128)}) %reduce-scatter.21.cloned.1.call-update) | async-done | bytes 12304
  1847.4 99.2 %reduce-scatter.19.cloned.1.call-done = f32[24,128]{1,0:T(8,128)} async-done(((f32[768,128]{1,0:T(8,128)}), f32[24,128]{1,0:T(8,128)}) %reduce-scatter.19.cloned.1.call-update) | async-done | bytes 12304
  (680 shorter events, 1009.8 us)
Async XLA Ops:
  7.2 676.3 %copy-start = (bf16[768,8]{0,1:T(8,128)(2,1)S(1)}, bf16[768,8]{0,1:T(8,128)(2,1)}, u32[]{:S(2)}) copy-start(bf16[768,8]{0,1:T(8,128)(2,1)} %param.46) | copy-start | bytes 36868
  7.2 382.6 %all-gather.8.cloned.1.call-start = ((), (), s32[]{:S(2)}) async-start(), calls=%async_computation.11 | async-start | bytes 3649536 | tf_op jit(solution)/shard_map/all_gather | solution.py:298
  8.0 664.3 %all-gather.10.cloned.1.call-start = ((), (), s32[]{:S(2)}) async-start(), calls=%async_computation.12 | async-start | bytes 1216512 | tf_op jit(solution)/shard_map/all_gather | solution.py:299
  8.7 770.2 %all-gather.14.cloned.1.call-start = ((), (), s32[]{:S(2)}) async-start(), calls=%async_computation.14 | async-start | bytes 1179648 | tf_op jit(solution)/shard_map/all_gather | solution.py:311
  9.4 769.5 %all-gather.16.cloned.1.call-start = ((), (), s32[]{:S(2)}) async-start(), calls=%async_computation.15 | async-start | bytes 3538944 | tf_op jit(solution)/shard_map/all_gather | solution.py:309
  44.4 342.6 %copy-start.1 = (s32[1280]{0:T(1024)}, s32[1280]{0:T(1024)S(1)}, u32[]{:S(2)}) copy-start(s32[1280]{0:T(1024)S(1)} %gather_fusion) | copy-start | bytes 15364
  56.1 657.1 %all-to-all-start.1 = ((bf16[4,2,204]{2,1,0:T(2,128)(2,1)}), bf16[4,2,204]{2,1,0:T(2,128)(2,1)}, u32[]{:S(2)}, u32[]{:S(2)}) async-start(bf16[4,2,204]{2,1,0:T(2,128)(2,1)} %reshape.848), calls=%async_computation.1 | async-start | bytes 8192 | tf_op jit(solution)/shard_map/all_to_all | solution.py:362
  61.5 717.5 %all-gather.12.cloned.1.call-start = ((), (), s32[]{:S(2)}) async-start(), calls=%async_computation.13 | async-start | bytes 7077888 | tf_op jit(solution)/shard_map/all_gather | solution.py:308
  62.1 324.9 %copy-start.137 = (s32[128]{0:T(128)}, s32[128]{0:T(128)S(1)}, u32[]{:S(2)}) copy-start(s32[128]{0:T(128)S(1)} %and_select_fusion.2) | copy-start | bytes 1540
  63.7 326.2 %copy-start.126 = (f32[768]{0:T(1024)}, f32[768]{0:T(1024)S(1)}, u32[]{:S(2)}) copy-start(f32[768]{0:T(1024)S(1)} %convert_element_type.276) | copy-start | bytes 9220
  69.5 450.7 %copy-start.86 = (s32[2048]{0:T(1024)}, s32[2048]{0:T(1024)S(1)}, u32[]{:S(2)}) copy-start(s32[2048]{0:T(1024)S(1)} %pad_clamp_fusion.3) | copy-start | bytes 24580
  69.6 147.6 %copy-start.132 = (bf16[4,768]{1,0:T(4,128)(2,1)S(1)}, bf16[4,768]{1,0:T(4,128)(2,1)}, u32[]{:S(2)}) copy-start(bf16[4,768]{1,0:T(4,128)(2,1)} %param.44) | copy-start | bytes 18436
  69.6 215.8 %copy-start.125 = (bf16[4,2304]{1,0:T(4,128)(2,1)S(1)}, bf16[4,2304]{1,0:T(4,128)(2,1)}, u32[]{:S(2)}) copy-start(bf16[4,2304]{1,0:T(4,128)(2,1)} %param.42) | copy-start | bytes 55300
  713.2 61.2 %all-to-all-start = ((bf16[4,408,768]{2,1,0:T(8,128)(2,1)}), bf16[4,408,768]{2,1,0:T(8,128)(2,1)}, u32[]{:S(2)}, u32[]{:S(2)}) async-start(bf16[4,408,768]{2,1,0:T(8,128)(2,1)} %get-tuple-element.900), calls=%async_computation | async-start | bytes 5013504 | tf_op jit(solution)/shard_map/all_to_all | solution.py:361
  774.4 79.2 %all-to-all-start.3 = ((bf16[4,408,768]{2,1,0:T(8,128)(2,1)}), bf16[4,408,768]{2,1,0:T(8,128)(2,1)}, u32[]{:S(2)}, u32[]{:S(2)}) async-start(bf16[4,408,768]{2,1,0:T(8,128)(2,1)} %get-tuple-element.899), calls=%async_computation.3 | async-start | bytes 5013504 | tf_op jit(solution)/shard_map/all_to_all | solution.py:400
  853.6 134.1 %all-to-all-start.2 = ((bf16[4,408,768]{2,1,0:T(8,128)(2,1)}), bf16[4,408,768]{2,1,0:T(8,128)(2,1)}, u32[]{:S(2)}, u32[]{:S(2)}) async-start(bf16[4,408,768]{2,1,0:T(8,128)(2,1)} %bitcast.368), calls=%async_computation.2 | async-start | bytes 5013504 | tf_op jit(solution)/shard_map/all_to_all | solution.py:368
  987.7 61.3 %all-to-all-start.4 = ((bf16[4,408,768]{2,1,0:T(8,128)(2,1)}), bf16[4,408,768]{2,1,0:T(8,128)(2,1)}, u32[]{:S(2)}, u32[]{:S(2)}) async-start(bf16[4,408,768]{2,1,0:T(8,128)(2,1)} %bitcast.367), calls=%async_computation.4 | async-start | bytes 5013504 | tf_op jit(solution)/shard_map/all_to_all | solution.py:415
  992.5 626.5 %reduce-scatter.11.cloned.1.call-start = ((), (), s32[]{:S(2)}) async-start(), calls=%async_computation.16 | async-start | bytes 221184 | tf_op jit(solution)/shard_map/reduce_scatter | solution.py:420
  993.5 626.9 %reduce-scatter.17.cloned.1.call-start = ((), (), s32[]{:S(2)}) async-start(), calls=%async_computation.19 | async-start | bytes 221184 | tf_op jit(solution)/shard_map/reduce_scatter | solution.py:429
  1013.9 607.9 %reduce-scatter.15.cloned.1.call-start = ((), (), s32[]{:S(2)}) async-start(), calls=%async_computation.18 | async-start | bytes 589824 | tf_op jit(solution)/shard_map/reduce_scatter | solution.py:426
  1014.9 608.4 %reduce-scatter.13.cloned.1.call-start = ((), (), s32[]{:S(2)}) async-start(), calls=%async_computation.17 | async-start | bytes 1179648 | tf_op jit(solution)/shard_map/reduce_scatter | solution.py:423
  1016.1 732.3 %all-reduce.9.cloned.1.call-start = ((), (), s32[]{:S(2)}) async-start(), calls=%async_computation.22 | async-start | bytes 3145728
  1618.9 228.5 %reduce-scatter.21.cloned.1.call-start = ((), (), s32[]{:S(2)}) async-start(), calls=%async_computation.21 | async-start | bytes 405504
  1631.0 315.7 %reduce-scatter.19.cloned.1.call-start = ((), (), s32[]{:S(2)}) async-start(), calls=%async_computation.20 | async-start | bytes 405504
  (175 other events, 2011.1 us)
Sparse Core Ops, SparseCore 0:
  10.9 62.6 all-gather.7
  76.4 52.9 all-gather.9
  131.3 22.5 all-gather.13
  155.6 32.3 all-gather.15
  189.8 45.9 all-gather.11
  996.6 34.3 reduce-scatter.10
  1034.3 33.5 reduce-scatter.16
  1070.9 34.1 reduce-scatter.14
  1108.6 36.3 reduce-scatter.12
  1619.0 129.3 all-reduce.8
  1754.7 92.6 reduce-scatter.20
  1852.8 93.8 reduce-scatter.18
where the time goes:
time: 1970 us; the launch traced here: 1950 us
  matrix products  489 us (25%)
  local copies, waits for them, and re-layouts  458 us (23%)
  waiting for transfers between devices  333 us (17%)
  other arithmetic  313 us (16%)
  blocking collectives  311 us (16%)
  starting transfers between devices  24.7 us (1%)
    unnamed x15, waiting for transfers between devices  287 us
    dot_general x22, matrix products, plain_product(): return jnp.dot(left_arr, right_arr, preferred_element_type=jnp.float32)  121 us
    dot_general x4, matrix products, one_block(): jnp.einsum('qhd,khd->hqk', query_blk, key_rows, preferred_element_type=jn...  93.5 us
    dot_general x18, matrix products, product_right_flipped(): lax.dot_general(left_arr, right_arr, (((1,), (1,)), ((), ())), preferred_...  75.7 us
    all_gather x1, blocking collectives, attention_weights(): lax.all_gather(adapter_in_output, ('dp', 'expert'), axis=0, tiled=True)  70.3 us
    all_gather x1, blocking collectives, attention_weights(): lax.all_gather(adapter_in_query, ('dp', 'expert'), axis=0, tiled=True)  70.1 us
    all_gather x1, blocking collectives, attention_weights(): lax.all_gather(adapter_out_query, ('dp', 'expert'), axis=0, tiled=True)  68.5 us
    all_gather x1, blocking collectives, attention_weights(): lax.all_gather(adapter_out_output, ('dp', 'expert'), axis=0, tiled=True)  67.5 us
  transfers between devices with their start and end apart: 17, of which 5 were waited for; matrix products, arithmetic and copies ran while one was open for 64% of the time, Pallas kernels for 0%

commit v1 on v0

v1 whole, which is shorter than its diff:
```python
import functools
import math

import jax
import jax.numpy as jnp
from jax import lax
from jax.experimental import pallas as pl
from jax.experimental.pallas import tpu as pltpu
from jax.sharding import PartitionSpec as P

MODEL_WIDTH = 768
HEAD_COUNT = 12
HEAD_DIM = 64
FEEDFWD_WIDTH = 2048
ADAPTER_RANK = 16
ROW_BLOCK = 256
HIDDEN_BLOCK = 512
LANES = 128
CONST_LANE = 64
CHOICE_LANE = 48
EPSILON = 1e-06
VMEM_BYTES = 60 * 2**20

F32 = jnp.float32
BF16 = jnp.bfloat16


def dot(a, b):
    return jnp.dot(a, b, preferred_element_type=F32)


def dot_nt(a, b):
    return lax.dot_general(a, b, (((1,), (1,)), ((), ())), preferred_element_type=F32)


def dot_tn(a, b):
    return lax.dot_general(a, b, (((0,), (0,)), ((), ())), preferred_element_type=F32)


def iota(shape, dim):
    return lax.broadcasted_iota(jnp.int32, shape, dim)


def hot_matrix(condition):
    return jnp.where(condition, 1.0, 0.0).astype(BF16)


def whole(shape):
    zeros = (0,) * len(shape)
    return pl.BlockSpec(shape, lambda *_: zeros)


def row_spec(width, rows=ROW_BLOCK):
    return pl.BlockSpec((rows, width), lambda i: (i, 0))


def col_spec(rows, width=LANES):
    return pl.BlockSpec((rows, width), lambda j: (0, j))


def sds(shape, dtype):
    return jax.ShapeDtypeStruct(shape, dtype)


def call(body, grid, in_specs, out_specs, out_shape, scratch=(), name=None):
    return pl.pallas_call(
        body,
        grid=grid,
        in_specs=in_specs,
        out_specs=out_specs,
        out_shape=out_shape,
        scratch_shapes=list(scratch),
        compiler_params=pltpu.CompilerParams(vmem_limit_bytes=VMEM_BYTES),
        name=name,
    )


def half_swap(values):
    lane = iota(values.shape, 1)
    up = pltpu.roll(values, 32, 1)
    down = pltpu.roll(values, LANES - 32, 1)
    return jnp.where(lane % HEAD_DIM < HEAD_DIM // 2, down, up)


def lane_value(values, lane_id):
    return jnp.sum(jnp.where(iota(values.shape, 1) == lane_id, values, 0.0), axis=1, keepdims=True)


def proj_in_body(
    place_row, hidden, upstream, small, cosine, sine, mask, gain, w_qkv, a_in, b_out,
    hid_s, dy_s, small_s, act_one, low_qkv, query, key, value,
):
    rows = hid_s.shape[0]
    base = pl.program_id(0) * rows
    perm = hot_matrix(place_row[...] == base + iota((rows, place_row.shape[1]), 0))
    hid = dot(perm, hidden[...])
    hid_s[...] = hid.astype(BF16)
    dy_s[...] = dot(perm, upstream[...]).astype(BF16)
    small_s[...] = dot(perm, small[...])
    scale = lax.rsqrt(jnp.mean(hid * hid, axis=-1, keepdims=True) + EPSILON)
    act = (hid * scale * gain[...]).astype(BF16)
    act_one[...] = act
    low = (dot(act, a_in[...]) * mask[...].astype(F32)).astype(BF16)
    low_qkv[...] = low
    cos, sin = cosine[...], sine[...]
    for out, start, factor in ((query, 0, HEAD_DIM**-0.5), (key, MODEL_WIDTH, 1.0)):
        vals = dot(act, w_qkv[:, start : start + MODEL_WIDTH]) + dot(
            low, b_out[:, start : start + MODEL_WIDTH]
        )
        for c in range(MODEL_WIDTH // LANES):
            piece = vals[:, c * LANES : (c + 1) * LANES]
            turned = (piece * cos + half_swap(piece) * sin).astype(BF16)
            if factor != 1.0:
                turned = turned * jnp.asarray(factor, BF16)
            out[:, c * LANES : (c + 1) * LANES] = turned
    value[...] = (
        dot(act, w_qkv[:, 2 * MODEL_WIDTH :]) + dot(low, b_out[:, 2 * MODEL_WIDTH :])
    ).astype(BF16)


def head_mask(shape, head):
    lane = iota(shape, 1)
    return (lane >= head * HEAD_DIM) & (lane < (head + 1) * HEAD_DIM)


def attention_fwd_body(query, key, value, starts, attended, lse):
    tok = query.shape[0]
    size = ROW_BLOCK
    zero = jnp.zeros((), BF16)
    for blk in range(tok // size):
        lo, hi = blk * size, (blk + 1) * size
        q_blk = query[lo:hi, :]
        k_all = key[:hi, :]
        v_all = value[:hi, :]
        begin = starts[lo:hi, :]
        col = iota((size, hi), 1)
        allowed = (col <= lo + iota((size, hi), 0)) & (col >= begin)
        total = jnp.zeros((size, LANES), F32)
        stats = jnp.zeros((size, LANES), F32)
        for head in range(2):
            mine = head_mask((size, LANES), head)
            scores = dot_nt(jnp.where(mine, q_blk, zero), k_all)
            scores = jnp.where(allowed, scores, -1000000000.0)
            top = jnp.max(scores, axis=1, keepdims=True)
            expo = jnp.exp(scores - top)
            norm = jnp.sum(expo, axis=1, keepdims=True)
            v_head = jnp.where(head_mask((hi, LANES), head), v_all, zero)
            total = total + dot(expo.astype(BF16), v_head) * (1.0 / norm)
            stats = jnp.where(mine, top + jnp.log(norm), stats)
        attended[lo:hi, :] = total.astype(BF16)
        lse[lo:hi, :] = stats


def attention_bwd_body(
    query, key, value, dout, attended, lse, starts, cosine, sine, d_query, d_key, d_value, kacc, vacc
):
    tok = query.shape[0]
    size = ROW_BLOCK
    zero = jnp.zeros((), BF16)
    kacc[...] = jnp.zeros_like(kacc)
    vacc[...] = jnp.zeros_like(vacc)
    for blk in range(tok // size):
        lo, hi = blk * size, (blk + 1) * size
        q_blk = query[lo:hi, :]
        do_blk = dout[lo:hi, :]
        k_all = key[:hi, :]
        v_all = value[:hi, :]
        begin = starts[lo:hi, :]
        col = iota((size, hi), 1)
        allowed = (col <= lo + iota((size, hi), 0)) & (col >= begin)
        prod = do_blk.astype(F32) * attended[lo:hi, :].astype(F32)
        q_total = jnp.zeros((size, LANES), F32)
        for head in range(2):
            mine = head_mask((size, LANES), head)
            q_head = jnp.where(mine, q_blk, zero)
            do_head = jnp.where(mine, do_blk, zero)
            lse_head = lse[lo:hi, head * HEAD_DIM : head * HEAD_DIM + 1]
            delta = jnp.sum(jnp.where(mine, prod, 0.0), axis=1, keepdims=True)
            scores = dot_nt(q_head, k_all)
            prob = jnp.where(allowed, jnp.exp(jnp.minimum(scores - lse_head, 0.0)), 0.0)
            dprob = dot_nt(do_head, v_all)
            dscore = (prob * (dprob - delta)).astype(BF16)
            k_head = jnp.where(head_mask((hi, LANES), head), k_all, zero)
            q_total = q_total + dot(dscore, k_head)
            kacc[:hi, :] += dot_tn(dscore, q_head)
            vacc[:hi, :] += dot_tn(prob.astype(BF16), do_head)
        q_total = q_total * HEAD_DIM**-0.5
        d_query[lo:hi, :] = (
            q_total * cosine[lo:hi, :] - half_swap(q_total) * sine[lo:hi, :]
        ).astype(BF16)
    for blk in range(tok // size):
        lo, hi = blk * size, (blk + 1) * size
        k_total = kacc[lo:hi, :]
        d_key[lo:hi, :] = (
            k_total * cosine[lo:hi, :] - half_swap(k_total) * sine[lo:hi, :]
        ).astype(BF16)
    d_value[...] = vacc[...].astype(BF16)


def post_attn_body(
    kinds, attn_low, hid_s, mask, small_s, w_out, a_out, b_out, router, gain,
    low_out, resid, act_two, gate,
):
    attn = attn_low[...]
    low = (dot(attn, a_out[...]) * mask[...].astype(F32)).astype(BF16)
    low_out[...] = low
    res = hid_s[...].astype(F32) + (dot(attn, w_out[...]) + dot(low, b_out[...]))
    resid[...] = res
    scale = lax.rsqrt(jnp.mean(res * res, axis=-1, keepdims=True) + EPSILON)
    act = (res * scale * gain[...]).astype(BF16)
    act_two[...] = act
    sm = small_s[...]
    carry = sm + (pltpu.roll(sm, LANES - 16, 1) + pltpu.roll(sm, LANES - 32, 1))
    logits = dot(act, router[...])
    lane = iota(logits.shape, 1)
    routed = jnp.where(lane < kinds, logits + carry, -1e30)
    top = jnp.max(routed, axis=1, keepdims=True)
    expo = jnp.exp(routed - top)
    prob = expo / jnp.sum(expo, axis=1, keepdims=True)
    gate[...] = jnp.where(lane < kinds, prob, logits)


def dispatch_body(experts, eids, small_s, gate, act_two, dy_s, mask, slot, sent, slot_rows):
    tok = act_two.shape[0]
    cap = sent.shape[1]
    step = pl.program_id(0)

    @pl.when(step == 0)
    def _():
        lane = iota((tok, LANES), 1)
        first = small_s[:, CHOICE_LANE : CHOICE_LANE + 1].astype(jnp.int32)
        second = small_s[:, CHOICE_LANE + 1 : CHOICE_LANE + 2].astype(jnp.int32)
        hot = ((first == lane) | (second == lane)) & (lane < experts)
        hot_low = hot_matrix(hot)
        for blk in range(tok // ROW_BLOCK):
            lo, hi = blk * ROW_BLOCK, (blk + 1) * ROW_BLOCK
            tri = hot_matrix(iota((ROW_BLOCK, hi), 1) < lo + iota((ROW_BLOCK, hi), 0))
            rank = dot(tri, hot_low[:hi, :])
            slot[lo:hi, :] = jnp.where(hot[lo:hi, :], rank, -1.0)
        slot_rows[...] = slot[...].T

    eid = eids[step]
    row = slot_rows[pl.ds(eid, 1), :].astype(jnp.int32)
    pick = hot_matrix(row == iota((cap, tok), 0))
    value = lane_value(gate[...], eid)
    scaled = (dy_s[...].astype(F32) * value).astype(BF16)
    sent[0, :, :MODEL_WIDTH] = dot(pick, act_two[...]).astype(BF16)
    sent[0, :, MODEL_WIDTH : 2 * MODEL_WIDTH] = dot(pick, scaled).astype(BF16)
    sent[0, :, 2 * MODEL_WIDTH :] = dot(pick, mask[...]).astype(BF16)


def ffn_body(
    came, w_gu, w_dn, a_gu, b_gu, a_dn, b_dn,
    back, ga_gu, gb_gu, ga_dn, gb_dn, acc_out, acc_dx, acc_low, acc_dlow,
):
    @pl.when(pl.program_id(0) == 0)
    def _():
        for ref in (ga_gu, gb_gu, ga_dn, gb_dn):
            ref[...] = jnp.zeros_like(ref)

    rows = came[0, :, :MODEL_WIDTH]
    d_out = came[0, :, MODEL_WIDTH : 2 * MODEL_WIDTH]
    mask = came[0, :, 2 * MODEL_WIDTH :].astype(F32)
    low_gu = (dot(rows, a_gu[...]) * mask).astype(BF16)
    dlow_dn = (dot_nt(d_out, b_dn[...]) * mask).astype(BF16)
    for ref in (acc_out, acc_dx, acc_low, acc_dlow):
        ref[...] = jnp.zeros_like(ref)

    def step(j, carry):
        lo = pl.multiple_of(j * HIDDEN_BLOCK, HIDDEN_BLOCK)
        g_cols = pl.ds(lo, HIDDEN_BLOCK)
        u_cols = pl.ds(pl.multiple_of(FEEDFWD_WIDTH + lo, HIDDEN_BLOCK), HIDDEN_BLOCK)
        gate = dot(rows, w_gu[:, g_cols]) + dot(low_gu, b_gu[:, g_cols])
        up = dot(rows, w_gu[:, u_cols]) + dot(low_gu, b_gu[:, u_cols])
        sig = 1.0 / (1.0 + jnp.exp(-gate))
        silu = gate * sig
        middle = (silu * up).astype(BF16)
        acc_out[...] += dot(middle, w_dn[g_cols, :])
        acc_low[...] += dot(middle, a_dn[g_cols, :])
        d_mid = dot_nt(d_out, w_dn[g_cols, :]) + dot_nt(dlow_dn, a_dn[g_cols, :])
        d_mid = d_mid.astype(BF16).astype(F32)
        d_gate = (d_mid * up * (sig * (1.0 + gate * (1.0 - sig)))).astype(BF16)
        d_up = (d_mid * silu).astype(BF16)
        acc_dx[...] += dot_nt(d_gate, w_gu[:, g_cols]) + dot_nt(d_up, w_gu[:, u_cols])
        acc_dlow[...] += dot_nt(d_gate, b_gu[:, g_cols]) + dot_nt(d_up, b_gu[:, u_cols])
        gb_gu[:, g_cols] += dot_tn(low_gu, d_gate)
        gb_gu[:, u_cols] += dot_tn(low_gu, d_up)
        ga_dn[g_cols, :] += dot_tn(middle, dlow_dn)
        return carry

    lax.fori_loop(0, FEEDFWD_WIDTH // HIDDEN_BLOCK, step, 0)
    low_dn = (acc_low[...] * mask).astype(BF16)
    back[0, :, :MODEL_WIDTH] = (acc_out[...] + dot(low_dn, b_dn[...])).astype(BF16)
    gb_dn[...] += dot_tn(low_dn, d_out)
    dlow_gu = (acc_dlow[...] * mask).astype(BF16)
    back[0, :, MODEL_WIDTH:] = (acc_dx[...] + dot_nt(dlow_gu, a_gu[...])).astype(BF16)
    ga_gu[...] += dot_tn(rows, dlow_gu)


def combine_body(
    experts, kinds, eids, resid, act_two, dy_s, gate, slot, small_s, low_out, attn_low, mask, came,
    w_out, a_out, b_out, router, const_value, gain,
    out_s, d_resid, d_attended, d_logits, ga_out, gb_out,
):
    @pl.when(pl.program_id(0) == 0)
    def _():
        ga_out[...] = jnp.zeros_like(ga_out)
        gb_out[...] = jnp.zeros_like(gb_out)

    rows = resid.shape[0]
    cap = came.shape[1]
    res = resid[...]
    act = act_two[...].astype(F32)
    dy = dy_s[...].astype(F32)
    prob = gate[...]
    lane = iota((rows, LANES), 1)
    out = res
    d_act = jnp.zeros((rows, MODEL_WIDTH), F32)
    d_gate = jnp.zeros((rows, LANES), F32)
    for k in range(came.shape[0]):
        eid = eids[k]
        place = lane_value(slot[...], eid).astype(jnp.int32)
        pick = hot_matrix(place == iota((rows, cap), 1))
        result = dot(pick, came[k, :, :MODEL_WIDTH])
        d_act = d_act + dot(pick, came[k, :, MODEL_WIDTH:])
        d_gate = jnp.where(lane == eid, jnp.sum(dy * result, axis=1, keepdims=True), d_gate)
        out = out + lane_value(prob, eid) * result
    sm = small_s[...]
    first = sm[:, CHOICE_LANE : CHOICE_LANE + 1]
    second = sm[:, CHOICE_LANE + 1 : CHOICE_LANE + 2]

    def chosen(kind):
        return jnp.where((first == kind) | (second == kind), 1.0, 0.0)

    has_copy, has_zero, has_one = chosen(experts + 1), chosen(experts + 2), chosen(experts + 3)
    g_copy = has_copy * prob[:, experts + 1 : experts + 2]
    g_zero = has_zero * prob[:, experts + 2 : experts + 3]
    g_one = has_one * prob[:, experts + 3 : experts + 4]

    def pair(at):
        left, right = prob[:, at : at + 1], prob[:, at + 1 : at + 2]
        top = jnp.maximum(left, right)
        e_left, e_right = jnp.exp(left - top), jnp.exp(right - top)
        return e_left / (e_left + e_right), e_right / (e_left + e_right)

    a00, a01 = pair(CONST_LANE)
    a10, a11 = pair(CONST_LANE + 2)
    v_zero, v_one = const_value[0:1, :], const_value[1:2, :]
    along_act = jnp.sum(dy * act, axis=1, keepdims=True)
    along_zero = jnp.sum(dy * v_zero, axis=1, keepdims=True)
    along_one = jnp.sum(dy * v_one, axis=1, keepdims=True)
    coef = g_copy + g_zero * a00 + g_one * a10
    out = out + coef * act + (g_zero * a01) * v_zero + (g_one * a11) * v_one
    out_s[...] = out.astype(BF16)
    d_gate = jnp.where(lane == experts + 1, has_copy * along_act, d_gate)
    d_gate = jnp.where(
        lane == experts + 2, has_zero * (a00 * along_act + a01 * along_zero), d_gate
    )
    d_gate = jnp.where(lane == experts + 3, has_one * (a10 * along_act + a11 * along_one), d_gate)
    prob = jnp.where(lane < kinds, prob, 0.0)
    d_logit = prob * (d_gate - jnp.sum(prob * d_gate, axis=1, keepdims=True))
    d_logits[...] = d_logit
    mix = d_logit
    for at, g_val, left, right, along in (
        (CONST_LANE, g_zero, a00, a01, along_zero),
        (CONST_LANE + 2, g_one, a10, a11, along_one),
    ):
        da_left, da_right = g_val * along_act, g_val * along
        level = left * da_left + right * da_right
        mix = jnp.where(lane == at, left * (da_left - level), mix)
        mix = jnp.where(lane == at + 1, right * (da_right - level), mix)
    mix_hi = mix.astype(BF16)
    mix_lo = (mix - mix_hi.astype(F32)).astype(BF16)
    d_act = d_act + coef * dy + (dot_nt(mix_hi, router[...]) + dot_nt(mix_lo, router[...]))
    scale = lax.rsqrt(jnp.mean(res * res, axis=-1, keepdims=True) + EPSILON)
    weighted = d_act * gain[...]
    d_res = dy + (
        scale * weighted
        - res * (scale * scale * scale) * jnp.mean(res * weighted, axis=-1, keepdims=True)
    )
    d_resid[...] = d_res
    d_attn = d_res.astype(BF16)
    dlow = (dot_nt(d_attn, b_out[...]) * mask[...].astype(F32)).astype(BF16)
    gb_out[...] += dot_tn(low_out[...], d_attn)
    ga_out[...] += dot_tn(attn_low[...], dlow)
    d_attended[...] = (dot_nt(d_attn, w_out[...]) + dot_nt(dlow, a_out[...])).astype(BF16)


def input_grad_body(
    d_query, d_key, d_value, low_qkv, act_one, mask, hid_s, d_resid, w_qkv, a_in, b_out, gain,
    high, lower, ga_qkv, gb_qkv,
):
    @pl.when(pl.program_id(0) == 0)
    def _():
        ga_qkv[...] = jnp.zeros_like(ga_qkv)
        gb_qkv[...] = jnp.zeros_like(gb_qkv)

    d_low = jnp.zeros((d_query.shape[0], LANES), F32)
    d_act = jnp.zeros((d_query.shape[0], MODEL_WIDTH), F32)
    for part, ref in enumerate((d_query, d_key, d_value)):
        cols = slice(part * MODEL_WIDTH, (part + 1) * MODEL_WIDTH)
        grad = ref[...]
        d_low = d_low + dot_nt(grad, b_out[:, cols])
        d_act = d_act + dot_nt(grad, w_qkv[:, cols])
        gb_qkv[:, cols] += dot_tn(low_qkv[...], grad)
    d_low = (d_low * mask[...].astype(F32)).astype(BF16)
    ga_qkv[...] += dot_tn(act_one[...], d_low)
    d_act = d_act + dot_nt(d_low, a_in[...])
    hid = hid_s[...].astype(F32)
    scale = lax.rsqrt(jnp.mean(hid * hid, axis=-1, keepdims=True) + EPSILON)
    weighted = d_act * gain[...]
    grad_hid = d_resid[...] + (
        scale * weighted
        - hid * (scale * scale * scale) * jnp.mean(hid * weighted, axis=-1, keepdims=True)
    )
    top = grad_hid.astype(BF16)
    high[...] = top
    lower[...] = (grad_hid - top.astype(F32)).astype(BF16)


def to_rows_body(place_col, out_s, d_logits, high, lower, out, grad_hidden, grad_gate):
    rows = out.shape[0]
    tok = out_s.shape[0]
    perm = hot_matrix(place_col[...] == iota((rows, tok), 1))
    out[...] = dot(perm, out_s[...]).astype(BF16)
    grad_hidden[...] = dot(perm, high[...]) + dot(perm, lower[...])
    logits = d_logits[...]
    top = logits.astype(BF16)
    rest = logits - top.astype(F32)
    mid = rest.astype(BF16)
    last = (rest - mid.astype(F32)).astype(BF16)
    grad_gate[...] = dot(perm, top) + (dot(perm, mid) + dot(perm, last))


def split_three(values):
    top = values.astype(BF16)
    rest = values - top.astype(F32)
    mid = rest.astype(BF16)
    return top, mid, (rest - mid.astype(F32)).astype(BF16)


class PairPlan:
    def __init__(self, dp, ex):
        self.axes = ("dp", "expert")
        self.dp, self.ex = dp, ex
        self.h = lax.axis_index("dp") & 1
        self.z = lax.axis_index("expert")
        self.own = (self.z & 1) + 2 * self.h
        self.local = (self.z >> 1) == self.h
        self.groups = [[2 * m + h for m in range(dp // 2)] for h in range(2)]

    def send(self, values, target):
        pairs = []
        for d in range(self.dp):
            for z in range(self.ex):
                goal = target(d, z)
                if goal is not None:
                    pairs.append((d * self.ex + z, goal[0] * self.ex + goal[1]))
        return lax.ppermute(values, self.axes, pairs)

    def gather(self, shard):
        near = self.send(shard, lambda d, z: (d, z ^ 2) if (z >> 1) == (d & 1) else None)
        cross = self.send(shard, lambda d, z: (d ^ 1, z ^ 2) if (z >> 1) != (d & 1) else None)
        over = self.send(shard, lambda d, z: (d ^ 1, z) if (z >> 1) != (d & 1) else None)
        mine = jnp.where(self.local, shard, near)
        other = jnp.where(self.local, over, cross)
        both = jnp.stack([jnp.where(self.h == 0, mine, other), jnp.where(self.h == 0, other, mine)])
        return lax.all_gather(both, "dp", axis=0, tiled=True, axis_index_groups=self.groups)

    def expert_ids(self):
        return self.own ^ jnp.arange(self.ex, dtype=jnp.int32)

    def exchange(self, values):
        moves = (
            lambda d, z: (d, z ^ 1),
            lambda d, z: (d ^ 1, z),
            lambda d, z: (d ^ 1, z ^ 1),
        )
        parts = [values[0]] + [self.send(values[k + 1], moves[k]) for k in range(3)]
        return jnp.stack(parts)

    def reduce(self, sums):
        part = lax.psum_scatter(
            sums, "dp", scatter_dimension=0, tiled=True, axis_index_groups=self.groups
        )
        same = jnp.where(self.h == 0, part[0], part[1])
        flip = jnp.where(self.h == 0, part[1], part[0])
        over = self.send(flip, lambda d, z: (d ^ 1, z) if (z >> 1) == (d & 1) else None)
        near = self.send(same, lambda d, z: (d, z ^ 2) if (z >> 1) != (d & 1) else None)
        cross = self.send(flip, lambda d, z: (d ^ 1, z ^ 2) if (z >> 1) != (d & 1) else None)
        first = jnp.where(self.local, same, over).astype(F32)
        return first + near.astype(F32) + cross.astype(F32)

    def reduce_all(self, sums):
        values = sums.reshape((self.dp // 2, 2, self.ex) + sums.shape[1:])
        move = lambda d, z: (d ^ 1, z)
        values = self._halve(values, 1, self.h, move)
        rest = self.dp // 2
        position = lax.axis_index("dp") >> 1
        while rest > 1:
            rest //= 2
            values = values.reshape((2, rest) + values.shape[1:])
            bit = position // rest % 2
            values = self._halve(values, 0, bit, functools.partial(self._flip_dp, 2 * rest))
        values = values[0]
        rest = self.ex
        while rest > 1:
            rest //= 2
            values = values.reshape((2, rest) + values.shape[1:])
            bit = self.z // rest % 2
            values = self._halve(values, 0, bit, functools.partial(self._flip_ex, rest))
        return values[0].astype(F32)

    @staticmethod
    def _flip_dp(bit, d, z):
        return (d ^ bit, z)

    @staticmethod
    def _flip_ex(bit, d, z):
        return (d, z ^ bit)

    def _halve(self, values, axis, bit, move):
        keep = lax.dynamic_index_in_dim(values, bit, axis, keepdims=False)
        give = lax.dynamic_index_in_dim(values, 1 - bit, axis, keepdims=False)
        return (keep.astype(F32) + self.send(give, move).astype(F32)).astype(BF16)


class AxisPlan:
    def __init__(self, dp, ex):
        self.dp, self.ex = dp, ex

    def gather(self, shard):
        return lax.all_gather(shard, "dp", axis=0)

    def expert_ids(self):
        return jnp.arange(self.ex, dtype=jnp.int32)

    def exchange(self, values):
        return lax.all_to_all(values, "expert", split_axis=0, concat_axis=0, tiled=True)

    def reduce(self, sums):
        return lax.psum_scatter(sums, "dp", scatter_dimension=0, tiled=True)[0].astype(F32)

    def reduce_all(self, sums):
        return lax.psum_scatter(
            sums, ("dp", "expert"), scatter_dimension=0, tiled=True
        )[0].astype(F32)


def shards(
    dp_size,
    expert_count,
    hidden_input,
    gate_carryover,
    sequence_length,
    token_stream_place,
    expert_choice_index,
    sequence_adapter,
    attention_gain,
    query_key_weight,
    output_weight,
    adapter_in_query,
    adapter_out_query,
    adapter_in_output,
    adapter_out_output,
    feedfwd_gain,
    router_weight,
    constant_gate,
    constant_value,
    gate_upward_weight,
    down_weight,
    adapter_in_gate,
    adapter_out_gate,
    adapter_in_down,
    adapter_out_down,
    output_gradient,
):
    tok = hidden_input.shape[0]
    width = MODEL_WIDTH
    kinds = expert_count + 4
    devices = dp_size * expert_count
    capacity = 5 * tok // (2 * kinds) // 8 * 8 + 8
    cap = -(-capacity // 16) * 16
    blocks = tok // ROW_BLOCK
    plan = (PairPlan if (dp_size, expert_count) == (8, 4) else AxisPlan)(dp_size, expert_count)

    a_rows, b_rows = query_key_weight.shape[0], adapter_out_query.shape[0]
    own_a = jnp.concatenate(
        [query_key_weight, output_weight, adapter_in_query, adapter_in_output], axis=1
    )
    own_b = jnp.concatenate([adapter_out_query, adapter_out_output], axis=1)
    pad_rows = -(a_rows + b_rows) % 8
    own_attn = jnp.concatenate(
        [
            own_a,
            jnp.pad(own_b, ((0, pad_rows), (0, own_a.shape[1] - own_b.shape[1]))),
        ],
        axis=0,
    )
    attn_all = lax.all_gather(own_attn, ("dp", "expert"), axis=0)
    in_rows = attn_all[:, :a_rows]
    out_rows = attn_all[:, a_rows : a_rows + b_rows]
    w_qkv = in_rows[:, :, : 3 * width].reshape(width, 3 * width)
    w_out = in_rows[:, :, 3 * width : 4 * width].reshape(width, width)
    a_qkv = in_rows[:, :, 4 * width : 4 * width + LANES].reshape(width, LANES)
    a_out = in_rows[:, :, 4 * width + LANES :].reshape(width, LANES)
    b_qkv = out_rows[:, :, : 3 * width].reshape(LANES, 3 * width)
    b_out = out_rows[:, :, 3 * width : 4 * width].reshape(LANES, width)

    gu_rows, up_rows, dn_rows = gate_upward_weight.shape[1], adapter_out_gate.shape[1], down_weight.shape[1]
    wide = plan.gather(jnp.concatenate([gate_upward_weight[0], adapter_out_gate[0]], axis=0))
    mid = plan.gather(jnp.concatenate([down_weight[0], adapter_out_down[0]], axis=0))
    thin = plan.gather(jnp.concatenate([adapter_in_gate[0], adapter_in_down[0]], axis=0))
    w_gu = wide[:, :gu_rows].reshape(width, 2 * FEEDFWD_WIDTH)
    b_gu = wide[:, gu_rows:].reshape(LANES, 2 * FEEDFWD_WIDTH)
    w_dn = mid[:, :dn_rows].reshape(FEEDFWD_WIDTH, width)
    b_dn = mid[:, dn_rows:].reshape(LANES, width)
    a_gu = thin[:, :gu_rows].reshape(width, LANES)
    a_dn = thin[:, gu_rows:].reshape(FEEDFWD_WIDTH, LANES)

    place = token_stream_place[0]
    ends = jnp.cumsum(sequence_length[0])
    begins = ends - sequence_length[0]
    stream = jnp.arange(tok, dtype=jnp.int32)
    seg = jnp.sum((stream[:, None] >= ends[None, :]).astype(jnp.int32), axis=1)
    seg_hot = seg[:, None] == jnp.arange(ends.shape[0], dtype=jnp.int32)[None, :]
    start = jnp.sum(jnp.where(seg_hot, begins[None, :], 0), axis=1)
    adapter = jnp.sum(jnp.where(seg_hot, sequence_adapter[0][None, :], 0), axis=1)
    half = HEAD_DIM // 2
    freq = jnp.exp(jnp.arange(half, dtype=F32) * (-math.log(10000.0) / half))
    angle = (stream - start).astype(F32)[:, None] * freq[None, :]
    cos, sin = jnp.cos(angle), jnp.sin(angle)
    cosine = jnp.concatenate([cos, cos, cos, cos], axis=1)
    sine = jnp.concatenate([-sin, sin, -sin, sin], axis=1)
    starts = start[:, None]
    mask = (jnp.arange(LANES)[None, :] // ADAPTER_RANK == adapter[:, None]).astype(BF16)
    top, middle, last = split_three(gate_carryover)
    gap = jnp.zeros((tok, 16 - kinds), BF16)
    small = jnp.concatenate(
        [top, gap, middle, gap, last, gap, expert_choice_index.astype(BF16),
         jnp.zeros((tok, LANES - CHOICE_LANE - 2), BF16)],
        axis=1,
    )
    gain_one = attention_gain.astype(F32)[None, :]
    gain_two = feedfwd_gain.astype(F32)[None, :]
    router = jnp.concatenate(
        [router_weight, jnp.zeros((width, CONST_LANE - kinds), BF16), constant_gate,
         jnp.zeros((width, LANES - CONST_LANE - 4), BF16)],
        axis=1,
    )
    const_value = constant_value.astype(F32)

    full = whole
    hid_s, dy_s, small_s, act_one, low_qkv, query, key, value = call(
        proj_in_body,
        (blocks,),
        [full((1, tok)), full((tok, width)), full((tok, width)), full((tok, LANES)),
         row_spec(LANES), row_spec(LANES), row_spec(LANES), full((1, width)),
         full((width, 3 * width)), full((width, LANES)), full((LANES, 3 * width))],
        [row_spec(width), row_spec(width), row_spec(LANES), row_spec(width), row_spec(LANES),
         row_spec(width), row_spec(width), row_spec(width)],
        [sds((tok, width), BF16), sds((tok, width), BF16), sds((tok, LANES), F32),
         sds((tok, width), BF16), sds((tok, LANES), BF16), sds((tok, width), BF16),
         sds((tok, width), BF16), sds((tok, width), BF16)],
        name="proj_in",
    )(place[None, :], hidden_input, output_gradient, small, cosine, sine, mask, gain_one,
      w_qkv, a_qkv, b_qkv)

    pairs = HEAD_COUNT // 2
    attn_low, lse = call(
        attention_fwd_body,
        (pairs,),
        [col_spec(tok)] * 3 + [full((tok, 1))],
        [col_spec(tok), col_spec(tok)],
        [sds((tok, width), BF16), sds((tok, width), F32)],
        name="attention_fwd",
    )(query, key, value, starts)

    low_out, resid, act_two, gate = call(
        functools.partial(post_attn_body, kinds),
        (blocks,),
        [row_spec(width), row_spec(width), row_spec(LANES), row_spec(LANES), full((width, width)),
         full((width, LANES)), full((LANES, width)), full((width, LANES)), full((1, width))],
        [row_spec(LANES), row_spec(width), row_spec(width), row_spec(LANES)],
        [sds((tok, LANES), BF16), sds((tok, width), F32), sds((tok, width), BF16),
         sds((tok, LANES), F32)],
        name="post_attn",
    )(attn_low, hid_s, mask, small_s, w_out, a_out, b_out, router, gain_two)

    eids = plan.expert_ids()
    smem = pl.BlockSpec(memory_space=pltpu.SMEM)
    sent_width = 2 * width + LANES
    slot, sent = call(
        functools.partial(dispatch_body, expert_count),
        (expert_count,),
        [smem, full((tok, LANES)), full((tok, LANES)), full((tok, width)), full((tok, width)),
         full((tok, LANES))],
        [full((tok, LANES)), pl.BlockSpec((1, cap, sent_width), lambda i: (i, 0, 0))],
        [sds((tok, LANES), F32), sds((expert_count, cap, sent_width), BF16)],
        scratch=[pltpu.VMEM((LANES, tok), F32)],
        name="dispatch",
    )(eids, small_s, gate, act_two, dy_s, mask)

    came = plan.exchange(sent)
    back, ga_gu, gb_gu, ga_dn, gb_dn = call(
        ffn_body,
        (expert_count,),
        [pl.BlockSpec((1, cap, sent_width), lambda i: (i, 0, 0)), full((width, 2 * FEEDFWD_WIDTH)),
         full((FEEDFWD_WIDTH, width)), full((width, LANES)), full((LANES, 2 * FEEDFWD_WIDTH)),
         full((FEEDFWD_WIDTH, LANES)), full((LANES, width))],
        [pl.BlockSpec((1, cap, 2 * width), lambda i: (i, 0, 0)), full((width, LANES)),
         full((LANES, 2 * FEEDFWD_WIDTH)), full((FEEDFWD_WIDTH, LANES)), full((LANES, width))],
        [sds((expert_count, cap, 2 * width), BF16), sds((width, LANES), F32),
         sds((LANES, 2 * FEEDFWD_WIDTH), F32), sds((FEEDFWD_WIDTH, LANES), F32),
         sds((LANES, width), F32)],
        scratch=[pltpu.VMEM((cap, width), F32), pltpu.VMEM((cap, width), F32),
                 pltpu.VMEM((cap, LANES), F32), pltpu.VMEM((cap, LANES), F32)],
        name="ffn",
    )(came, w_gu, w_dn, a_gu, b_gu, a_dn, b_dn)
    returned = plan.exchange(back)

    owned_wide = plan.reduce(
        jnp.concatenate([gb_gu, gb_dn], axis=1).astype(BF16).reshape(dp_size, up_rows, -1)
    )
    owned_thin = plan.reduce(
        jnp.concatenate(
            [ga_gu.reshape(dp_size, gu_rows, LANES), ga_dn.reshape(dp_size, dn_rows, LANES)], axis=1
        ).astype(BF16)
    )

    out_s, d_resid, d_attended, d_logits, ga_out, gb_out = call(
        functools.partial(combine_body, expert_count, kinds),
        (blocks,),
        [smem, row_spec(width), row_spec(width), row_spec(width), row_spec(LANES), row_spec(LANES),
         row_spec(LANES), row_spec(LANES), row_spec(width), row_spec(LANES),
         full((expert_count, cap, 2 * width)), full((width, width)), full((width, LANES)),
         full((LANES, width)), full((width, LANES)), full((2, width)), full((1, width))],
        [row_spec(width), row_spec(width), row_spec(width), row_spec(LANES), full((width, LANES)),
         full((LANES, width))],
        [sds((tok, width), BF16), sds((tok, width), F32), sds((tok, width), BF16),
         sds((tok, LANES), F32), sds((width, LANES), F32), sds((LANES, width), F32)],
        name="combine",
    )(eids, resid, act_two, dy_s, gate, slot, small_s, low_out, attn_low, mask, returned,
      w_out, a_out, b_out, router, const_value, gain_two)

    d_query, d_key, d_value = call(
        attention_bwd_body,
        (pairs,),
        [col_spec(tok)] * 6 + [full((tok, 1)), full((tok, LANES)), full((tok, LANES))],
        [col_spec(tok)] * 3,
        [sds((tok, width), BF16)] * 3,
        scratch=[pltpu.VMEM((tok, LANES), F32), pltpu.VMEM((tok, LANES), F32)],
        name="attention_bwd",
    )(query, key, value, d_attended, attn_low, lse, starts, cosine, sine)

    high, lower, ga_qkv, gb_qkv = call(
        input_grad_body,
        (blocks,),
        [row_spec(width)] * 3 + [row_spec(LANES), row_spec(width), row_spec(LANES), row_spec(width),
         row_spec(width), full((width, 3 * width)), full((width, LANES)), full((LANES, 3 * width)),
         full((1, width))],
        [row_spec(width), row_spec(width), full((width, LANES)), full((LANES, 3 * width))],
        [sds((tok, width), BF16), sds((tok, width), BF16), sds((width, LANES), F32),
         sds((LANES, 3 * width), F32)],
        name="input_grad",
    )(d_query, d_key, d_value, low_qkv, act_one, mask, hid_s, d_resid, w_qkv, a_qkv, b_qkv,
      gain_one)

    owned = plan.reduce_all(
        jnp.concatenate(
            [
                ga_qkv.reshape(devices, b_rows, -1),
                ga_out.reshape(devices, b_rows, -1),
                gb_qkv.reshape(devices, b_rows, -1),
                gb_out.reshape(devices, b_rows, -1),
            ],
            axis=2,
        ).astype(BF16)
    )

    output, grad_hidden, grad_gate = call(
        to_rows_body,
        (blocks,),
        [row_spec(1), full((tok, width)), full((tok, LANES)), full((tok, width)),
         full((tok, width))],
        [row_spec(width), row_spec(width), row_spec(LANES)],
        [sds((tok, width), BF16), sds((tok, width), F32), sds((tok, LANES), F32)],
        name="to_rows",
    )(place[:, None], out_s, d_logits, high, lower)

    return (
        output,
        grad_hidden,
        grad_gate[:, :kinds],
        owned[:, :width].reshape(a_rows, LANES),
        owned[:, 2 * width : 5 * width],
        owned[:, width : 2 * width].reshape(a_rows, LANES),
        owned[:, 5 * width :],
        owned_thin[None, :gu_rows],
        owned_wide[None, :, : 2 * FEEDFWD_WIDTH],
        owned_thin[None, gu_rows:],
        owned_wide[None, :, 2 * FEEDFWD_WIDTH :],
    )


def solution(mesh):
    rows = P(("dp", "expert"), None)
    expert_rows = P("expert", "dp", None)
    in_specs = (
        (rows,) * 6 + (P(),) + (rows,) * 6 + (P(),) * 4 + (expert_rows,) * 6 + (rows,)
    )
    out_specs = (rows,) * 7 + (expert_rows,) * 4
    body = functools.partial(shards, mesh.shape["dp"], mesh.shape["expert"])
    return jax.shard_map(body, mesh=mesh, in_specs=in_specs, out_specs=out_specs, check_vma=False)
```

time: 1970 us -> 634 us (0.32)
  matrix products: 489 us -> 0 us
  local copies, waits for them, and re-layouts: 458 us -> 61.9 us
  blocking collectives: 311 us -> 9.87 us
  other arithmetic: 313 us -> 34.1 us
  Pallas kernels: 0 us -> 255 us
  waiting for transfers between devices: 333 us -> 198 us
  starting transfers between devices: 24.7 us -> 48.8 us
    dot_general x68 -> x0, matrix products: 489 us -> none  [the longest x22 121 us: plain_product(): return jnp.dot(left_arr, right_arr, preferred_element_type=jnp.float32)]
    all_gather x7 -> x1, blocking collectives: 311 us -> 9.87 us  [gather(): lax.all_gather(both, 'dp', axis=0, tiled=True, axis_index_groups=self.gro...]
    unnamed x15 -> x5, waiting for transfers between devices: 287 us -> 0.08 us
    pallas_call x0 -> x9, Pallas kernels: none -> 255 us  [the longest x1 65.5 us: shards(): call(ffn_body, (expert_count,), [pl.BlockSpec((1, cap, sent_width), lambd...]
    ppermute x0 -> x26, waiting for transfers between devices: none -> 188 us  [send(): return lax.ppermute(values, self.axes, pairs)]
    gather x16 -> x0, local copies, waits for them, and re-layouts: 143 us -> none  [the longest x2 14.5 us: shards(): attended[order_row].reshape(tok_rows, MODEL_WIDTH).astype(jnp.bfloat16)]
    reduce_sum x16 -> x2, other arithmetic: 115 us -> 0.19 us  [the longest x1 0.1 us: shards(): jnp.sum(jnp.where(seg_hot, sequence_adapter[0][None, :], 0), axis=1)]
    convert_element_type x26 -> x11, other arithmetic: 96.1 us -> 3.55 us  [the longest x4 1.85 us: _halve(): return (keep.astype(F32) + self.send(give, move).astype(F32)).astype(BF16)]
  transfers between devices with their start and end apart: 17 -> 31, of which waited for: 5 -> 14; matrix products, arithmetic and copies ran while one was open for 64% -> 11% of each run, Pallas kernels for 0% -> 15%
where the time goes in v1:
time: 634 us; the launch traced here: 623 us
  Pallas kernels  255 us (40%)
  waiting for transfers between devices  198 us (31%)
  local copies, waits for them, and re-layouts  61.9 us (10%)
  starting transfers between devices  48.8 us (8%)
  other arithmetic  34.1 us (5%)
  between operations  14.9 us (2%)
  blocking collectives  9.87 us (2%)
    ppermute x26, waiting for transfers between devices, send(): return lax.ppermute(values, self.axes, pairs)  188 us
    pallas_call x1, Pallas kernels, shards(): call(ffn_body, (expert_count,), [pl.BlockSpec((1, cap, sent_width), lambd...  65.5 us
    ppermute x26, starting transfers between devices, send(): return lax.ppermute(values, self.axes, pairs)  48.6 us
    pallas_call x1, Pallas kernels, shards(): call(attention_bwd_body, (pairs,), [col_spec(tok)] * 6 + [full((tok, 1)),...  48.6 us
    pallas_call x1, Pallas kernels, shards(): call(attention_fwd_body, (pairs,), [col_spec(tok)] * 3 + [full((tok, 1))]...  34.6 us
    pallas_call x1, Pallas kernels, shards(): call(functools.partial(combine_body, expert_count, kinds), (blocks,), [sm...  32.2 us
    pallas_call x1, Pallas kernels, shards(): call(proj_in_body, (blocks,), [full((1, tok)), full((tok, width)), full((...  21 us
    pallas_call x1, Pallas kernels, shards(): call(to_rows_body, (blocks,), [row_spec(1), full((tok, width)), full((tok...  15.5 us
  transfers between devices with their start and end apart: 31, of which 14 were waited for; matrix products, arithmetic and copies ran while one was open for 11% of the time, Pallas kernels for 15%

profile of v1, /device:TPU:1, one launch (start us, length us, event | category | flops | bytes accessed | tf_op | source)
XLA Modules:
  0.0 622.5 jit_solution(4373303687340925624)
XLA Ops:
  12.1 6.7 %collective-permute-start.7 = (bf16[272,768]{1,0:T(8,128)(2,1)S(1)}, bf16[272,768]{1,0:T(8,128)(2,1)S(1)}, u32[]{:S(2)}, u32[]{:S(2)}) collective-permute-start(bf16[272,768]{1,0:T(8,128)(2,1)S(1)} %pad_maximum_fusion.9), channel_id=1, source_target_pairs={{2,6},{3,7},{4,0},{5,1},{10,14},{11,15},{12,8},{13,9},{18,22},{19,... | collective-permute-start | bytes 1253384 | tf_op jit(solution)/shard_map/ppermute | solution.py:459
  20.7 5.0 collective-permute-done.6
  25.7 13.1 %collective-permute-done.8 = bf16[272,768]{1,0:T(8,128)(2,1)S(1)} collective-permute-done((bf16[272,768]{1,0:T(8,128)(2,1)S(1)}, bf16[272,768]{1,0:T(8,128)(2,1)S(1)}, u32[]{:S(2)}, u32[]{:S(2)}) %collective-permute-start.8) | collective-permute-done | bytes 417824 | tf_op jit(solution)/shard_map/ppermute | solution.py:459
  50.0 48.0 %collective-permute-done.3 = bf16[112,4096]{1,0:T(8,128)(2,1)S(1)} collective-permute-done((bf16[112,4096]{1,0:T(8,128)(2,1)S(1)}, bf16[112,4096]{1,0:T(8,128)(2,1)S(1)}, u32[]{:S(2)}, u32[]{:S(2)}) %collective-permute-start.3) | collective-permute-done | bytes 917536 | tf_op jit(solution)/shard_map/ppermute | solution.py:459
  97.9 10.8 %collective-permute-done.5 = bf16[112,4096]{1,0:T(8,128)(2,1)S(1)} collective-permute-done((bf16[112,4096]{1,0:T(8,128)(2,1)S(1)}, bf16[112,4096]{1,0:T(8,128)(2,1)S(1)}, u32[]{:S(2)}, u32[]{:S(2)}) %collective-permute-start.5) | collective-permute-done | bytes 917536 | tf_op jit(solution)/shard_map/ppermute | solution.py:459
  139.8 21.0 %proj_in.1 = (bf16[1280,768]{1,0:T(8,128)(2,1)}, bf16[1280,768]{1,0:T(8,128)(2,1)}, f32[1280,128]{1,0:T(8,128)}, bf16[1280,768]{1,0:T(8,128)(2,1)}, bf16[1280,12...) custom-call(s32[1,1280]{1,0:T(1,128)} %place_row.1, ...), custom_call_target="tpu_custom_call" | custom-call | tf_op jit(solution)/shard_map/proj_in/pallas_call | solution.py:654
  160.9 34.6 %attention_fwd.1 = (bf16[1280,768]{1,0:T(8,128)(2,1)}, f32[1280,768]{1,0:T(8,128)}) custom-call(bf16[1280,768]{1,0:T(8,128)(2,1)} %get-tuple-element.48.query, bf16[1280,768]{1,0:T(8,128)(2,1)} %get-tuple-element.49.key, bf16[1280,768]{1,0:T(8,128)(2,1)} %get-tuple-element.50.value, s32[1280,1]{1,0:T(8,128)} %reduce_sum.33.starts), custom_call_target="tpu_custom_call" | custom-call | tf_op jit(solution)/shard_map/attention_fwd/pallas_call | solution.py:670
  195.5 10.0 %post_attn.1 = (bf16[1280,128]{1,0:T(8,128)(2,1)}, f32[1280,768]{1,0:T(8,128)}, bf16[1280,768]{1,0:T(8,128)(2,1)}, f32[1280,128]{1,0:T(8,128)}) custom-call(bf16[1280,768]{1,0:T(8,128)(2,1)} %get-tuple-element.51.attn_low.attended, bf16[1280,768]{1,0:T(8,128)(2,1)} %get-tuple-element.52.hid_s, bf16[1280,128]{1,0:T(8,128)(2,1)} %compare_convert_fusion.mask, ...), custom_call_target="tpu_custom_call" | custom-call | tf_op jit(solution)/shard_map/post_attn/pallas_call | solution.py:679
  205.5 13.2 %dispatch.1 = (f32[1280,128]{1,0:T(8,128)}, bf16[4,416,1664]{2,1,0:T(8,128)(2,1)}) custom-call(s32[4]{0:T(128)} %iota_xor_fusion.eids, f32[1280,128]{1,0:T(8,128)} %get-tuple-element.53.small_s, f32[1280,128]{1,0:T(8,128)} %get-tuple-element.57.gate, bf16[1280,768]{1,0:T(8,128)(2,1)} %get-tuple-element.55.act_two, bf16[1280,768]{1,0:T(8,128)(2,1)} %get-tuple-element.56.dy_s, ...), custom_call_target="tpu_custom_call" | custom-call | tf_op jit(solution)/shard_map/dispatch/pallas_call | solution.py:693
  230.3 48.7 %collective-permute-done.11 = bf16[352,128]{1,0:T(8,128)(2,1)S(1)} collective-permute-done((bf16[352,128]{1,0:T(8,128)(2,1)S(1)}, bf16[352,128]{1,0:T(8,128)(2,1)S(1)}, u32[]{:S(2)}, u32[]{:S(2)}) %collective-permute-start.11) | collective-permute-done | bytes 90144 | tf_op jit(solution)/shard_map/ppermute | solution.py:459
  279.1 9.9 %all_gather.19 = bf16[8,352,128]{2,1,0:T(8,128)(2,1)S(1)} all-gather(bf16[2,352,128]{2,1,0:T(8,128)(2,1)S(1)} %pad_maximum_fusion.11), channel_id=1, replica_groups={{0,8,16,24},{4,12,20,28},{1,9,17,25},{5,13,21,29},{2,10,18,26},{6,14,22..., dimensions={0}, use_global_device_ids=true | all-gather | bytes 901120 | tf_op jit(solution)/shard_map/all_gather | solution.py:468
  295.9 6.2 %slice.150 = bf16[8,96,4096]{2,1,0:T(8,128)(2,1)} slice(bf16[8,112,4096]{2,1,0:T(8,128)(2,1)} %all-gather.5.cloned.1.call-done), slice={[0:8], [0:96], [0:4096]} | slice | bytes 12582912 | tf_op jit(solution)/shard_map/slice | solution.py:614
  304.5 5.7 pad_maximum_fusion.came
  310.2 65.5 %ffn.1 = (bf16[4,416,1536]{2,1,0:T(8,128)(2,1)}, f32[768,128]{1,0:T(8,128)}, f32[128,4096]{1,0:T(8,128)}, f32[2048,128]{1,0:T(8,128)}, f32[128,768]{1,0:T(8,128)}) custom-call(bf16[4,416,1664]{2,1,0:T(8,128)(2,1)} %pad_maximum_fusion.came, bf16[768,4096]{1,0:T(8,128)(2,1)} %bitcast.102, bf16[2048,768]{1,0:T(8,128)(2,1)} %bitcast.103, ...), custom_call_target="tpu_custom_call" | custom-call | tf_op jit(solution)/shard_map/ffn/pallas_call | solution.py:705
  382.4 27.7 %collective-permute-done.12 = bf16[416,1536]{1,0:T(8,128)(2,1)} collective-permute-done((bf16[416,1536]{1,0:T(8,128)(2,1)}, bf16[416,1536]{1,0:T(8,128)(2,1)}, u32[]{:S(2)}, u32[]{:S(2)}) %collective-permute-start.12) | collective-permute-done | bytes 1277984 | tf_op jit(solution)/shard_map/ppermute | solution.py:459
  410.1 21.2 %collective-permute-done.14 = bf16[416,1536]{1,0:T(8,128)(2,1)} collective-permute-done((bf16[416,1536]{1,0:T(8,128)(2,1)S(1)}, bf16[416,1536]{1,0:T(8,128)(2,1)}, u32[]{:S(2)}, u32[]{:S(2)}) %collective-permute-start.14) | collective-permute-done | bytes 1277984 | tf_op jit(solution)/shard_map/ppermute | solution.py:459
  431.4 5.2 pad_maximum_fusion.1.came
  436.6 32.2 %combine.1 = (bf16[1280,768]{1,0:T(8,128)(2,1)}, f32[1280,768]{1,0:T(8,128)}, bf16[1280,768]{1,0:T(8,128)(2,1)}, f32[1280,128]{1,0:T(8,128)}, f32[768,128]{1,0:T(8,128)}, /*index=5*/f32[128,768]{1,0:T(8,128)}) custom-call(s32[4]{0:T(128)} %iota_xor_fusion.eids, f32[1280,768]{1,0:T(8,128)} %get-tuple-element.54.resid, ...), custom_call_target="tpu_custom_call" | custom-call | tf_op jit(solution)/shard_map/combine/pallas_call | solution.py:731
  468.8 48.6 %attention_bwd.1 = (bf16[1280,768]{1,0:T(8,128)(2,1)}, bf16[1280,768]{1,0:T(8,128)(2,1)}, bf16[1280,768]{1,0:T(8,128)(2,1)}) custom-call(bf16[1280,768]{1,0:T(8,128)(2,1)} %get-tuple-element.48.query, bf16[1280,768]{1,0:T(8,128)(2,1)} %get-tuple-element.49.key, bf16[1280,768]{1,0:T(8,128)(2,1)} %get-tuple-element.50.value, ...), custom_call_target="tpu_custom_call" | custom-call | tf_op jit(solution)/shard_map/attention_bwd/pallas_call | solution.py:746
  517.5 14.8 %input_grad.1 = (bf16[1280,768]{1,0:T(8,128)(2,1)}, bf16[1280,768]{1,0:T(8,128)(2,1)}, f32[768,128]{1,0:T(8,128)}, f32[128,2304]{1,0:T(8,128)}) custom-call(bf16[1280,768]{1,0:T(8,128)(2,1)} %get-tuple-element.66.d_query, bf16[1280,768]{1,0:T(8,128)(2,1)} %get-tuple-element.67.d_key, bf16[1280,768]{1,0:T(8,128)(2,1)} %get-tuple-element.68.d_value, ...), custom_call_target="tpu_custom_call" | custom-call | tf_op jit(solution)/shard_map/input_grad/pallas_call | solution.py:756
  550.4 15.5 %to_rows.1 = (bf16[1280,768]{1,0:T(8,128)(2,1)}, f32[1280,768]{1,0:T(8,128)}, f32[1280,128]{1,0:T(8,128)}) custom-call(s32[1280,1]{1,0:T(8,128)} %copy.81.place_col, bf16[1280,768]{1,0:T(8,128)(2,1)} %get-tuple-element.62.out_s, f32[1280,128]{1,0:T(8,128)} %get-tuple-element.63.d_logits, bf16[1280,768]{1,0:T(8,128)(2,1)} %get-tuple-element.72.high, ...), custom_call_target="tpu_custom_call" | custom-call | tf_op jit(solution)/shard_map/to_rows/pallas_call | solution.py:781
  571.2 4.6 collective-permute-start.22
  578.9 5.2 collective-permute-done.17
  592.7 8.3 %reduce-scatter.5.cloned.1.call-done = bf16[2,16,4864]{2,1,0:T(8,128)(2,1)} async-done(((bf16[8,16,4864]{2,1,0:T(8,128)(2,1)}), bf16[2,16,4864]{2,1,0:T(8,128)(2,1)}) %reduce-scatter.5.cloned.1.call-update) | async-done | bytes 311312 | tf_op jit(solution)/shard_map/reduce_scatter | solution.py:483
  (199 shorter events, 125.8 us)
Async XLA Ops:
  7.2 120.3 %all-gather.9.cloned.1.call-start = ((), (), s32[]{:S(2)}) async-start(), calls=%async_computation.6 | async-start | bytes 7028736 | tf_op jit(solution)/shard_map/all_gather | solution.py:600
  9.7 280.8 %all-gather.7.cloned.1.call-start = ((), (), s32[]{:S(2)}) async-start(), calls=%async_computation.3 | async-start | bytes 4177920 | tf_op jit(solution)/shard_map/all_gather | solution.py:468
  10.8 14.9 %collective-permute-start.6 = (bf16[272,768]{1,0:T(8,128)(2,1)S(1)}, bf16[272,768]{1,0:T(8,128)(2,1)S(1)}, u32[]{:S(2)}, u32[]{:S(2)}) collective-permute-start(bf16[272,768]{1,0:T(8,128)(2,1)S(1)} %pad_maximum_fusion.9), channel_id=1, source_target_pairs={{0,2},{1,3},{6,4},{7,5},{8,10},{9,11},{14,12},{15,13},{16,18},{17,... | collective-permute-start | bytes 1253384 | tf_op jit(solution)/shard_map/ppermute | solution.py:459
  12.1 13.6 %collective-permute-start.7 = (bf16[272,768]{1,0:T(8,128)(2,1)S(1)}, bf16[272,768]{1,0:T(8,128)(2,1)S(1)}, u32[]{:S(2)}, u32[]{:S(2)}) collective-permute-start(bf16[272,768]{1,0:T(8,128)(2,1)S(1)} %pad_maximum_fusion.9), channel_id=1, source_target_pairs={{2,6},{3,7},{4,0},{5,1},{10,14},{11,15},{12,8},{13,9},{18,22},{19,... | collective-permute-start | bytes 1253384 | tf_op jit(solution)/shard_map/ppermute | solution.py:459
  18.8 20.0 %collective-permute-start.8 = (bf16[272,768]{1,0:T(8,128)(2,1)S(1)}, bf16[272,768]{1,0:T(8,128)(2,1)S(1)}, u32[]{:S(2)}, u32[]{:S(2)}) collective-permute-start(bf16[272,768]{1,0:T(8,128)(2,1)S(1)} %pad_maximum_fusion.9), channel_id=1, source_target_pairs={{2,4},{3,5},{4,2},{5,3},{10,12},{11,13},{12,10},{13,11},{18,20},{1... | collective-permute-start | bytes 1253384 | tf_op jit(solution)/shard_map/ppermute | solution.py:459
  40.9 255.1 %all-gather.5.cloned.1.call-start = ((), (), s32[]{:S(2)}) async-start(), calls=%async_computation.2 | async-start | bytes 9175040 | tf_op jit(solution)/shard_map/all_gather | solution.py:468
  41.3 56.6 %collective-permute-start.3 = (bf16[112,4096]{1,0:T(8,128)(2,1)S(1)}, bf16[112,4096]{1,0:T(8,128)(2,1)S(1)}, u32[]{:S(2)}, u32[]{:S(2)}) collective-permute-start(bf16[112,4096]{1,0:T(8,128)(2,1)S(1)} %pad_maximum_fusion.4), channel_id=1, source_target_pairs={{0,2},{1,3},{6,4},{7,5},{8,10},{9,11},{14,12},{15,13},{16,18},{17,... | collective-permute-start | bytes 2752520 | tf_op jit(solution)/shard_map/ppermute | solution.py:459
  42.6 55.3 %collective-permute-start.4 = (bf16[112,4096]{1,0:T(8,128)(2,1)S(1)}, bf16[112,4096]{1,0:T(8,128)(2,1)S(1)}, u32[]{:S(2)}, u32[]{:S(2)}) collective-permute-start(bf16[112,4096]{1,0:T(8,128)(2,1)S(1)} %pad_maximum_fusion.4), channel_id=1, source_target_pairs={{2,6},{3,7},{4,0},{5,1},{10,14},{11,15},{12,8},{13,9},{18,22},{19,... | collective-permute-start | bytes 2752520 | tf_op jit(solution)/shard_map/ppermute | solution.py:459
  45.3 63.5 %collective-permute-start.5 = (bf16[112,4096]{1,0:T(8,128)(2,1)S(1)}, bf16[112,4096]{1,0:T(8,128)(2,1)S(1)}, u32[]{:S(2)}, u32[]{:S(2)}) collective-permute-start(bf16[112,4096]{1,0:T(8,128)(2,1)S(1)} %pad_maximum_fusion.4), channel_id=1, source_target_pairs={{2,4},{3,5},{4,2},{5,3},{10,12},{11,13},{12,10},{13,11},{18,20},{1... | collective-permute-start | bytes 2752520 | tf_op jit(solution)/shard_map/ppermute | solution.py:459
  110.9 458.0 %reduce-scatter.3.cloned.1.call-start = ((), (), s32[]{:S(2)}) async-start(), calls=%async_computation.4 | async-start | bytes 901120 | tf_op jit(solution)/shard_map/reduce_scatter | solution.py:483
  223.2 81.3 %collective-permute-start = (bf16[416,1664]{1,0:T(8,128)(2,1)}, bf16[416,1664]{1,0:T(8,128)(2,1)}, u32[]{:S(2)}, u32[]{:S(2)}) collective-permute-start(bf16[416,1664]{1,0:T(8,128)(2,1)} %get-tuple-element.147), channel_id=1, source_target_pairs={{0,1},{1,0},{2,3},{3,2},{4,5},{5,4},{6,7},{7,6},{8,9},{9,8},{10,11... | collective-permute-start | bytes 4153352 | tf_op jit(solution)/shard_map/ppermute | solution.py:459
  223.2 81.3 %collective-permute-start.1 = (bf16[416,1664]{1,0:T(8,128)(2,1)}, bf16[416,1664]{1,0:T(8,128)(2,1)}, u32[]{:S(2)}, u32[]{:S(2)}) collective-permute-start(bf16[416,1664]{1,0:T(8,128)(2,1)} %get-tuple-element.146), channel_id=1, source_target_pairs={{0,4},{1,5},{2,6},{3,7},{4,0},{5,1},{6,2},{7,3},{8,12},{9,13},{10,... | collective-permute-start | bytes 4153352 | tf_op jit(solution)/shard_map/ppermute | solution.py:459
  223.2 81.3 %collective-permute-start.2 = (bf16[416,1664]{1,0:T(8,128)(2,1)S(1)}, bf16[416,1664]{1,0:T(8,128)(2,1)}, u32[]{:S(2)}, u32[]{:S(2)}) collective-permute-start(bf16[416,1664]{1,0:T(8,128)(2,1)S(1)} %get-tuple-element.145), channel_id=1, source_target_pairs={{0,5},{1,4},{2,7},{3,6},{4,1},{5,0},{6,3},{7,2},{8,13},{9,12},{10,... | collective-permute-start | bytes 4153352 | tf_op jit(solution)/shard_map/ppermute | solution.py:459
  227.0 51.9 %collective-permute-start.11 = (bf16[352,128]{1,0:T(8,128)(2,1)S(1)}, bf16[352,128]{1,0:T(8,128)(2,1)S(1)}, u32[]{:S(2)}, u32[]{:S(2)}) collective-permute-start(bf16[352,128]{1,0:T(8,128)(2,1)S(1)} %pad_maximum_fusion.12), channel_id=1, source_target_pairs={{2,4},{3,5},{4,2},{5,3},{10,12},{11,13},{12,10},{13,11},{18,20},{1... | collective-permute-start | bytes 270344 | tf_op jit(solution)/shard_map/ppermute | solution.py:459
  229.0 50.0 %collective-permute-start.9 = (bf16[352,128]{1,0:T(8,128)(2,1)S(1)}, bf16[352,128]{1,0:T(8,128)(2,1)S(1)}, u32[]{:S(2)}, u32[]{:S(2)}) collective-permute-start(bf16[352,128]{1,0:T(8,128)(2,1)S(1)} %pad_maximum_fusion.12), channel_id=1, source_target_pairs={{0,2},{1,3},{6,4},{7,5},{8,10},{9,11},{14,12},{15,13},{16,18},{17,... | collective-permute-start | bytes 270344 | tf_op jit(solution)/shard_map/ppermute | solution.py:459
  379.9 30.2 %collective-permute-start.12 = (bf16[416,1536]{1,0:T(8,128)(2,1)}, bf16[416,1536]{1,0:T(8,128)(2,1)}, u32[]{:S(2)}, u32[]{:S(2)}) collective-permute-start(bf16[416,1536]{1,0:T(8,128)(2,1)} %get-tuple-element.151), channel_id=1, source_target_pairs={{0,1},{1,0},{2,3},{3,2},{4,5},{5,4},{6,7},{7,6},{8,9},{9,8},{10,11... | collective-permute-start | bytes 3833864 | tf_op jit(solution)/shard_map/ppermute | solution.py:459
  379.9 30.2 %collective-permute-start.13 = (bf16[416,1536]{1,0:T(8,128)(2,1)}, bf16[416,1536]{1,0:T(8,128)(2,1)}, u32[]{:S(2)}, u32[]{:S(2)}) collective-permute-start(bf16[416,1536]{1,0:T(8,128)(2,1)} %get-tuple-element.150), channel_id=1, source_target_pairs={{0,4},{1,5},{2,6},{3,7},{4,0},{5,1},{6,2},{7,3},{8,12},{9,13},{10,... | collective-permute-start | bytes 3833864 | tf_op jit(solution)/shard_map/ppermute | solution.py:459
  379.9 51.4 %collective-permute-start.14 = (bf16[416,1536]{1,0:T(8,128)(2,1)S(1)}, bf16[416,1536]{1,0:T(8,128)(2,1)}, u32[]{:S(2)}, u32[]{:S(2)}) collective-permute-start(bf16[416,1536]{1,0:T(8,128)(2,1)S(1)} %get-tuple-element.149), channel_id=1, source_target_pairs={{0,5},{1,4},{2,7},{3,6},{4,1},{5,0},{6,3},{7,2},{8,13},{9,12},{10,... | collective-permute-start | bytes 3833864 | tf_op jit(solution)/shard_map/ppermute | solution.py:459
  546.4 54.6 %reduce-scatter.5.cloned.1.call-start = ((), (), s32[]{:S(2)}) async-start(), calls=%async_computation.5 | async-start | bytes 1556480 | tf_op jit(solution)/shard_map/reduce_scatter | solution.py:483
  548.1 29.2 %collective-permute-start.16 = (bf16[2,4,4,4608]{3,2,1,0:T(4,128)(2,1)S(1)}, bf16[2,4,4,4608]{3,2,1,0:T(4,128)(2,1)S(1)}, u32[]{:S(2)}, u32[]{:S(2)}) collective-permute-start(bf16[2,4,4,4608]{3,2,1,0:T(4,128)(2,1)S(1)} %dynamic-slice_bitcast_fusion.1), channel_id=1, source_target_pairs={{0,16},{1,17},{2,18},{3,19},{4,20},{5,21},{6,22},{7,23},{8,24},{9,... | collective-permute-start | bytes 884744 | tf_op jit(solution)/shard_map/ppermute | solution.py:459
  569.9 8.8 %collective-permute-start.20 = (bf16[352,128]{1,0:T(8,128)(2,1)S(1)}, bf16[352,128]{1,0:T(8,128)(2,1)S(1)}, u32[]{:S(2)}, u32[]{:S(2)}) collective-permute-start(bf16[352,128]{1,0:T(8,128)(2,1)S(1)} %get-tuple-element.163), channel_id=1, source_target_pairs={{0,4},{1,5},{6,2},{7,3},{8,12},{9,13},{14,10},{15,11},{16,20},{17,... | collective-permute-start | bytes 270344 | tf_op jit(solution)/shard_map/ppermute | solution.py:459
  571.2 7.6 %collective-permute-start.22 = (bf16[352,128]{1,0:T(8,128)(2,1)S(1)}, bf16[352,128]{1,0:T(8,128)(2,1)S(1)}, u32[]{:S(2)}, u32[]{:S(2)}) collective-permute-start(bf16[352,128]{1,0:T(8,128)(2,1)S(1)} %get-tuple-element.163), channel_id=1, source_target_pairs={{2,4},{3,5},{4,2},{5,3},{10,12},{11,13},{12,10},{13,11},{18,20},{1... | collective-permute-start | bytes 270344 | tf_op jit(solution)/shard_map/ppermute | solution.py:459
  602.0 9.1 %collective-permute-start.23 = (bf16[16,4864]{1,0:T(8,128)(2,1)S(1)}, bf16[16,4864]{1,0:T(8,128)(2,1)S(1)}, u32[]{:S(2)}, u32[]{:S(2)}) collective-permute-start(bf16[16,4864]{1,0:T(8,128)(2,1)S(1)} %get-tuple-element.161), channel_id=1, source_target_pairs={{0,4},{1,5},{6,2},{7,3},{8,12},{9,13},{14,10},{15,11},{16,20},{17,... | collective-permute-start | bytes 466952 | tf_op jit(solution)/shard_map/ppermute | solution.py:459
  603.3 10.8 %collective-permute-start.25 = (bf16[16,4864]{1,0:T(8,128)(2,1)S(1)}, bf16[16,4864]{1,0:T(8,128)(2,1)S(1)}, u32[]{:S(2)}, u32[]{:S(2)}) collective-permute-start(bf16[16,4864]{1,0:T(8,128)(2,1)S(1)} %get-tuple-element.161), channel_id=1, source_target_pairs={{2,4},{3,5},{4,2},{5,3},{10,12},{11,13},{12,10},{13,11},{18,20},{1... | collective-permute-start | bytes 466952 | tf_op jit(solution)/shard_map/ppermute | solution.py:459
  (29 other events, 144.1 us)
Sparse Core Ops, SparseCore 0:
  11.4 104.3 all-gather.8
  117.7 44.8 all-gather.6
  164.4 78.9 all-gather.4
  546.5 22.4 reduce-scatter.2
  572.0 28.9 reduce-scatter.4

commit v2 on v1

--- a/solution.py
+++ b/solution.py
@@ -249,18 +249,10 @@
     sent[0, :, 2 * MODEL_WIDTH :] = dot(pick, mask[...]).astype(BF16)
 
 
-def ffn_body(
-    came, w_gu, w_dn, a_gu, b_gu, a_dn, b_dn,
-    back, ga_gu, gb_gu, ga_dn, gb_dn, acc_out, acc_dx, acc_low, acc_dlow,
+def ffn_math(
+    rows, d_out, mask, w_gu, w_dn, a_gu, b_gu, a_dn, b_dn,
+    ga_gu, gb_gu, ga_dn, gb_dn, acc_out, acc_dx, acc_low, acc_dlow,
 ):
-    @pl.when(pl.program_id(0) == 0)
-    def _():
-        for ref in (ga_gu, gb_gu, ga_dn, gb_dn):
-            ref[...] = jnp.zeros_like(ref)
-
-    rows = came[0, :, :MODEL_WIDTH]
-    d_out = came[0, :, MODEL_WIDTH : 2 * MODEL_WIDTH]
-    mask = came[0, :, 2 * MODEL_WIDTH :].astype(F32)
     low_gu = (dot(rows, a_gu[...]) * mask).astype(BF16)
     dlow_dn = (dot_nt(d_out, b_dn[...]) * mask).astype(BF16)
     for ref in (acc_out, acc_dx, acc_low, acc_dlow):
@@ -290,11 +282,119 @@
 
     lax.fori_loop(0, FEEDFWD_WIDTH // HIDDEN_BLOCK, step, 0)
     low_dn = (acc_low[...] * mask).astype(BF16)
-    back[0, :, :MODEL_WIDTH] = (acc_out[...] + dot(low_dn, b_dn[...])).astype(BF16)
+    result = (acc_out[...] + dot(low_dn, b_dn[...])).astype(BF16)
     gb_dn[...] += dot_tn(low_dn, d_out)
     dlow_gu = (acc_dlow[...] * mask).astype(BF16)
-    back[0, :, MODEL_WIDTH:] = (acc_dx[...] + dot_nt(dlow_gu, a_gu[...])).astype(BF16)
+    d_rows = (acc_dx[...] + dot_nt(dlow_gu, a_gu[...])).astype(BF16)
     ga_gu[...] += dot_tn(rows, dlow_gu)
+    return result, d_rows
+
+
+def ffn_body(
+    came, w_gu, w_dn, a_gu, b_gu, a_dn, b_dn,
+    back, ga_gu, gb_gu, ga_dn, gb_dn, acc_out, acc_dx, acc_low, acc_dlow,
+):
+    @pl.when(pl.program_id(0) == 0)
+    def _():
+        for ref in (ga_gu, gb_gu, ga_dn, gb_dn):
+            ref[...] = jnp.zeros_like(ref)
+
+    back[0, :, :MODEL_WIDTH], back[0, :, MODEL_WIDTH:] = ffn_math(
+        came[0, :, :MODEL_WIDTH], came[0, :, MODEL_WIDTH : 2 * MODEL_WIDTH],
+        came[0, :, 2 * MODEL_WIDTH :].astype(F32), w_gu, w_dn, a_gu, b_gu, a_dn, b_dn,
+        ga_gu, gb_gu, ga_dn, gb_dn, acc_out, acc_dx, acc_low, acc_dlow,
+    )
+
+
+def pair_ffn_body(
+    sent, wide, mid, thin,
+    returned, ga_gu, gb_gu, ga_dn, gb_dn,
+    came, back, w_gu, w_dn, a_gu, b_gu, a_dn, b_dn, acc_out, acc_dx, acc_low, acc_dlow,
+    load_sems, send_sems, came_sems, back_sems, done_sems,
+):
+    dp, z = lax.axis_index("dp"), lax.axis_index("expert")
+    core, plane = dp % 2, z % 2
+    mesh_id = pl.DeviceIdType.MESH
+
+    def peer(k):
+        return (dp + (k // 2) * (1 - 2 * core), z + (k % 2) * (1 - 2 * plane))
+
+    barrier = pltpu.get_barrier_semaphore()
+    for k in (1, 2, 3):
+        pl.semaphore_signal(barrier, inc=1, device_id=peer(k), device_id_type=mesh_id)
+    pl.semaphore_wait(barrier, 3)
+
+    def rows_out(k):
+        return pltpu.make_async_remote_copy(
+            src_ref=sent.at[k], dst_ref=came.at[k], send_sem=send_sems.at[k],
+            recv_sem=came_sems.at[k], device_id=peer(k), device_id_type=mesh_id,
+        )
+
+    def result_out(k):
+        return pltpu.make_async_remote_copy(
+            src_ref=back.at[k], dst_ref=returned.at[k], send_sem=back_sems.at[k],
+            recv_sem=done_sems.at[k], device_id=peer(k), device_id_type=mesh_id,
+        )
+
+    for k in (1, 2, 3):
+        rows_out(k).start()
+    own_in = pltpu.make_async_copy(sent.at[0], came.at[0], came_sems.at[0])
+    own_in.start()
+
+    gu_rows = w_gu.shape[0] // wide.shape[0]
+    up_rows = b_gu.shape[0] // wide.shape[0]
+    dn_rows = w_dn.shape[0] // wide.shape[0]
+    plans = (
+        (wide, 0, gu_rows, w_gu), (wide, gu_rows, up_rows, b_gu), (mid, 0, dn_rows, w_dn),
+        (mid, dn_rows, up_rows, b_dn), (thin, 0, gu_rows, a_gu), (thin, gu_rows, dn_rows, a_dn),
+    )
+
+    def load(d, carry):
+        for i, (source, at, count, target) in enumerate(plans):
+            pltpu.make_async_copy(
+                source.at[d, pl.ds(at, count)],
+                target.at[pl.ds(pl.multiple_of(d * count, 16), count)],
+                load_sems.at[i],
+            ).start()
+        return carry
+
+    lax.fori_loop(0, wide.shape[0], load, 0)
+    for ref in (ga_gu, gb_gu, ga_dn, gb_dn):
+        ref[...] = jnp.zeros_like(ref)
+    for i, (_, _, _, target) in enumerate(plans):
+        pltpu.make_async_copy(target, target, load_sems.at[i]).wait()
+
+    def source_step(s, carry):
+        k = (s % 2) * 2 + s // 2
+
+        @pl.when(s == 0)
+        def _():
+            own_in.wait()
+
+        @pl.when(s > 0)
+        def _():
+            rows_out(k).wait_recv()
+
+        back[k, :, :MODEL_WIDTH], back[k, :, MODEL_WIDTH:] = ffn_math(
+            came[k, :, :MODEL_WIDTH], came[k, :, MODEL_WIDTH : 2 * MODEL_WIDTH],
+            came[k, :, 2 * MODEL_WIDTH :].astype(F32), w_gu, w_dn, a_gu, b_gu, a_dn, b_dn,
+            ga_gu, gb_gu, ga_dn, gb_dn, acc_out, acc_dx, acc_low, acc_dlow,
+        )
+
+        @pl.when(s > 0)
+        def _():
+            result_out(k).start()
+
+        return carry
+
+    lax.fori_loop(0, 4, source_step, 0)
+    own_out = pltpu.make_async_copy(back.at[0], returned.at[0], done_sems.at[0])
+    own_out.start()
+    own_out.wait()
+    for k in (1, 2, 3):
+        rows_out(k).wait_send()
+        result_out(k).wait_send()
+        result_out(k).wait_recv()
 
 
 def combine_body(
@@ -440,6 +540,8 @@
 
 
 class PairPlan:
+    paired = True
+
     def __init__(self, dp, ex):
         self.axes = ("dp", "expert")
         self.dp, self.ex = dp, ex
@@ -469,15 +571,6 @@
 
     def expert_ids(self):
         return self.own ^ jnp.arange(self.ex, dtype=jnp.int32)
-
-    def exchange(self, values):
-        moves = (
-            lambda d, z: (d, z ^ 1),
-            lambda d, z: (d ^ 1, z),
-            lambda d, z: (d ^ 1, z ^ 1),
-        )
-        parts = [values[0]] + [self.send(values[k + 1], moves[k]) for k in range(3)]
-        return jnp.stack(parts)
 
     def reduce(self, sums):
         part = lax.psum_scatter(
@@ -526,6 +619,8 @@
 
 
 class AxisPlan:
+    paired = False
+
     def __init__(self, dp, ex):
         self.dp, self.ex = dp, ex
 
@@ -611,12 +706,6 @@
     wide = plan.gather(jnp.concatenate([gate_upward_weight[0], adapter_out_gate[0]], axis=0))
     mid = plan.gather(jnp.concatenate([down_weight[0], adapter_out_down[0]], axis=0))
     thin = plan.gather(jnp.concatenate([adapter_in_gate[0], adapter_in_down[0]], axis=0))
-    w_gu = wide[:, :gu_rows].reshape(width, 2 * FEEDFWD_WIDTH)
-    b_gu = wide[:, gu_rows:].reshape(LANES, 2 * FEEDFWD_WIDTH)
-    w_dn = mid[:, :dn_rows].reshape(FEEDFWD_WIDTH, width)
-    b_dn = mid[:, dn_rows:].reshape(LANES, width)
-    a_gu = thin[:, :gu_rows].reshape(width, LANES)
-    a_dn = thin[:, gu_rows:].reshape(FEEDFWD_WIDTH, LANES)
 
     place = token_stream_place[0]
     ends = jnp.cumsum(sequence_length[0])
@@ -701,23 +790,58 @@
         name="dispatch",
     )(eids, small_s, gate, act_two, dy_s, mask)
 
-    came = plan.exchange(sent)
-    back, ga_gu, gb_gu, ga_dn, gb_dn = call(
-        ffn_body,
-        (expert_count,),
-        [pl.BlockSpec((1, cap, sent_width), lambda i: (i, 0, 0)), full((width, 2 * FEEDFWD_WIDTH)),
-         full((FEEDFWD_WIDTH, width)), full((width, LANES)), full((LANES, 2 * FEEDFWD_WIDTH)),
-         full((FEEDFWD_WIDTH, LANES)), full((LANES, width))],
-        [pl.BlockSpec((1, cap, 2 * width), lambda i: (i, 0, 0)), full((width, LANES)),
-         full((LANES, 2 * FEEDFWD_WIDTH)), full((FEEDFWD_WIDTH, LANES)), full((LANES, width))],
-        [sds((expert_count, cap, 2 * width), BF16), sds((width, LANES), F32),
-         sds((LANES, 2 * FEEDFWD_WIDTH), F32), sds((FEEDFWD_WIDTH, LANES), F32),
-         sds((LANES, width), F32)],
-        scratch=[pltpu.VMEM((cap, width), F32), pltpu.VMEM((cap, width), F32),
-                 pltpu.VMEM((cap, LANES), F32), pltpu.VMEM((cap, LANES), F32)],
-        name="ffn",
-    )(came, w_gu, w_dn, a_gu, b_gu, a_dn, b_dn)
-    returned = plan.exchange(back)
+    grad_shapes = [
+        sds((width, LANES), F32), sds((LANES, 2 * FEEDFWD_WIDTH), F32),
+        sds((FEEDFWD_WIDTH, LANES), F32), sds((LANES, width), F32),
+    ]
+    accumulators = [
+        pltpu.VMEM((cap, width), F32), pltpu.VMEM((cap, width), F32),
+        pltpu.VMEM((cap, LANES), F32), pltpu.VMEM((cap, LANES), F32),
+    ]
+    if plan.paired:
+        hbm = pl.BlockSpec(memory_space=pl.ANY)
+        vmem = pl.BlockSpec(memory_space=pltpu.VMEM)
+        returned, ga_gu, gb_gu, ga_dn, gb_dn = pl.pallas_call(
+            pair_ffn_body,
+            in_specs=[hbm] * 4,
+            out_specs=[hbm] + [vmem] * 4,
+            out_shape=[sds((expert_count, cap, 2 * width), BF16)] + grad_shapes,
+            scratch_shapes=[
+                pltpu.VMEM((expert_count, cap, sent_width), BF16),
+                pltpu.VMEM((expert_count, cap, 2 * width), BF16),
+                pltpu.VMEM((width, 2 * FEEDFWD_WIDTH), BF16), pltpu.VMEM((FEEDFWD_WIDTH, width), BF16),
+                pltpu.VMEM((width, LANES), BF16), pltpu.VMEM((LANES, 2 * FEEDFWD_WIDTH), BF16),
+                pltpu.VMEM((FEEDFWD_WIDTH, LANES), BF16), pltpu.VMEM((LANES, width), BF16),
+                *accumulators,
+                pltpu.SemaphoreType.DMA((6,)),
+                *[pltpu.SemaphoreType.DMA((expert_count,)) for _ in range(4)],
+            ],
+            compiler_params=pltpu.CompilerParams(
+                vmem_limit_bytes=VMEM_BYTES, collective_id=1, has_side_effects=True
+            ),
+            name="pair_ffn",
+        )(sent, wide, mid, thin)
+    else:
+        w_gu = wide[:, :gu_rows].reshape(width, 2 * FEEDFWD_WIDTH)
+        b_gu = wide[:, gu_rows:].reshape(LANES, 2 * FEEDFWD_WIDTH)
+        w_dn = mid[:, :dn_rows].reshape(FEEDFWD_WIDTH, width)
+        b_dn = mid[:, dn_rows:].reshape(LANES, width)
+        a_gu = thin[:, :gu_rows].reshape(width, LANES)
+        a_dn = thin[:, gu_rows:].reshape(FEEDFWD_WIDTH, LANES)
+        came = plan.exchange(sent)
+        back, ga_gu, gb_gu, ga_dn, gb_dn = call(
+            ffn_body,
+            (expert_count,),
+            [pl.BlockSpec((1, cap, sent_width), lambda i: (i, 0, 0)),
+             full((width, 2 * FEEDFWD_WIDTH)), full((FEEDFWD_WIDTH, width)), full((width, LANES)),
+             full((LANES, 2 * FEEDFWD_WIDTH)), full((FEEDFWD_WIDTH, LANES)), full((LANES, width))],
+            [pl.BlockSpec((1, cap, 2 * width), lambda i: (i, 0, 0)), full((width, LANES)),
+             full((LANES, 2 * FEEDFWD_WIDTH)), full((FEEDFWD_WIDTH, LANES)), full((LANES, width))],
+            [sds((expert_count, cap, 2 * width), BF16)] + grad_shapes,
+            scratch=accumulators,
+            name="ffn",
+        )(came, w_gu, w_dn, a_gu, b_gu, a_dn, b_dn)
+        returned = plan.exchange(back)
 
     owned_wide = plan.reduce(
         jnp.concatenate([gb_gu, gb_dn], axis=1).astype(BF16).reshape(dp_size, up_rows, -1)

time: 634 us -> 572 us (0.902)
  waiting for transfers between devices: 198 us -> 111 us
  Pallas kernels: 255 us -> 309 us
  local copies, waits for them, and re-layouts: 61.9 us -> 33.3 us
  other arithmetic: 34.1 us -> 25.9 us
  blocking collectives: 9.87 us -> 16.5 us
    ppermute x26 -> x20, waiting for transfers between devices: 188 us -> 91.2 us  [send(): return lax.ppermute(values, self.axes, pairs)]
    pallas_call x1, Pallas kernels: 65.5 us -> 120 us  [shards(): pl.pallas_call(pair_ffn_body, in_specs=[hbm] * 4, out_specs=[hbm] + [vmem...]
    slice x8 -> x0, local copies, waits for them, and re-layouts: 24.3 us -> none  [the longest x2 8.79 us: exchange(): parts = [values[0]] + [self.send(values[k + 1], moves[k]) for k in range(3)]]
    another operation x11 -> x9, other arithmetic: 12.6 us -> 3.69 us  [the longest x2 11 us: exchange(): return jnp.stack(parts)]
    reduce_scatter x2, waiting for transfers between devices: 9.49 us -> 18.2 us  [reduce(): lax.psum_scatter(sums, 'dp', scatter_dimension=0, tiled=True, axis_index_...]
    all_gather x1, blocking collectives: 9.87 us -> 16.5 us  [gather(): lax.all_gather(both, 'dp', axis=0, tiled=True, axis_index_groups=self.gro...]
    ppermute x26 -> x20, starting transfers between devices: 48.6 us -> 50.7 us  [send(): return lax.ppermute(values, self.axes, pairs)]
  transfers between devices with their start and end apart: 31 -> 25, of which waited for: 14 -> 13; matrix products, arithmetic and copies ran while one was open for 11% -> 8% of each run, Pallas kernels for 15% -> 17%
where the time goes in v2:
time: 572 us; the launch traced here: 561 us
  Pallas kernels  309 us (54%)
  waiting for transfers between devices  111 us (19%)
  starting transfers between devices  51.1 us (9%)
  local copies, waits for them, and re-layouts  33.3 us (6%)
  other arithmetic  25.9 us (5%)
  blocking collectives  16.5 us (3%)
  between operations  14.7 us (3%)
    pallas_call x1, Pallas kernels, shards(): pl.pallas_call(pair_ffn_body, in_specs=[hbm] * 4, out_specs=[hbm] + [vmem...  120 us
    ppermute x20, waiting for transfers between devices, send(): return lax.ppermute(values, self.axes, pairs)  91.2 us
    ppermute x20, starting transfers between devices, send(): return lax.ppermute(values, self.axes, pairs)  50.7 us
    pallas_call x1, Pallas kernels, shards(): call(attention_bwd_body, (pairs,), [col_spec(tok)] * 6 + [full((tok, 1)),...  48.6 us
    pallas_call x1, Pallas kernels, shards(): call(attention_fwd_body, (pairs,), [col_spec(tok)] * 3 + [full((tok, 1))]...  34.1 us
    pallas_call x1, Pallas kernels, shards(): call(functools.partial(combine_body, expert_count, kinds), (blocks,), [sm...  32.3 us
    pallas_call x1, Pallas kernels, shards(): call(proj_in_body, (blocks,), [full((1, tok)), full((tok, width)), full((...  20.7 us
    reduce_scatter x2, waiting for transfers between devices, reduce(): lax.psum_scatter(sums, 'dp', scatter_dimension=0, tiled=True, axis_index_...  18.2 us
  transfers between devices with their start and end apart: 25, of which 13 were waited for; matrix products, arithmetic and copies ran while one was open for 8% of the time, Pallas kernels for 17%

profile of v2, /device:TPU:1, one launch (start us, length us, event | category | flops | bytes accessed | tf_op | source)
XLA Modules:
  0.0 561.4 jit_solution(1841814395001900162)
XLA Ops:
  12.1 6.7 %collective-permute-start.4 = (bf16[272,768]{1,0:T(8,128)(2,1)S(1)}, bf16[272,768]{1,0:T(8,128)(2,1)S(1)}, u32[]{:S(2)}, u32[]{:S(2)}) collective-permute-start(bf16[272,768]{1,0:T(8,128)(2,1)S(1)} %pad_maximum_fusion.7), channel_id=1, source_target_pairs={{2,6},{3,7},{4,0},{5,1},{10,14},{11,15},{12,8},{13,9},{18,22},{19,... | collective-permute-start | bytes 1253384 | tf_op jit(solution)/shard_map/ppermute | solution.py:561
  20.7 5.0 collective-permute-done.3
  25.7 13.1 %collective-permute-done.5 = bf16[272,768]{1,0:T(8,128)(2,1)S(1)} collective-permute-done((bf16[272,768]{1,0:T(8,128)(2,1)S(1)}, bf16[272,768]{1,0:T(8,128)(2,1)S(1)}, u32[]{:S(2)}, u32[]{:S(2)}) %collective-permute-start.5) | collective-permute-done | bytes 417824 | tf_op jit(solution)/shard_map/ppermute | solution.py:561
  42.6 2.7 collective-permute-start.1
  45.3 4.6 collective-permute-start.2
  50.0 48.0 %collective-permute-done = bf16[112,4096]{1,0:T(8,128)(2,1)S(1)} collective-permute-done((bf16[112,4096]{1,0:T(8,128)(2,1)S(1)}, bf16[112,4096]{1,0:T(8,128)(2,1)S(1)}, u32[]{:S(2)}, u32[]{:S(2)}) %collective-permute-start) | collective-permute-done | bytes 917536 | tf_op jit(solution)/shard_map/ppermute | solution.py:561
  97.9 10.8 %collective-permute-done.2 = bf16[112,4096]{1,0:T(8,128)(2,1)S(1)} collective-permute-done((bf16[112,4096]{1,0:T(8,128)(2,1)S(1)}, bf16[112,4096]{1,0:T(8,128)(2,1)S(1)}, u32[]{:S(2)}, u32[]{:S(2)}) %collective-permute-start.2) | collective-permute-done | bytes 917536 | tf_op jit(solution)/shard_map/ppermute | solution.py:561
  114.5 5.7 %collective-permute-start.8 = (bf16[352,128]{1,0:T(8,128)(2,1)S(1)}, bf16[352,128]{1,0:T(8,128)(2,1)S(1)}, u32[]{:S(2)}, u32[]{:S(2)}) collective-permute-start(bf16[352,128]{1,0:T(8,128)(2,1)S(1)} %pad_maximum_fusion.10), channel_id=1, source_target_pairs={{2,4},{3,5},{4,2},{5,3},{10,12},{11,13},{12,10},{13,11},{18,20},{1... | collective-permute-start | bytes 270344 | tf_op jit(solution)/shard_map/ppermute | solution.py:561
  125.1 4.6 concatenate.56.small
  136.7 16.5 %all_gather.19.thin = bf16[8,352,128]{2,1,0:T(8,128)(2,1)} all-gather(bf16[2,352,128]{2,1,0:T(8,128)(2,1)S(1)} %pad_maximum_fusion.9), channel_id=1, replica_groups={{0,8,16,24},{4,12,20,28},{1,9,17,25},{5,13,21,29},{2,10,18,26},{6,14,22..., dimensions={0}, use_global_device_ids=true | all-gather | bytes 901120 | tf_op jit(solution)/shard_map/all_gather | solution.py:570
  153.2 4.1 slice.88
  165.7 20.7 %proj_in.1 = (bf16[1280,768]{1,0:T(8,128)(2,1)}, bf16[1280,768]{1,0:T(8,128)(2,1)}, f32[1280,128]{1,0:T(8,128)}, bf16[1280,768]{1,0:T(8,128)(2,1)}, bf16[1280,12...) custom-call(s32[1,1280]{1,0:T(1,128)} %place_row.1, ...), custom_call_target="tpu_custom_call" | custom-call | tf_op jit(solution)/shard_map/proj_in/pallas_call | solution.py:743
  186.4 34.1 %attention_fwd.1 = (bf16[1280,768]{1,0:T(8,128)(2,1)}, f32[1280,768]{1,0:T(8,128)}) custom-call(bf16[1280,768]{1,0:T(8,128)(2,1)} %get-tuple-element.48.query, bf16[1280,768]{1,0:T(8,128)(2,1)} %get-tuple-element.49.key, bf16[1280,768]{1,0:T(8,128)(2,1)} %get-tuple-element.50.value, s32[1280,1]{1,0:T(8,128)} %reduce_sum.33.starts), custom_call_target="tpu_custom_call" | custom-call | tf_op jit(solution)/shard_map/attention_fwd/pallas_call | solution.py:759
  220.5 10.0 %post_attn.1 = (bf16[1280,128]{1,0:T(8,128)(2,1)}, f32[1280,768]{1,0:T(8,128)}, bf16[1280,768]{1,0:T(8,128)(2,1)}, f32[1280,128]{1,0:T(8,128)}) custom-call(bf16[1280,768]{1,0:T(8,128)(2,1)} %get-tuple-element.51.attn_low.attended, bf16[1280,768]{1,0:T(8,128)(2,1)} %get-tuple-element.52.hid_s, bf16[1280,128]{1,0:T(8,128)(2,1)} %compare_convert_fusion.mask, ...), custom_call_target="tpu_custom_call" | custom-call | tf_op jit(solution)/shard_map/post_attn/pallas_call | solution.py:768
  230.5 13.2 %dispatch.1 = (f32[1280,128]{1,0:T(8,128)}, bf16[4,416,1664]{2,1,0:T(8,128)(2,1)}) custom-call(s32[4]{0:T(128)} %iota_xor_fusion.eids, f32[1280,128]{1,0:T(8,128)} %get-tuple-element.53.small_s, f32[1280,128]{1,0:T(8,128)} %get-tuple-element.57.gate, bf16[1280,768]{1,0:T(8,128)(2,1)} %get-tuple-element.55.act_two, bf16[1280,768]{1,0:T(8,128)(2,1)} %get-tuple-element.56.dy_s, ...), custom_call_target="tpu_custom_call" | custom-call | tf_op jit(solution)/shard_map/dispatch/pallas_call | solution.py:782
  245.6 119.6 %pair_ffn.1 = (bf16[4,416,1536]{2,1,0:T(8,128)(2,1)}, f32[768,128]{1,0:T(8,128)}, f32[128,4096]{1,0:T(8,128)}, f32[2048,128]{1,0:T(8,128)}, f32[128,768]{1,0:T(8,128)}) custom-call(bf16[4,416,1664]{2,1,0:T(8,128)(2,1)} %get-tuple-element.60.sent, bf16[8,112,4096]{2,1,0:T(8,128)(2,1)} %all-gather.5.cloned.1.call-done.wide, ...), custom_call_target="tpu_custom_call" | custom-call | tf_op jit(solution)/shard_map/pair_ffn/pallas_call | solution.py:804
  365.2 32.3 %combine.1 = (bf16[1280,768]{1,0:T(8,128)(2,1)}, f32[1280,768]{1,0:T(8,128)}, bf16[1280,768]{1,0:T(8,128)(2,1)}, f32[1280,128]{1,0:T(8,128)}, f32[768,128]{1,0:T(8,128)}, /*index=5*/f32[128,768]{1,0:T(8,128)}) custom-call(s32[4]{0:T(128)} %iota_xor_fusion.eids, f32[1280,768]{1,0:T(8,128)} %get-tuple-element.54.resid, ...), custom_call_target="tpu_custom_call" | custom-call | tf_op jit(solution)/shard_map/combine/pallas_call | solution.py:855
  397.5 48.6 %attention_bwd.1 = (bf16[1280,768]{1,0:T(8,128)(2,1)}, bf16[1280,768]{1,0:T(8,128)(2,1)}, bf16[1280,768]{1,0:T(8,128)(2,1)}) custom-call(bf16[1280,768]{1,0:T(8,128)(2,1)} %get-tuple-element.48.query, bf16[1280,768]{1,0:T(8,128)(2,1)} %get-tuple-element.49.key, bf16[1280,768]{1,0:T(8,128)(2,1)} %get-tuple-element.50.value, ...), custom_call_target="tpu_custom_call" | custom-call | tf_op jit(solution)/shard_map/attention_bwd/pallas_call | solution.py:870
  446.1 14.8 %input_grad.1 = (bf16[1280,768]{1,0:T(8,128)(2,1)}, bf16[1280,768]{1,0:T(8,128)(2,1)}, f32[768,128]{1,0:T(8,128)}, f32[128,2304]{1,0:T(8,128)}) custom-call(bf16[1280,768]{1,0:T(8,128)(2,1)} %get-tuple-element.66.d_query, bf16[1280,768]{1,0:T(8,128)(2,1)} %get-tuple-element.67.d_key, bf16[1280,768]{1,0:T(8,128)(2,1)} %get-tuple-element.68.d_value, ...), custom_call_target="tpu_custom_call" | custom-call | tf_op jit(solution)/shard_map/input_grad/pallas_call | solution.py:880
  469.8 7.2 %collective-permute-done.10 = bf16[2,4,4,4608]{3,2,1,0:T(4,128)(2,1)S(1)} collective-permute-done((bf16[2,4,4,4608]{3,2,1,0:T(4,128)(2,1)S(1)}, bf16[2,4,4,4608]{3,2,1,0:T(4,128)(2,1)S(1)}, u32[]{:S(2)}, u32[]{:S(2)}) %collective-permute-start.10) | collective-permute-done | bytes 294944 | tf_op jit(solution)/shard_map/ppermute | solution.py:561
  490.3 15.3 %to_rows.1 = (bf16[1280,768]{1,0:T(8,128)(2,1)}, f32[1280,768]{1,0:T(8,128)}, f32[1280,128]{1,0:T(8,128)}) custom-call(s32[1280,1]{1,0:T(8,128)} %copy.81.place_col, bf16[1280,768]{1,0:T(8,128)(2,1)} %get-tuple-element.62.out_s, f32[1280,128]{1,0:T(8,128)} %get-tuple-element.63.d_logits, bf16[1280,768]{1,0:T(8,128)(2,1)} %get-tuple-element.72.high, ...), custom_call_target="tpu_custom_call" | custom-call | tf_op jit(solution)/shard_map/to_rows/pallas_call | solution.py:905
  510.3 7.4 %collective-permute-start.16 = (bf16[352,128]{1,0:T(8,128)(2,1)S(1)}, bf16[352,128]{1,0:T(8,128)(2,1)S(1)}, u32[]{:S(2)}, u32[]{:S(2)}) collective-permute-start(bf16[352,128]{1,0:T(8,128)(2,1)S(1)} %get-tuple-element.155), channel_id=1, source_target_pairs={{2,4},{3,5},{4,2},{5,3},{10,12},{11,13},{12,10},{13,11},{18,20},{1... | collective-permute-start | bytes 270344 | tf_op jit(solution)/shard_map/ppermute | solution.py:561
  522.3 17.7 %reduce-scatter.5.cloned.1.call-done = bf16[2,16,4864]{2,1,0:T(8,128)(2,1)} async-done(((bf16[8,16,4864]{2,1,0:T(8,128)(2,1)}), bf16[2,16,4864]{2,1,0:T(8,128)(2,1)}) %reduce-scatter.5.cloned.1.call-update) | async-done | bytes 311312 | tf_op jit(solution)/shard_map/reduce_scatter | solution.py:576
  542.4 4.6 collective-permute-start.19
  (177 shorter events, 79.4 us)
Async XLA Ops:
  7.2 146.1 %all-gather.9.cloned.1.call-start = ((), (), s32[]{:S(2)}) async-start(), calls=%async_computation.6 | async-start | bytes 7028736 | tf_op jit(solution)/shard_map/all_gather | solution.py:695
  9.7 234.0 %all-gather.7.cloned.1.call-start = ((), (), s32[]{:S(2)}) async-start(), calls=%async_computation.3 | async-start | bytes 4177920 | tf_op jit(solution)/shard_map/all_gather | solution.py:570
  10.8 14.9 %collective-permute-start.3 = (bf16[272,768]{1,0:T(8,128)(2,1)S(1)}, bf16[272,768]{1,0:T(8,128)(2,1)S(1)}, u32[]{:S(2)}, u32[]{:S(2)}) collective-permute-start(bf16[272,768]{1,0:T(8,128)(2,1)S(1)} %pad_maximum_fusion.7), channel_id=1, source_target_pairs={{0,2},{1,3},{6,4},{7,5},{8,10},{9,11},{14,12},{15,13},{16,18},{17,... | collective-permute-start | bytes 1253384 | tf_op jit(solution)/shard_map/ppermute | solution.py:561
  12.1 13.6 %collective-permute-start.4 = (bf16[272,768]{1,0:T(8,128)(2,1)S(1)}, bf16[272,768]{1,0:T(8,128)(2,1)S(1)}, u32[]{:S(2)}, u32[]{:S(2)}) collective-permute-start(bf16[272,768]{1,0:T(8,128)(2,1)S(1)} %pad_maximum_fusion.7), channel_id=1, source_target_pairs={{2,6},{3,7},{4,0},{5,1},{10,14},{11,15},{12,8},{13,9},{18,22},{19,... | collective-permute-start | bytes 1253384 | tf_op jit(solution)/shard_map/ppermute | solution.py:561
  18.8 20.0 %collective-permute-start.5 = (bf16[272,768]{1,0:T(8,128)(2,1)S(1)}, bf16[272,768]{1,0:T(8,128)(2,1)S(1)}, u32[]{:S(2)}, u32[]{:S(2)}) collective-permute-start(bf16[272,768]{1,0:T(8,128)(2,1)S(1)} %pad_maximum_fusion.7), channel_id=1, source_target_pairs={{2,4},{3,5},{4,2},{5,3},{10,12},{11,13},{12,10},{13,11},{18,20},{1... | collective-permute-start | bytes 1253384 | tf_op jit(solution)/shard_map/ppermute | solution.py:561
  40.9 204.8 %all-gather.5.cloned.1.call-start = ((), (), s32[]{:S(2)}) async-start(), calls=%async_computation.2 | async-start | bytes 9175040 | tf_op jit(solution)/shard_map/all_gather | solution.py:570
  41.3 56.6 %collective-permute-start = (bf16[112,4096]{1,0:T(8,128)(2,1)S(1)}, bf16[112,4096]{1,0:T(8,128)(2,1)S(1)}, u32[]{:S(2)}, u32[]{:S(2)}) collective-permute-start(bf16[112,4096]{1,0:T(8,128)(2,1)S(1)} %pad_maximum_fusion.2), channel_id=1, source_target_pairs={{0,2},{1,3},{6,4},{7,5},{8,10},{9,11},{14,12},{15,13},{16,18},{17,... | collective-permute-start | bytes 2752520 | tf_op jit(solution)/shard_map/ppermute | solution.py:561
  42.6 55.3 %collective-permute-start.1 = (bf16[112,4096]{1,0:T(8,128)(2,1)S(1)}, bf16[112,4096]{1,0:T(8,128)(2,1)S(1)}, u32[]{:S(2)}, u32[]{:S(2)}) collective-permute-start(bf16[112,4096]{1,0:T(8,128)(2,1)S(1)} %pad_maximum_fusion.2), channel_id=1, source_target_pairs={{2,6},{3,7},{4,0},{5,1},{10,14},{11,15},{12,8},{13,9},{18,22},{19,... | collective-permute-start | bytes 2752520 | tf_op jit(solution)/shard_map/ppermute | solution.py:561
  45.3 63.5 %collective-permute-start.2 = (bf16[112,4096]{1,0:T(8,128)(2,1)S(1)}, bf16[112,4096]{1,0:T(8,128)(2,1)S(1)}, u32[]{:S(2)}, u32[]{:S(2)}) collective-permute-start(bf16[112,4096]{1,0:T(8,128)(2,1)S(1)} %pad_maximum_fusion.2), channel_id=1, source_target_pairs={{2,4},{3,5},{4,2},{5,3},{10,12},{11,13},{12,10},{13,11},{18,20},{1... | collective-permute-start | bytes 2752520 | tf_op jit(solution)/shard_map/ppermute | solution.py:561
  111.0 397.1 %reduce-scatter.3.cloned.1.call-start = ((), (), s32[]{:S(2)}) async-start(), calls=%async_computation.4 | async-start | bytes 901120 | tf_op jit(solution)/shard_map/reduce_scatter | solution.py:576
  111.7 24.9 %collective-permute-start.6 = (bf16[352,128]{1,0:T(8,128)(2,1)S(1)}, bf16[352,128]{1,0:T(8,128)(2,1)S(1)}, u32[]{:S(2)}, u32[]{:S(2)}) collective-permute-start(bf16[352,128]{1,0:T(8,128)(2,1)S(1)} %pad_maximum_fusion.10), channel_id=1, source_target_pairs={{0,2},{1,3},{6,4},{7,5},{8,10},{9,11},{14,12},{15,13},{16,18},{17,... | collective-permute-start | bytes 270344 | tf_op jit(solution)/shard_map/ppermute | solution.py:561
  113.0 23.6 %collective-permute-start.7 = (bf16[352,128]{1,0:T(8,128)(2,1)S(1)}, bf16[352,128]{1,0:T(8,128)(2,1)S(1)}, u32[]{:S(2)}, u32[]{:S(2)}) collective-permute-start(bf16[352,128]{1,0:T(8,128)(2,1)S(1)} %pad_maximum_fusion.10), channel_id=1, source_target_pairs={{2,6},{3,7},{4,0},{5,1},{10,14},{11,15},{12,8},{13,9},{18,22},{19,... | collective-permute-start | bytes 270344 | tf_op jit(solution)/shard_map/ppermute | solution.py:561
  114.5 22.1 %collective-permute-start.8 = (bf16[352,128]{1,0:T(8,128)(2,1)S(1)}, bf16[352,128]{1,0:T(8,128)(2,1)S(1)}, u32[]{:S(2)}, u32[]{:S(2)}) collective-permute-start(bf16[352,128]{1,0:T(8,128)(2,1)S(1)} %pad_maximum_fusion.10), channel_id=1, source_target_pairs={{2,4},{3,5},{4,2},{5,3},{10,12},{11,13},{12,10},{13,11},{18,20},{1... | collective-permute-start | bytes 270344 | tf_op jit(solution)/shard_map/ppermute | solution.py:561
  468.6 8.5 %collective-permute-start.10 = (bf16[2,4,4,4608]{3,2,1,0:T(4,128)(2,1)S(1)}, bf16[2,4,4,4608]{3,2,1,0:T(4,128)(2,1)S(1)}, u32[]{:S(2)}, u32[]{:S(2)}) collective-permute-start(bf16[2,4,4,4608]{3,2,1,0:T(4,128)(2,1)S(1)} %dynamic-slice_bitcast_fusion.1), channel_id=1, source_target_pairs={{0,16},{1,17},{2,18},{3,19},{4,20},{5,21},{6,22},{7,23},{8,24},{9,... | collective-permute-start | bytes 884744 | tf_op jit(solution)/shard_map/ppermute | solution.py:561
  477.9 4.6 collective-permute-start.11
  481.5 58.5 %reduce-scatter.5.cloned.1.call-start = ((), (), s32[]{:S(2)}) async-start(), calls=%async_computation.5 | async-start | bytes 1556480 | tf_op jit(solution)/shard_map/reduce_scatter | solution.py:576
  483.6 4.2 collective-permute-start.12
  487.9 19.7 %collective-permute-start.13 = (bf16[1,4,4608]{2,1,0:T(4,128)(2,1)S(1)}, bf16[1,4,4608]{2,1,0:T(4,128)(2,1)S(1)}, u32[]{:S(2)}, u32[]{:S(2)}) collective-permute-start(bf16[1,4,4608]{2,1,0:T(4,128)(2,1)S(1)} %constant_dynamic-slice_fusion.1), channel_id=1, source_target_pairs={{0,1},{1,0},{2,3},{3,2},{4,5},{5,4},{6,7},{7,6},{8,9},{9,8},{10,11... | collective-permute-start | bytes 110600 | tf_op jit(solution)/shard_map/ppermute | solution.py:561
  509.0 12.6 %collective-permute-start.14 = (bf16[352,128]{1,0:T(8,128)(2,1)S(1)}, bf16[352,128]{1,0:T(8,128)(2,1)S(1)}, u32[]{:S(2)}, u32[]{:S(2)}) collective-permute-start(bf16[352,128]{1,0:T(8,128)(2,1)S(1)} %get-tuple-element.155), channel_id=1, source_target_pairs={{0,4},{1,5},{6,2},{7,3},{8,12},{9,13},{14,10},{15,11},{16,20},{17,... | collective-permute-start | bytes 270344 | tf_op jit(solution)/shard_map/ppermute | solution.py:561
  510.3 11.3 %collective-permute-start.16 = (bf16[352,128]{1,0:T(8,128)(2,1)S(1)}, bf16[352,128]{1,0:T(8,128)(2,1)S(1)}, u32[]{:S(2)}, u32[]{:S(2)}) collective-permute-start(bf16[352,128]{1,0:T(8,128)(2,1)S(1)} %get-tuple-element.155), channel_id=1, source_target_pairs={{2,4},{3,5},{4,2},{5,3},{10,12},{11,13},{12,10},{13,11},{18,20},{1... | collective-permute-start | bytes 270344 | tf_op jit(solution)/shard_map/ppermute | solution.py:561
  517.7 3.9 collective-permute-start.15
  541.1 8.0 %collective-permute-start.17 = (bf16[16,4864]{1,0:T(8,128)(2,1)S(1)}, bf16[16,4864]{1,0:T(8,128)(2,1)S(1)}, u32[]{:S(2)}, u32[]{:S(2)}) collective-permute-start(bf16[16,4864]{1,0:T(8,128)(2,1)S(1)} %get-tuple-element.153), channel_id=1, source_target_pairs={{0,4},{1,5},{6,2},{7,3},{8,12},{9,13},{14,10},{15,11},{16,20},{17,... | collective-permute-start | bytes 466952 | tf_op jit(solution)/shard_map/ppermute | solution.py:561
  542.4 10.8 %collective-permute-start.19 = (bf16[16,4864]{1,0:T(8,128)(2,1)S(1)}, bf16[16,4864]{1,0:T(8,128)(2,1)S(1)}, u32[]{:S(2)}, u32[]{:S(2)}) collective-permute-start(bf16[16,4864]{1,0:T(8,128)(2,1)S(1)} %get-tuple-element.153), channel_id=1, source_target_pairs={{2,4},{3,5},{4,2},{5,3},{10,12},{11,13},{12,10},{13,11},{18,20},{1... | collective-permute-start | bytes 466952 | tf_op jit(solution)/shard_map/ppermute | solution.py:561
  547.0 3.9 collective-permute-start.18
  (23 other events, 180.3 us)
Sparse Core Ops, SparseCore 0:
  11.4 105.3 all-gather.8
  118.7 47.0 all-gather.6
  167.6 77.9 all-gather.4
  481.7 26.3 reduce-scatter.2
  511.1 28.9 reduce-scatter.4

commit v3 on v2

--- a/solution.py
+++ b/solution.py
@@ -20,6 +20,7 @@
 CHOICE_LANE = 48
 EPSILON = 1e-06
 VMEM_BYTES = 60 * 2**20
+MESH_ID = pl.DeviceIdType.MESH
 
 F32 = jnp.float32
 BF16 = jnp.bfloat16
@@ -197,6 +198,294 @@
     d_value[...] = vacc[...].astype(BF16)
 
 
+def start_kernel(send_to, hear_from, count):
+    barrier = pltpu.get_barrier_semaphore()
+    for device, remote in hear_from:
+        if remote is None:
+            pl.semaphore_signal(barrier, inc=1, device_id=device, device_id_type=MESH_ID)
+        else:
+
+            @pl.when(remote)
+            def _(device=device):
+                pl.semaphore_signal(barrier, inc=1, device_id=device, device_id_type=MESH_ID)
+
+    pl.semaphore_wait(barrier, count)
+
+
+def pair_attention_bwd_body(
+    query, key, value, dout, attended, lse, starts, cosine, sine, ga_gu, gb_gu, ga_dn, gb_dn,
+    d_query, d_key, d_value, own_ga_gu, own_gb_gu, own_ga_dn, own_gb_dn,
+    kacc, vacc, r_ga_gu, r_gb_gu, r_ga_dn, r_gb_dn, send_sems, recv_sems,
+):
+    dp, z = lax.axis_index("dp"), lax.axis_index("expert")
+    core, spot, half = dp % 2, dp // 2, z // 2
+    own = z % 2 + 2 * core
+    far = (z + 2) % 4
+    at_home = core == half
+    away = 1 - (core * half + (1 - core) * (1 - half))
+    slot = 2 * spot + away
+    groups = (
+        (ga_gu, r_ga_gu, own_ga_gu), (gb_gu, r_gb_gu, own_gb_gu),
+        (ga_dn, r_ga_dn, own_ga_dn), (gb_dn, r_gb_dn, own_gb_dn),
+    )
+    owners = 8
+
+    def piece(i, d):
+        source, target, _ = groups[i]
+        count = target.shape[1]
+        return source.at[pl.ds(pl.multiple_of(d * count, 16), count)]
+
+    def push(i, d):
+        return pltpu.make_async_remote_copy(
+            src_ref=piece(i, d), dst_ref=groups[i][1].at[slot], send_sem=send_sems.at[i, d],
+            recv_sem=recv_sems.at[i, slot], device_id=(d, own), device_id_type=MESH_ID,
+        )
+
+    def keep(i):
+        return pltpu.make_async_copy(
+            piece(i, dp), groups[i][1].at[2 * spot], recv_sems.at[i, 2 * spot]
+        )
+
+    def arrival(i, s):
+        return pltpu.make_async_remote_copy(
+            src_ref=piece(i, 0), dst_ref=groups[i][1].at[s], send_sem=send_sems.at[i, 0],
+            recv_sem=recv_sems.at[i, s], device_id=(0, own), device_id_type=MESH_ID,
+        )
+
+    @pl.when(pl.program_id(0) == 0)
+    def _():
+        senders = []
+        for m in range(owners // 2):
+            device = 2 * m + half
+            senders.append(((device, z), device != dp))
+            senders.append(((device, far), None))
+        start_kernel(None, senders, owners - 1 + away)
+
+        def send(d, carry):
+            mine = at_home & (d == dp)
+
+            @pl.when(mine)
+            def _():
+                for i in range(4):
+                    keep(i).start()
+
+            @pl.when(jnp.logical_not(mine))
+            def _():
+                for i in range(4):
+                    push(i, d).start()
+
+            return carry
+
+        lax.fori_loop(0, owners, send, 0)
+
+    attention_bwd_body(
+        query, key, value, dout, attended, lse, starts, cosine, sine, d_query, d_key, d_value,
+        kacc, vacc,
+    )
+
+    @pl.when(pl.program_id(0) == pl.num_programs(0) - 1)
+    def _():
+        def finish(s, carry):
+            mine = at_home & (s == 2 * spot)
+
+            @pl.when(mine)
+            def _():
+                for i in range(4):
+                    keep(i).wait()
+
+            @pl.when(jnp.logical_not(mine))
+            def _():
+                for i in range(4):
+                    arrival(i, s).wait_recv()
+
+            @pl.when(jnp.logical_not(at_home & (s == dp)))
+            def _():
+                for i in range(4):
+                    push(i, s).wait_send()
+
+            return carry
+
+        lax.fori_loop(0, owners, finish, 0)
+        for _, target, out in groups:
+            total = target[0].astype(F32)
+            for s in range(1, owners):
+                total = total + target[s].astype(F32)
+            out[...] = total
+
+
+def pair_tail_body(
+    place_col, d_query, d_key, d_value, low_qkv, act_one, mask, a_in, b_out, gain, ga_out, gb_out,
+    d_logits, hid_hbm, resid_hbm, w_hbm, out_hbm,
+    out, grad_hidden, grad_gate, own_ga_qkv, own_gb_qkv, own_ga_out, own_gb_out,
+    hid_s, d_resid, w_qkv, out_s, high, lower, d_low_all, ga_sum, gb_sum,
+    s_ga_qkv, s_gb_qkv, s_ga_out, s_gb_out, r_ga_qkv, r_gb_qkv, r_ga_out, r_gb_out,
+    thin_out, wide_out, thin_in, wide_in, load_sems, send_sems, recv_sems, far_send, far_recv,
+):
+    dp, z = lax.axis_index("dp"), lax.axis_index("expert")
+    others, planes = 7, 3
+    tok = place_col.shape[0]
+    blocks = tok // ROW_BLOCK
+    loads = [
+        pltpu.make_async_copy(source, target, load_sems.at[i])
+        for i, (source, target) in enumerate(
+            ((w_hbm, w_qkv), (hid_hbm, hid_s), (resid_hbm, d_resid), (out_hbm, out_s))
+        )
+    ]
+    for load in loads:
+        load.start()
+    start_kernel(
+        None,
+        [(((dp + i) % 8, z), None) for i in range(1, 8)] + [((dp, (z + j) % 4), None) for j in (1, 2, 3)],
+        others + planes,
+    )
+    ga_sum[...] = jnp.zeros_like(ga_sum)
+    gb_sum[...] = jnp.zeros_like(gb_sum)
+    parts = [slice(p * MODEL_WIDTH, (p + 1) * MODEL_WIDTH) for p in range(3)]
+    d_refs = (d_query, d_key, d_value)
+
+    def block_rows(b):
+        return pl.ds(pl.multiple_of(b * ROW_BLOCK, ROW_BLOCK), ROW_BLOCK)
+
+    def sums(b, carry):
+        rows = block_rows(b)
+        low = low_qkv[rows, :]
+        d_low = jnp.zeros((ROW_BLOCK, LANES), F32)
+        for cols, ref in zip(parts, d_refs):
+            grad = ref[rows, :]
+            d_low = d_low + dot_nt(grad, b_out[:, cols])
+            gb_sum[:, cols] += dot_tn(low, grad)
+        d_low = (d_low * mask[rows, :].astype(F32)).astype(BF16)
+        d_low_all[rows, :] = d_low
+        ga_sum[...] += dot_tn(act_one[rows, :], d_low)
+        return carry
+
+    lax.fori_loop(0, blocks, sums, 0)
+    s_ga_qkv[...] = ga_sum[...].astype(BF16)
+    s_gb_qkv[...] = gb_sum[...].astype(BF16)
+    s_ga_out[...] = ga_out[...].astype(BF16)
+    s_gb_out[...] = gb_out[...].astype(BF16)
+    groups = (
+        (s_ga_qkv, r_ga_qkv), (s_gb_qkv, r_gb_qkv), (s_ga_out, r_ga_out), (s_gb_out, r_gb_out),
+    )
+
+    def share(i, d):
+        count = groups[i][1].shape[1]
+        return groups[i][0].at[pl.ds(pl.multiple_of(d * count, 16), count)]
+
+    def near(i, n):
+        goal = (dp + n + 1) % 8
+        return pltpu.make_async_remote_copy(
+            src_ref=share(i, goal), dst_ref=groups[i][1].at[n], send_sem=send_sems.at[i, n],
+            recv_sem=recv_sems.at[i, n], device_id=(goal, z), device_id_type=MESH_ID,
+        )
+
+    def send_near(n, carry):
+        for i in range(4):
+            near(i, n).start()
+        return carry
+
+    lax.fori_loop(0, others, send_near, 0)
+
+    for load in loads[:3]:
+        load.wait()
+
+    def back(b, carry):
+        rows = block_rows(b)
+        d_act = dot_nt(d_low_all[rows, :], a_in[...])
+        for cols, ref in zip(parts, d_refs):
+            d_act = d_act + dot_nt(ref[rows, :], w_qkv[:, cols])
+        hid = hid_s[rows, :].astype(F32)
+        scale = lax.rsqrt(jnp.mean(hid * hid, axis=-1, keepdims=True) + EPSILON)
+        weighted = d_act * gain[...]
+        grad_hid = d_resid[rows, :] + (
+            scale * weighted
+            - hid * (scale * scale * scale) * jnp.mean(hid * weighted, axis=-1, keepdims=True)
+        )
+        top = grad_hid.astype(BF16)
+        high[rows, :] = top
+        lower[rows, :] = (grad_hid - top.astype(F32)).astype(BF16)
+        return carry
+
+    lax.fori_loop(0, blocks, back, 0)
+
+    def near_done(n, carry):
+        for i in range(4):
+            near(i, n).wait_recv()
+        return carry
+
+    lax.fori_loop(0, others, near_done, 0)
+    totals = []
+    for i in range(4):
+        total = share(i, dp)[...].astype(F32)
+        for n in range(others):
+            total = total + groups[i][1][n].astype(F32)
+        totals.append(total)
+    a_qkv, b_qkv, a_o, b_o = totals
+    a_count, b_count = a_qkv.shape[0] // 4, b_qkv.shape[0] // 4
+    for p in range(4):
+        a_rows, b_rows = slice(p * a_count, (p + 1) * a_count), slice(p * b_count, (p + 1) * b_count)
+        thin_out[p, :a_count, :LANES] = a_qkv[a_rows].astype(BF16)
+        thin_out[p, :a_count, LANES:] = a_o[a_rows].astype(BF16)
+        thin_out[p, a_count:, :] = jnp.zeros((thin_out.shape[1] - a_count, 2 * LANES), BF16)
+        wide_out[p] = jnp.concatenate(
+            [b_qkv[b_rows, cols] for cols in parts] + [b_o[b_rows]], axis=0
+        ).astype(BF16)
+
+    def far(i, j):
+        goal = (z + j + 1) % 4
+        source, target = ((thin_out, thin_in), (wide_out, wide_in))[i]
+        return pltpu.make_async_remote_copy(
+            src_ref=source.at[goal], dst_ref=target.at[j], send_sem=far_send.at[i, j],
+            recv_sem=far_recv.at[i, j], device_id=(dp, goal), device_id_type=MESH_ID,
+        )
+
+    for j in range(planes):
+        for i in range(2):
+            far(i, j).start()
+    loads[3].wait()
+
+    def to_rows(b, carry):
+        rows = block_rows(b)
+        perm = hot_matrix(place_col[rows, :] == iota((ROW_BLOCK, tok), 1))
+        out[rows, :] = dot(perm, out_s[...]).astype(BF16)
+        grad_hidden[rows, :] = dot(perm, high[...]) + dot(perm, lower[...])
+        top, mid, last = split_three(d_logits[...])
+        grad_gate[rows, :] = dot(perm, top) + (dot(perm, mid) + dot(perm, last))
+        return carry
+
+    lax.fori_loop(0, blocks, to_rows, 0)
+    for j in range(planes):
+        for i in range(2):
+            far(i, j).wait_recv()
+    thin = thin_out[z].astype(F32)
+    wide = wide_out[z].astype(F32)
+    for j in range(planes):
+        thin = thin + thin_in[j].astype(F32)
+        wide = wide + wide_in[j].astype(F32)
+    own_ga_qkv[...] = thin[:a_count, :LANES]
+    own_ga_out[...] = thin[:a_count, LANES:]
+    for p, cols in enumerate(parts):
+        own_gb_qkv[:, cols] = wide[p * b_count : (p + 1) * b_count]
+    own_gb_out[...] = wide[3 * b_count : 4 * b_count]
+
+    def sent(n, carry):
+        for i in range(4):
+            near(i, n).wait_send()
+        return carry
+
+    lax.fori_loop(0, others, sent, 0)
+    for j in range(planes):
+        for i in range(2):
+            far(i, j).wait_send()
+
+
+def split_three(values):
+    top = values.astype(BF16)
+    rest = values - top.astype(F32)
+    mid = rest.astype(BF16)
+    return top, mid, (rest - mid.astype(F32)).astype(BF16)
+
+
 def post_attn_body(
     kinds, attn_low, hid_s, mask, small_s, w_out, a_out, b_out, router, gain,
     low_out, resid, act_two, gate,
@@ -308,32 +597,31 @@
 
 def pair_ffn_body(
     sent, wide, mid, thin,
-    returned, ga_gu, gb_gu, ga_dn, gb_dn,
-    came, back, w_gu, w_dn, a_gu, b_gu, a_dn, b_dn, acc_out, acc_dx, acc_low, acc_dlow,
+    returned, out_ga_gu, out_gb_gu, out_ga_dn, out_gb_dn,
+    came, back, ga_gu, gb_gu, ga_dn, gb_dn, w_gu, w_dn, a_gu, b_gu, a_dn, b_dn, acc_out, acc_dx, acc_low, acc_dlow,
     load_sems, send_sems, came_sems, back_sems, done_sems,
 ):
     dp, z = lax.axis_index("dp"), lax.axis_index("expert")
     core, plane = dp % 2, z % 2
-    mesh_id = pl.DeviceIdType.MESH
 
     def peer(k):
         return (dp + (k // 2) * (1 - 2 * core), z + (k % 2) * (1 - 2 * plane))
 
     barrier = pltpu.get_barrier_semaphore()
     for k in (1, 2, 3):
-        pl.semaphore_signal(barrier, inc=1, device_id=peer(k), device_id_type=mesh_id)
+        pl.semaphore_signal(barrier, inc=1, device_id=peer(k), device_id_type=MESH_ID)
     pl.semaphore_wait(barrier, 3)
 
     def rows_out(k):
         return pltpu.make_async_remote_copy(
             src_ref=sent.at[k], dst_ref=came.at[k], send_sem=send_sems.at[k],
-            recv_sem=came_sems.at[k], device_id=peer(k), device_id_type=mesh_id,
+            recv_sem=came_sems.at[k], device_id=peer(k), device_id_type=MESH_ID,
         )
 
     def result_out(k):
         return pltpu.make_async_remote_copy(
             src_ref=back.at[k], dst_ref=returned.at[k], send_sem=back_sems.at[k],
-            recv_sem=done_sems.at[k], device_id=peer(k), device_id_type=mesh_id,
+            recv_sem=done_sems.at[k], device_id=peer(k), device_id_type=MESH_ID,
         )
 
     for k in (1, 2, 3):
@@ -388,6 +676,10 @@
         return carry
 
     lax.fori_loop(0, 4, source_step, 0)
+    for out, total in (
+        (out_ga_gu, ga_gu), (out_gb_gu, gb_gu), (out_ga_dn, ga_dn), (out_gb_dn, gb_dn),
+    ):
+        out[...] = total[...].astype(BF16)
     own_out = pltpu.make_async_copy(back.at[0], returned.at[0], done_sems.at[0])
     own_out.start()
     own_out.wait()
@@ -532,13 +824,6 @@
     grad_gate[...] = dot(perm, top) + (dot(perm, mid) + dot(perm, last))
 
 
-def split_three(values):
-    top = values.astype(BF16)
-    rest = values - top.astype(F32)
-    mid = rest.astype(BF16)
-    return top, mid, (rest - mid.astype(F32)).astype(BF16)
-
-
 class PairPlan:
     paired = True
 
@@ -571,51 +856,6 @@
 
     def expert_ids(self):
         return self.own ^ jnp.arange(self.ex, dtype=jnp.int32)
-
-    def reduce(self, sums):
-        part = lax.psum_scatter(
-            sums, "dp", scatter_dimension=0, tiled=True, axis_index_groups=self.groups
-        )
-        same = jnp.where(self.h == 0, part[0], part[1])
-        flip = jnp.where(self.h == 0, part[1], part[0])
-        over = self.send(flip, lambda d, z: (d ^ 1, z) if (z >> 1) == (d & 1) else None)
-        near = self.send(same, lambda d, z: (d, z ^ 2) if (z >> 1) != (d & 1) else None)
-        cross = self.send(flip, lambda d, z: (d ^ 1, z ^ 2) if (z >> 1) != (d & 1) else None)
-        first = jnp.where(self.local, same, over).astype(F32)
-        return first + near.astype(F32) + cross.astype(F32)
-
-    def reduce_all(self, sums):
-        values = sums.reshape((self.dp // 2, 2, self.ex) + sums.shape[1:])
-        move = lambda d, z: (d ^ 1, z)
-        values = self._halve(values, 1, self.h, move)
-        rest = self.dp // 2
-        position = lax.axis_index("dp") >> 1
-        while rest > 1:
-            rest //= 2
-            values = values.reshape((2, rest) + values.shape[1:])
-            bit = position // rest % 2
-            values = self._halve(values, 0, bit, functools.partial(self._flip_dp, 2 * rest))
-        values = values[0]
-        rest = self.ex
-        while rest > 1:
-            rest //= 2
-            values = values.reshape((2, rest) + values.shape[1:])
-            bit = self.z // rest % 2
-            values = self._halve(values, 0, bit, functools.partial(self._flip_ex, rest))
-        return values[0].astype(F32)
-
-    @staticmethod
-    def _flip_dp(bit, d, z):
-        return (d ^ bit, z)
-
-    @staticmethod
-    def _flip_ex(bit, d, z):
-        return (d, z ^ bit)
-
-    def _halve(self, values, axis, bit, move):
-        keep = lax.dynamic_index_in_dim(values, bit, axis, keepdims=False)
-        give = lax.dynamic_index_in_dim(values, 1 - bit, axis, keepdims=False)
-        return (keep.astype(F32) + self.send(give, move).astype(F32)).astype(BF16)
 
 
 class AxisPlan:
@@ -798,17 +1038,19 @@
         pltpu.VMEM((cap, width), F32), pltpu.VMEM((cap, width), F32),
         pltpu.VMEM((cap, LANES), F32), pltpu.VMEM((cap, LANES), F32),
     ]
+    hbm = pl.BlockSpec(memory_space=pl.ANY)
+    vmem = pl.BlockSpec(memory_space=pltpu.VMEM)
     if plan.paired:
-        hbm = pl.BlockSpec(memory_space=pl.ANY)
-        vmem = pl.BlockSpec(memory_space=pltpu.VMEM)
         returned, ga_gu, gb_gu, ga_dn, gb_dn = pl.pallas_call(
             pair_ffn_body,
             in_specs=[hbm] * 4,
             out_specs=[hbm] + [vmem] * 4,
-            out_shape=[sds((expert_count, cap, 2 * width), BF16)] + grad_shapes,
+            out_shape=[sds((expert_count, cap, 2 * width), BF16)]
+            + [sds(g.shape, BF16) for g in grad_shapes],
             scratch_shapes=[
                 pltpu.VMEM((expert_count, cap, sent_width), BF16),
                 pltpu.VMEM((expert_count, cap, 2 * width), BF16),
+                *[pltpu.VMEM(g.shape, F32) for g in grad_shapes],
                 pltpu.VMEM((width, 2 * FEEDFWD_WIDTH), BF16), pltpu.VMEM((FEEDFWD_WIDTH, width), BF16),
                 pltpu.VMEM((width, LANES), BF16), pltpu.VMEM((LANES, 2 * FEEDFWD_WIDTH), BF16),
                 pltpu.VMEM((FEEDFWD_WIDTH, LANES), BF16), pltpu.VMEM((LANES, width), BF16),
@@ -843,15 +1085,6 @@
         )(came, w_gu, w_dn, a_gu, b_gu, a_dn, b_dn)
         returned = plan.exchange(back)
 
-    owned_wide = plan.reduce(
-        jnp.concatenate([gb_gu, gb_dn], axis=1).astype(BF16).reshape(dp_size, up_rows, -1)
-    )
-    owned_thin = plan.reduce(
-        jnp.concatenate(
-            [ga_gu.reshape(dp_size, gu_rows, LANES), ga_dn.reshape(dp_size, dn_rows, LANES)], axis=1
-        ).astype(BF16)
-    )
-
     out_s, d_resid, d_attended, d_logits, ga_out, gb_out = call(
         functools.partial(combine_body, expert_count, kinds),
         (blocks,),
@@ -867,6 +1100,73 @@
     )(eids, resid, act_two, dy_s, gate, slot, small_s, low_out, attn_low, mask, returned,
       w_out, a_out, b_out, router, const_value, gain_two)
 
+    if plan.paired:
+        flow = dict(vmem_limit_bytes=VMEM_BYTES, has_side_effects=True)
+        own_shapes = [
+            sds((gu_rows, LANES), F32), sds((up_rows, 2 * FEEDFWD_WIDTH), F32),
+            sds((dn_rows, LANES), F32), sds((up_rows, width), F32),
+        ]
+        d_query, d_key, d_value, *expert_owned = pl.pallas_call(
+            pair_attention_bwd_body,
+            grid=(pairs,),
+            in_specs=[col_spec(tok)] * 6
+            + [full((tok, 1)), full((tok, LANES)), full((tok, LANES))]
+            + [hbm] * 4,
+            out_specs=[col_spec(tok)] * 3 + [full(s.shape) for s in own_shapes],
+            out_shape=[sds((tok, width), BF16)] * 3 + own_shapes,
+            scratch_shapes=[pltpu.VMEM((tok, LANES), F32), pltpu.VMEM((tok, LANES), F32)]
+            + [pltpu.VMEM((dp_size,) + s.shape, BF16) for s in own_shapes]
+            + [pltpu.SemaphoreType.DMA((4, dp_size)), pltpu.SemaphoreType.DMA((4, dp_size))],
+            compiler_params=pltpu.CompilerParams(collective_id=2, **flow),
+            name="pair_attention_bwd",
+        )(query, key, value, d_attended, attn_low, lse, starts, cosine, sine,
+          ga_gu, gb_gu, ga_dn, gb_dn)
+        sum_shapes = [(width, LANES), (LANES, 3 * width), (width, LANES), (LANES, width)]
+        got_shapes = [(dp_size - 1, a // dp_size, b) for a, b in sum_shapes]
+        thin_rows = -(-a_rows // 16) * 16
+        output, grad_hidden, grad_gate, *attn_owned = pl.pallas_call(
+            pair_tail_body,
+            in_specs=[vmem] * 13 + [hbm] * 4,
+            out_specs=[vmem] * 7,
+            out_shape=[
+                sds((tok, width), BF16), sds((tok, width), F32), sds((tok, LANES), F32),
+                sds((a_rows, LANES), F32), sds((b_rows, 3 * width), F32),
+                sds((a_rows, LANES), F32), sds((b_rows, width), F32),
+            ],
+            scratch_shapes=[
+                pltpu.VMEM((tok, width), BF16), pltpu.VMEM((tok, width), F32),
+                pltpu.VMEM((width, 3 * width), BF16), pltpu.VMEM((tok, width), BF16),
+                pltpu.VMEM((tok, width), BF16), pltpu.VMEM((tok, width), BF16),
+                pltpu.VMEM((tok, LANES), BF16),
+                pltpu.VMEM((width, LANES), F32), pltpu.VMEM((LANES, 3 * width), F32),
+                *[pltpu.VMEM(shape, BF16) for shape in sum_shapes + got_shapes],
+                pltpu.VMEM((expert_count, thin_rows, 2 * LANES), BF16),
+                pltpu.VMEM((expert_count, 4 * b_rows, width), BF16),
+                pltpu.VMEM((expert_count - 1, thin_rows, 2 * LANES), BF16),
+                pltpu.VMEM((expert_count - 1, 4 * b_rows, width), BF16),
+                pltpu.SemaphoreType.DMA((4,)),
+                pltpu.SemaphoreType.DMA((4, dp_size - 1)), pltpu.SemaphoreType.DMA((4, dp_size - 1)),
+                pltpu.SemaphoreType.DMA((2, expert_count - 1)),
+                pltpu.SemaphoreType.DMA((2, expert_count - 1)),
+            ],
+            compiler_params=pltpu.CompilerParams(collective_id=3, **flow),
+            name="pair_tail",
+        )(place[:, None], d_query, d_key, d_value, low_qkv, act_one, mask, a_qkv, b_qkv, gain_one,
+          ga_out, gb_out, d_logits, hid_s, d_resid, w_qkv, out_s)
+        return (
+            output, grad_hidden, grad_gate[:, :kinds], *attn_owned,
+            *[expert_owned[i][None] for i in range(4)],
+        )
+
+    owned_wide = plan.reduce(
+        jnp.concatenate([gb_gu, gb_dn], axis=1).astype(BF16).reshape(dp_size, up_rows, -1)
+    )
+    owned_thin = plan.reduce(
+        jnp.concatenate(
+            [ga_gu.reshape(dp_size, gu_rows, LANES), ga_dn.reshape(dp_size, dn_rows, LANES)], axis=1
+        ).astype(BF16)
+    )
+
     d_query, d_key, d_value = call(
         attention_bwd_body,
         (pairs,),

time: 572 us -> 524 us (0.916)
  waiting for transfers between devices: 111 us -> 78.3 us
  starting transfers between devices: 51.1 us -> 27.1 us
  Pallas kernels: 309 us -> 331 us
  other arithmetic: 25.9 us -> 15.8 us
    ppermute x20 -> x9, starting transfers between devices: 50.7 us -> 27 us  [send(): return lax.ppermute(values, self.axes, pairs)]
    pallas_call x3 -> x2, Pallas kernels: 78.7 us -> 102 us  [the longest x1 53.1 us: shards(): pl.pallas_call(pair_attention_bwd_body, grid=(pairs,), in_specs=[col_spec...]
    reduce_scatter x2 -> x0, waiting for transfers between devices: 18.2 us -> none  [reduce(): lax.psum_scatter(sums, 'dp', scatter_dimension=0, tiled=True, axis_index_...]
    ppermute x20 -> x9, waiting for transfers between devices: 91.2 us -> 77 us  [send(): return lax.ppermute(values, self.axes, pairs)]
    unnamed x51 -> x60, local copies, waits for them, and re-layouts: 4.69 us -> 12.6 us
  transfers between devices with their start and end apart: 25 -> 12, of which waited for: 13 -> 5; matrix products, arithmetic and copies ran while one was open for 8% -> 7% of each run, Pallas kernels for 17% -> 15%
where the time goes in v3:
time: 524 us; the launch traced here: 517 us
  Pallas kernels  331 us (63%)
  waiting for transfers between devices  78.3 us (15%)
  local copies, waits for them, and re-layouts  34 us (6%)
  starting transfers between devices  27.1 us (5%)
  blocking collectives  16.4 us (3%)
  other arithmetic  15.8 us (3%)
  between operations  14.7 us (3%)
    pallas_call x1, Pallas kernels, shards(): pl.pallas_call(pair_ffn_body, in_specs=[hbm] * 4, out_specs=[hbm] + [vmem...  119 us
    ppermute x9, waiting for transfers between devices, send(): return lax.ppermute(values, self.axes, pairs)  77 us
    pallas_call x1, Pallas kernels, shards(): pl.pallas_call(pair_attention_bwd_body, grid=(pairs,), in_specs=[col_spec...  53.1 us
    pallas_call x1, Pallas kernels, shards(): pl.pallas_call(pair_tail_body, in_specs=[vmem] * 13 + [hbm] * 4, out_spec...  48.5 us
    pallas_call x1, Pallas kernels, shards(): call(attention_fwd_body, (pairs,), [col_spec(tok)] * 3 + [full((tok, 1))]...  34.1 us
    pallas_call x1, Pallas kernels, shards(): call(functools.partial(combine_body, expert_count, kinds), (blocks,), [sm...  32.3 us
    ppermute x9, starting transfers between devices, send(): return lax.ppermute(values, self.axes, pairs)  27 us
    pallas_call x1, Pallas kernels, shards(): call(proj_in_body, (blocks,), [full((1, tok)), full((tok, width)), full((...  20.7 us
  transfers between devices with their start and end apart: 12, of which 5 were waited for; matrix products, arithmetic and copies ran while one was open for 7% of the time, Pallas kernels for 15%

profile of v3, /device:TPU:1, one launch (start us, length us, event | category | flops | bytes accessed | tf_op | source)
XLA Modules:
  0.0 517.0 jit_solution(7129853408345060775)
XLA Ops:
  12.1 6.7 %collective-permute-start.4 = (bf16[272,768]{1,0:T(8,128)(2,1)S(1)}, bf16[272,768]{1,0:T(8,128)(2,1)S(1)}, u32[]{:S(2)}, u32[]{:S(2)}) collective-permute-start(bf16[272,768]{1,0:T(8,128)(2,1)S(1)} %pad_maximum_fusion.5), channel_id=1, source_target_pairs={{2,6},{3,7},{4,0},{5,1},{10,14},{11,15},{12,8},{13,9},{18,22},{19,... | collective-permute-start | bytes 1253384 | tf_op jit(solution)/shard_map/ppermute | solution.py:846
  20.7 5.0 collective-permute-done.3
  25.7 13.2 %collective-permute-done.5 = bf16[272,768]{1,0:T(8,128)(2,1)S(1)} collective-permute-done((bf16[272,768]{1,0:T(8,128)(2,1)S(1)}, bf16[272,768]{1,0:T(8,128)(2,1)S(1)}, u32[]{:S(2)}, u32[]{:S(2)}) %collective-permute-start.5) | collective-permute-done | bytes 417824 | tf_op jit(solution)/shard_map/ppermute | solution.py:846
  42.5 2.6 collective-permute-start.1
  45.2 4.7 collective-permute-start.2
  49.9 48.0 %collective-permute-done = bf16[112,4096]{1,0:T(8,128)(2,1)S(1)} collective-permute-done((bf16[112,4096]{1,0:T(8,128)(2,1)S(1)}, bf16[112,4096]{1,0:T(8,128)(2,1)S(1)}, u32[]{:S(2)}, u32[]{:S(2)}) %collective-permute-start) | collective-permute-done | bytes 917536 | tf_op jit(solution)/shard_map/ppermute | solution.py:846
  97.9 10.9 %collective-permute-done.2 = bf16[112,4096]{1,0:T(8,128)(2,1)S(1)} collective-permute-done((bf16[112,4096]{1,0:T(8,128)(2,1)S(1)}, bf16[112,4096]{1,0:T(8,128)(2,1)S(1)}, u32[]{:S(2)}, u32[]{:S(2)}) %collective-permute-start.2) | collective-permute-done | bytes 917536 | tf_op jit(solution)/shard_map/ppermute | solution.py:846
  113.9 5.7 %collective-permute-start.8 = (bf16[352,128]{1,0:T(8,128)(2,1)S(1)}, bf16[352,128]{1,0:T(8,128)(2,1)S(1)}, u32[]{:S(2)}, u32[]{:S(2)}) collective-permute-start(bf16[352,128]{1,0:T(8,128)(2,1)S(1)} %pad_maximum_fusion.8), channel_id=1, source_target_pairs={{2,4},{3,5},{4,2},{5,3},{10,12},{11,13},{12,10},{13,11},{18,20},{1... | collective-permute-start | bytes 270344 | tf_op jit(solution)/shard_map/ppermute | solution.py:846
  125.6 4.6 concatenate.30.small
  131.1 2.4 fusion
  133.4 2.1 pad_maximum_fusion.3
  137.1 16.4 %all_gather.19.thin = bf16[8,352,128]{2,1,0:T(8,128)(2,1)} all-gather(bf16[2,352,128]{2,1,0:T(8,128)(2,1)S(1)} %pad_maximum_fusion.7), channel_id=1, replica_groups={{0,8,16,24},{4,12,20,28},{1,9,17,25},{5,13,21,29},{2,10,18,26},{6,14,22..., dimensions={0}, use_global_device_ids=true | all-gather | bytes 901120 | tf_op jit(solution)/shard_map/all_gather | solution.py:855
  153.6 4.1 slice.36
  159.1 2.4 slice.39
  166.0 20.7 %proj_in.1 = (bf16[1280,768]{1,0:T(8,128)(2,1)}, bf16[1280,768]{1,0:T(8,128)(2,1)}, f32[1280,128]{1,0:T(8,128)}, bf16[1280,768]{1,0:T(8,128)(2,1)}, bf16[1280,12...) custom-call(s32[1,1280]{1,0:T(1,128)} %place_row.1, ...), custom_call_target="tpu_custom_call" | custom-call | tf_op jit(solution)/shard_map/proj_in/pallas_call | solution.py:983
  186.7 34.1 %attention_fwd.1 = (bf16[1280,768]{1,0:T(8,128)(2,1)}, f32[1280,768]{1,0:T(8,128)}) custom-call(bf16[1280,768]{1,0:T(8,128)(2,1)} %get-tuple-element.52.query, bf16[1280,768]{1,0:T(8,128)(2,1)} %get-tuple-element.53.key, bf16[1280,768]{1,0:T(8,128)(2,1)} %get-tuple-element.54.value, s32[1280,1]{1,0:T(8,128)} %reduce_sum.33.starts), custom_call_target="tpu_custom_call" | custom-call | tf_op jit(solution)/shard_map/attention_fwd/pallas_call | solution.py:999
  220.8 10.0 %post_attn.1 = (bf16[1280,128]{1,0:T(8,128)(2,1)}, f32[1280,768]{1,0:T(8,128)}, bf16[1280,768]{1,0:T(8,128)(2,1)}, f32[1280,128]{1,0:T(8,128)}) custom-call(bf16[1280,768]{1,0:T(8,128)(2,1)} %get-tuple-element.55.attn_low.attended, bf16[1280,768]{1,0:T(8,128)(2,1)} %get-tuple-element.56.hid_s.hid_hbm, bf16[1280,128]{1,0:T(8,128)(2,1)} %compare_convert_fusion.mask, ...), custom_call_target="tpu_custom_call" | custom-call | tf_op jit(solution)/shard_map/post_attn/pallas_call | solution.py:1008
  230.8 13.2 %dispatch.1 = (f32[1280,128]{1,0:T(8,128)}, bf16[4,416,1664]{2,1,0:T(8,128)(2,1)}) custom-call(s32[4]{0:T(128)} %iota_xor_fusion.eids, f32[1280,128]{1,0:T(8,128)} %get-tuple-element.57.small_s, f32[1280,128]{1,0:T(8,128)} %get-tuple-element.61.gate, bf16[1280,768]{1,0:T(8,128)(2,1)} %get-tuple-element.59.act_two, bf16[1280,768]{1,0:T(8,128)(2,1)} %get-tuple-element.60.dy_s, ...), custom_call_target="tpu_custom_call" | custom-call | tf_op jit(solution)/shard_map/dispatch/pallas_call | solution.py:1022
  245.2 118.9 %pair_ffn.1 = (bf16[4,416,1536]{2,1,0:T(8,128)(2,1)}, bf16[768,128]{1,0:T(8,128)(2,1)}, bf16[128,4096]{1,0:T(8,128)(2,1)}, bf16[2048,128]{1,0:T(8,128)(2,1)}, bf16[128,768]{1,0:T(8,128)(2,1)}) custom-call(bf16[4,416,1664]{2,1,0:T(8,128)(2,1)} %get-tuple-element.64.sent, bf16[8,112,4096]{2,1,0:T(8,128)(2,1)} %all-gather.5.cloned.1.call-done.wide, ...), custom_call_target="tpu_custom_call" | custom-call | tf_op jit(solution)/shard_map/pair_ffn/pallas_call | solution.py:1044
  364.1 32.3 %combine.1 = (bf16[1280,768]{1,0:T(8,128)(2,1)}, f32[1280,768]{1,0:T(8,128)}, bf16[1280,768]{1,0:T(8,128)(2,1)}, f32[1280,128]{1,0:T(8,128)}, f32[768,128]{1,0:T(8,128)}, /*index=5*/f32[128,768]{1,0:T(8,128)}) custom-call(s32[4]{0:T(128)} %iota_xor_fusion.eids, f32[1280,768]{1,0:T(8,128)} %get-tuple-element.58.resid, ...), custom_call_target="tpu_custom_call" | custom-call | tf_op jit(solution)/shard_map/combine/pallas_call | solution.py:1088
  396.4 53.1 %pair_attention_bwd.1 = (bf16[1280,768]{1,0:T(8,128)(2,1)}, bf16[1280,768]{1,0:T(8,128)(2,1)}, bf16[1280,768]{1,0:T(8,128)(2,1)}, f32[96,128]{1,0:T(8,128)}, f32...) custom-call(bf16[1280,768]{1,0:T(8,128)(2,1)} %get-tuple-element.52.query, ...), custom_call_target="tpu_custom_call" | custom-call | tf_op jit(solution)/shard_map/pair_attention_bwd/pallas_call | solution.py:1109
  449.5 48.5 %pair_tail.1 = (bf16[1280,768]{1,0:T(8,128)(2,1)}, f32[1280,768]{1,0:T(8,128)}, f32[1280,128]{1,0:T(8,128)}, f32[24,128]{1,0:T(8,128)}, f32[4,2304]{1,0:T(4,128)}, /*index=5*/f32[24,128]{1,0:T(8,128)}, f32[4,768]{1,0:T(4,128)}) custom-call(s32[1280,1]{1,0:T(8,128)} %copy.81.place_col, bf16[1280,768]{1,0:T(8,128)(2,1)} %get-tuple-element.72.d_query, ...), custom_call_target="tpu_custom_call" | custom-call | tf_op jit(solution)/shard_map/pair_tail/pallas_call | solution.py:1127
  499.9 3.1 copy.93
  503.0 1.9 copy.94
  (120 shorter events, 37.8 us)
Async XLA Ops:
  7.2 146.4 %all-gather.9.cloned.1.call-start = ((), (), s32[]{:S(2)}) async-start(), calls=%async_computation.2 | async-start | bytes 7028736 | tf_op jit(solution)/shard_map/all_gather | solution.py:935
  9.7 234.4 %all-gather.7.cloned.1.call-start = ((), (), s32[]{:S(2)}) async-start(), calls=%async_computation.1 | async-start | bytes 4177920 | tf_op jit(solution)/shard_map/all_gather | solution.py:855
  10.8 14.9 %collective-permute-start.3 = (bf16[272,768]{1,0:T(8,128)(2,1)S(1)}, bf16[272,768]{1,0:T(8,128)(2,1)S(1)}, u32[]{:S(2)}, u32[]{:S(2)}) collective-permute-start(bf16[272,768]{1,0:T(8,128)(2,1)S(1)} %pad_maximum_fusion.5), channel_id=1, source_target_pairs={{0,2},{1,3},{6,4},{7,5},{8,10},{9,11},{14,12},{15,13},{16,18},{17,... | collective-permute-start | bytes 1253384 | tf_op jit(solution)/shard_map/ppermute | solution.py:846
  12.1 13.6 %collective-permute-start.4 = (bf16[272,768]{1,0:T(8,128)(2,1)S(1)}, bf16[272,768]{1,0:T(8,128)(2,1)S(1)}, u32[]{:S(2)}, u32[]{:S(2)}) collective-permute-start(bf16[272,768]{1,0:T(8,128)(2,1)S(1)} %pad_maximum_fusion.5), channel_id=1, source_target_pairs={{2,6},{3,7},{4,0},{5,1},{10,14},{11,15},{12,8},{13,9},{18,22},{19,... | collective-permute-start | bytes 1253384 | tf_op jit(solution)/shard_map/ppermute | solution.py:846
  18.7 20.1 %collective-permute-start.5 = (bf16[272,768]{1,0:T(8,128)(2,1)S(1)}, bf16[272,768]{1,0:T(8,128)(2,1)S(1)}, u32[]{:S(2)}, u32[]{:S(2)}) collective-permute-start(bf16[272,768]{1,0:T(8,128)(2,1)S(1)} %pad_maximum_fusion.5), channel_id=1, source_target_pairs={{2,4},{3,5},{4,2},{5,3},{10,12},{11,13},{12,10},{13,11},{18,20},{1... | collective-permute-start | bytes 1253384 | tf_op jit(solution)/shard_map/ppermute | solution.py:846
  20.7 20.5 %copy-start.1 = (bf16[1,96,4096]{2,1,0:T(8,128)(2,1)S(1)}, bf16[1,96,4096]{2,1,0:T(8,128)(2,1)}, u32[]{:S(2)}) copy-start(bf16[1,96,4096]{2,1,0:T(8,128)(2,1)} %param.41) | copy-start | bytes 2359300
  20.7 20.5 %copy-start.2 = (bf16[1,16,4096]{2,1,0:T(8,128)(2,1)S(1)}, bf16[1,16,4096]{2,1,0:T(8,128)(2,1)}, u32[]{:S(2)}) copy-start(bf16[1,16,4096]{2,1,0:T(8,128)(2,1)} %param.44) | copy-start | bytes 393220
  41.1 204.1 %all-gather.5.cloned.1.call-start = ((), (), s32[]{:S(2)}) async-start(), calls=%async_computation | async-start | bytes 9175040 | tf_op jit(solution)/shard_map/all_gather | solution.py:855
  41.2 56.6 %collective-permute-start = (bf16[112,4096]{1,0:T(8,128)(2,1)S(1)}, bf16[112,4096]{1,0:T(8,128)(2,1)S(1)}, u32[]{:S(2)}, u32[]{:S(2)}) collective-permute-start(bf16[112,4096]{1,0:T(8,128)(2,1)S(1)} %pad_maximum_fusion.1), channel_id=1, source_target_pairs={{0,2},{1,3},{6,4},{7,5},{8,10},{9,11},{14,12},{15,13},{16,18},{17,... | collective-permute-start | bytes 2752520 | tf_op jit(solution)/shard_map/ppermute | solution.py:846
  42.5 55.4 %collective-permute-start.1 = (bf16[112,4096]{1,0:T(8,128)(2,1)S(1)}, bf16[112,4096]{1,0:T(8,128)(2,1)S(1)}, u32[]{:S(2)}, u32[]{:S(2)}) collective-permute-start(bf16[112,4096]{1,0:T(8,128)(2,1)S(1)} %pad_maximum_fusion.1), channel_id=1, source_target_pairs={{2,6},{3,7},{4,0},{5,1},{10,14},{11,15},{12,8},{13,9},{18,22},{19,... | collective-permute-start | bytes 2752520 | tf_op jit(solution)/shard_map/ppermute | solution.py:846
  45.2 63.6 %collective-permute-start.2 = (bf16[112,4096]{1,0:T(8,128)(2,1)S(1)}, bf16[112,4096]{1,0:T(8,128)(2,1)S(1)}, u32[]{:S(2)}, u32[]{:S(2)}) collective-permute-start(bf16[112,4096]{1,0:T(8,128)(2,1)S(1)} %pad_maximum_fusion.1), channel_id=1, source_target_pairs={{2,4},{3,5},{4,2},{5,3},{10,12},{11,13},{12,10},{13,11},{18,20},{1... | collective-permute-start | bytes 2752520 | tf_op jit(solution)/shard_map/ppermute | solution.py:846
  109.5 10.1 %copy-start.5 = (f32[1280,8]{0,1:T(8,128)S(1)}, f32[1280,8]{0,1:T(8,128)}, u32[]{:S(2)}) copy-start(f32[1280,8]{0,1:T(8,128)} %param.25) | copy-start | bytes 122884
  110.9 9.3 %copy-start.22 = (s32[1,5]{1,0:T(1,128)S(1)}, s32[1,5]{1,0:T(1,128)}, u32[]{:S(2)}) copy-start(s32[1,5]{1,0:T(1,128)} %param.26) | copy-start | bytes 64
  110.9 9.5 %copy-start.16 = (s32[1280,2]{0,1:T(2,128)S(1)}, s32[1280,2]{0,1:T(2,128)}, u32[]{:S(2)}) copy-start(s32[1280,2]{0,1:T(2,128)} %param.28) | copy-start | bytes 30724
  110.9 9.7 %copy-start.19 = (bf16[768]{0:T(1024)(128)(2,1)S(1)}, bf16[768]{0:T(1024)(128)(2,1)}, u32[]{:S(2)}) copy-start(bf16[768]{0:T(1024)(128)(2,1)} %param.30) | copy-start | bytes 4612
  110.9 10.4 %copy-start.21 = (s32[1,5]{1,0:T(1,128)S(1)}, s32[1,5]{1,0:T(1,128)}, u32[]{:S(2)}) copy-start(s32[1,5]{1,0:T(1,128)} %param.29) | copy-start | bytes 64
  110.9 11.6 %copy-start.12 = (bf16[768,8]{0,1:T(8,128)(2,1)S(1)}, bf16[768,8]{0,1:T(8,128)(2,1)}, u32[]{:S(2)}) copy-start(bf16[768,8]{0,1:T(8,128)(2,1)} %param.38) | copy-start | bytes 36868
  111.0 11.8 %copy-start.17 = (bf16[768,4]{0,1:T(4,128)(2,1)S(1)}, bf16[768,4]{0,1:T(4,128)(2,1)}, u32[]{:S(2)}) copy-start(bf16[768,4]{0,1:T(4,128)(2,1)} %param.39) | copy-start | bytes 18436
  111.0 12.1 %copy-start.20 = (bf16[768]{0:T(1024)(128)(2,1)S(1)}, bf16[768]{0:T(1024)(128)(2,1)}, u32[]{:S(2)}) copy-start(bf16[768]{0:T(1024)(128)(2,1)} %param.37) | copy-start | bytes 4612
  111.0 12.7 %copy-start.18 = (bf16[2,768]{1,0:T(2,128)(2,1)S(1)}, bf16[2,768]{1,0:T(2,128)(2,1)}, u32[]{:S(2)}) copy-start(bf16[2,768]{1,0:T(2,128)(2,1)} %param.40) | copy-start | bytes 9220
  111.0 13.3 %copy-start.11 = (s32[1,1280]{1,0:T(1,128)S(1)}, s32[1,1280]{1,0:T(1,128)}, u32[]{:S(2)}) copy-start(s32[1,1280]{1,0:T(1,128)} %place_row.1) | copy-start | bytes 15364
  111.0 26.0 %collective-permute-start.6 = (bf16[352,128]{1,0:T(8,128)(2,1)S(1)}, bf16[352,128]{1,0:T(8,128)(2,1)S(1)}, u32[]{:S(2)}, u32[]{:S(2)}) collective-permute-start(bf16[352,128]{1,0:T(8,128)(2,1)S(1)} %pad_maximum_fusion.8), channel_id=1, source_target_pairs={{0,2},{1,3},{6,4},{7,5},{8,10},{9,11},{14,12},{15,13},{16,18},{17,... | collective-permute-start | bytes 270344 | tf_op jit(solution)/shard_map/ppermute | solution.py:846
  112.3 24.7 %collective-permute-start.7 = (bf16[352,128]{1,0:T(8,128)(2,1)S(1)}, bf16[352,128]{1,0:T(8,128)(2,1)S(1)}, u32[]{:S(2)}, u32[]{:S(2)}) collective-permute-start(bf16[352,128]{1,0:T(8,128)(2,1)S(1)} %pad_maximum_fusion.8), channel_id=1, source_target_pairs={{2,6},{3,7},{4,0},{5,1},{10,14},{11,15},{12,8},{13,9},{18,22},{19,... | collective-permute-start | bytes 270344 | tf_op jit(solution)/shard_map/ppermute | solution.py:846
  113.9 23.1 %collective-permute-start.8 = (bf16[352,128]{1,0:T(8,128)(2,1)S(1)}, bf16[352,128]{1,0:T(8,128)(2,1)S(1)}, u32[]{:S(2)}, u32[]{:S(2)}) collective-permute-start(bf16[352,128]{1,0:T(8,128)(2,1)S(1)} %pad_maximum_fusion.8), channel_id=1, source_target_pairs={{2,4},{3,5},{4,2},{5,3},{10,12},{11,13},{12,10},{13,11},{18,20},{1... | collective-permute-start | bytes 270344 | tf_op jit(solution)/shard_map/ppermute | solution.py:846
  (11 other events, 39.3 us)
Sparse Core Ops, SparseCore 0:
  11.4 105.2 all-gather.8
  118.6 46.8 all-gather.6
  167.3 77.8 all-gather.4

commit v4 on v3

--- a/solution.py
+++ b/solution.py
@@ -98,25 +98,34 @@
     hid_s[...] = hid.astype(BF16)
     dy_s[...] = dot(perm, upstream[...]).astype(BF16)
     small_s[...] = dot(perm, small[...])
-    scale = lax.rsqrt(jnp.mean(hid * hid, axis=-1, keepdims=True) + EPSILON)
-    act = (hid * scale * gain[...]).astype(BF16)
+    act = normed(hid, gain)
     act_one[...] = act
-    low = (dot(act, a_in[...]) * mask[...].astype(F32)).astype(BF16)
+    low, q_val, k_val, value[...] = project(
+        act, mask[...], cosine[...], sine[...], w_qkv, a_in, b_out
+    )
     low_qkv[...] = low
-    cos, sin = cosine[...], sine[...]
-    for out, start, factor in ((query, 0, HEAD_DIM**-0.5), (key, MODEL_WIDTH, 1.0)):
-        vals = dot(act, w_qkv[:, start : start + MODEL_WIDTH]) + dot(
-            low, b_out[:, start : start + MODEL_WIDTH]
-        )
+    query[...], key[...] = q_val, k_val
+
+
+def normed(values, gain):
+    scale = lax.rsqrt(jnp.mean(values * values, axis=-1, keepdims=True) + EPSILON)
+    return (values * scale * gain[...]).astype(BF16)
+
+
+def project(act, mask, cos, sin, w_qkv, a_in, b_out):
+    low = (dot(act, a_in[...]) * mask.astype(F32)).astype(BF16)
+    turned = []
+    for start, factor in ((0, HEAD_DIM**-0.5), (MODEL_WIDTH, 1.0)):
+        cols = slice(start, start + MODEL_WIDTH)
+        vals = dot(act, w_qkv[:, cols]) + dot(low, b_out[:, cols])
+        pieces = []
         for c in range(MODEL_WIDTH // LANES):
             piece = vals[:, c * LANES : (c + 1) * LANES]
-            turned = (piece * cos + half_swap(piece) * sin).astype(BF16)
-            if factor != 1.0:
-                turned = turned * jnp.asarray(factor, BF16)
-            out[:, c * LANES : (c + 1) * LANES] = turned
-    value[...] = (
-        dot(act, w_qkv[:, 2 * MODEL_WIDTH :]) + dot(low, b_out[:, 2 * MODEL_WIDTH :])
-    ).astype(BF16)
+            piece = (piece * cos + half_swap(piece) * sin).astype(BF16)
+            pieces.append(piece if factor == 1.0 else piece * jnp.asarray(factor, BF16))
+        turned.append(jnp.concatenate(pieces, axis=1))
+    value = dot(act, w_qkv[:, 2 * MODEL_WIDTH :]) + dot(low, b_out[:, 2 * MODEL_WIDTH :])
+    return low, turned[0], turned[1], value.astype(BF16)
 
 
 def head_mask(shape, head):
@@ -125,6 +134,14 @@
 
 
 def attention_fwd_body(query, key, value, starts, attended, lse):
+    @pl.when(pl.program_id(0) == 0)
+    def _():
+        lse[...] = jnp.zeros_like(lse)
+
+    attention_fwd_pair(pl.program_id(0), query, key, value, starts, attended, lse)
+
+
+def attention_fwd_pair(pair, query, key, value, starts, attended, lse):
     tok = query.shape[0]
     size = ROW_BLOCK
     zero = jnp.zeros((), BF16)
@@ -137,7 +154,8 @@
         col = iota((size, hi), 1)
         allowed = (col <= lo + iota((size, hi), 0)) & (col >= begin)
         total = jnp.zeros((size, LANES), F32)
-        stats = jnp.zeros((size, LANES), F32)
+        stats = lse[lo:hi, :]
+        lane = iota((size, LANES), 1)
         for head in range(2):
             mine = head_mask((size, LANES), head)
             scores = dot_nt(jnp.where(mine, q_blk, zero), k_all)
@@ -147,7 +165,7 @@
             norm = jnp.sum(expo, axis=1, keepdims=True)
             v_head = jnp.where(head_mask((hi, LANES), head), v_all, zero)
             total = total + dot(expo.astype(BF16), v_head) * (1.0 / norm)
-            stats = jnp.where(mine, top + jnp.log(norm), stats)
+            stats = jnp.where(lane == 2 * pair + head, top + jnp.log(norm), stats)
         attended[lo:hi, :] = total.astype(BF16)
         lse[lo:hi, :] = stats
 
@@ -175,7 +193,7 @@
             mine = head_mask((size, LANES), head)
             q_head = jnp.where(mine, q_blk, zero)
             do_head = jnp.where(mine, do_blk, zero)
-            lse_head = lse[lo:hi, head * HEAD_DIM : head * HEAD_DIM + 1]
+            lse_head = lane_value(lse[lo:hi, :], 2 * pl.program_id(0) + head)
             delta = jnp.sum(jnp.where(mine, prod, 0.0), axis=1, keepdims=True)
             scores = dot_nt(q_head, k_all)
             prob = jnp.where(allowed, jnp.exp(jnp.minimum(scores - lse_head, 0.0)), 0.0)
@@ -196,6 +214,711 @@
             k_total * cosine[lo:hi, :] - half_swap(k_total) * sine[lo:hi, :]
         ).astype(BF16)
     d_value[...] = vacc[...].astype(BF16)
+
+
+def start_kernel(send_to, hear_from, count):
+    barrier = pltpu.get_barrier_semaphore()
+    for device, remote in hear_from:
+        if remote is None:
+            pl.semaphore_signal(barrier, inc=1, device_id=device, device_id_type=MESH_ID)
+        else:
+
+            @pl.when(remote)
+            def _(device=device):
+                pl.semaphore_signal(barrier, inc=1, device_id=device, device_id_type=MESH_ID)
+
+    pl.semaphore_wait(barrier, count)
+
+
+def pair_front_body(
+    kinds, a_rows, b_rows,
+    place_row, hidden, upstream, small, cosine, sine, mask, starts, gain_one, gain_two, router,
+    own_qkv, own_out, own_wide, own_mid, own_thin, *rest,
+):
+    outs, rest = rest[:20], rest[20:]
+    all_wide, all_mid, all_thin, rest = *rest[:3], rest[3:]
+    kept, rest = rest[:20], rest[20:]
+    (
+        hid_s, dy_s, small_s, act_one, low_qkv, query, key, value, w_qkv, a_qkv, b_qkv,
+        w_out, a_out, b_out, attn_low, lse, low_out, resid, act_two, gate,
+    ) = kept
+    g_qkv, g_out, a_send, a_recv, e_send, e_recv, out_sems, own_sems = rest
+    dp, z = lax.axis_index("dp"), lax.axis_index("expert")
+    core, x_bit, y_bit = dp % 2, dp // 2 % 2, dp // 4
+    across = dp + 1 - 2 * core
+    x_dev, y_dev = dp + 2 - 4 * x_bit, dp + 4 - 8 * y_bit
+    diag = x_dev + 4 - 8 * y_bit
+    far = (z + 2) % 4
+    home = z // 2
+    columns = (dp, x_dev, y_dev, diag)
+    tok = hidden.shape[0]
+    blocks = tok // ROW_BLOCK
+
+    def remote(source, target, send, recv, device):
+        return pltpu.make_async_remote_copy(
+            src_ref=source, dst_ref=target, send_sem=send, recv_sem=recv,
+            device_id=device, device_id_type=MESH_ID,
+        )
+
+    packs = ((own_qkv, g_qkv), (own_out, g_out))
+
+    def at(kind, back):
+        return columns[kind] * 4 + (z + 4 - back) % 4
+
+    def shard(p, kind, back, rows=None):
+        view = packs[p][1].at[at(kind, back)]
+        if rows is None:
+            return view
+        half = packs[p][1].shape[1] // 2
+        return view.at[pl.ds(rows * half, half)]
+
+    def along_z(p, j):
+        return remote(
+            packs[p][0], packs[p][1].at[at(0, 0)], a_send.at[p, j - 1], a_recv.at[p, j - 1],
+            (dp, (z + j) % 4),
+        )
+
+    def z_arrival(p, j):
+        return remote(
+            packs[p][0], shard(p, 0, j), a_send.at[p, j - 1], a_recv.at[p, j - 1], (dp, (z + j) % 4)
+        )
+
+    def to_x(p, back):
+        return remote(
+            shard(p, 0, back), shard(p, 0, back), a_send.at[p, 3 + back], a_recv.at[p, 3 + back],
+            (x_dev, z),
+        )
+
+    def to_y(p, back):
+        return remote(
+            shard(p, 0, back), shard(p, 0, back), a_send.at[p, 7 + back], a_recv.at[p, 7 + back],
+            (y_dev, z),
+        )
+
+    def relay_y(p, back):
+        return remote(
+            shard(p, 1, back, 0), shard(p, 1, back, 0), a_send.at[p, 11 + back],
+            a_recv.at[p, 11 + back], (y_dev, z),
+        )
+
+    def relay_x(p, back):
+        return remote(
+            shard(p, 2, back, 1), shard(p, 2, back, 1), a_send.at[p, 15 + back],
+            a_recv.at[p, 15 + back], (x_dev, z),
+        )
+
+    def to_core(p, kind, back):
+        sem = 19 + 4 * kind + back
+        return remote(
+            shard(p, kind, back), shard(p, kind, back), a_send.at[p, sem], a_recv.at[p, sem],
+            (across, z),
+        )
+
+    def keep_own(p):
+        return pltpu.make_async_copy(packs[p][0], shard(p, 0, 0), own_sems.at[p])
+
+    half_wide = own_wide.shape[1] // 2
+    parts = []
+    for own, everything, cols in (
+        (own_mid, all_mid, None), (own_thin, all_thin, None),
+        (own_wide, all_wide, (0, half_wide)), (own_wide, all_wide, (half_wide, half_wide)),
+    ):
+        if cols is None:
+            parts.append((own, lambda d, ref=everything: ref.at[d]))
+        else:
+            parts.append(
+                (own.at[:, pl.ds(*cols)], lambda d, ref=everything, c=cols: ref.at[d, :, pl.ds(*c)])
+            )
+    chunks = ((0, 1), (2,), (3,))
+
+    def first_far(a):
+        return remote(
+            parts[a][0], parts[a][1](dp), e_send.at[a, 0], e_recv.at[a, core],
+            (dp - core + home, far),
+        )
+
+    def first_across(a):
+        return remote(
+            parts[a][0], parts[a][1](dp), e_send.at[a, 1], e_recv.at[a, core], (across, z)
+        )
+
+    def first_keep(a):
+        return pltpu.make_async_copy(parts[a][0], parts[a][1](dp), e_recv.at[a, core])
+
+    def first_arrival(a, i):
+        view = parts[a][1](dp - core + i)
+        return remote(view, view, e_send.at[a, 0], e_recv.at[a, i], (dp, far))
+
+    def expert_hop(a, column, i, sem, device):
+        view = parts[a][1](column - core + i)
+        return remote(view, view, e_send.at[a, sem], e_recv.at[a, sem], (device, z))
+
+    def expert_x(a, i):
+        return expert_hop(a, dp, i, 2 + i, x_dev)
+
+    def expert_y(a, i):
+        return expert_hop(a, dp, i, 4 + i, y_dev)
+
+    def expert_relay_y(a):
+        return expert_hop(a, x_dev, 0, 6, y_dev)
+
+    def expert_relay_x(a):
+        return expert_hop(a, y_dev, 1, 7, x_dev)
+
+    def expert_first(c):
+        for a in chunks[c]:
+            first_far(a).start()
+
+            @pl.when(core == home)
+            def _(a=a):
+                first_keep(a).start()
+
+            @pl.when(core != home)
+            def _(a=a):
+                first_across(a).start()
+
+    def expert_spread(c):
+        for a in chunks[c]:
+
+            @pl.when(core == home)
+            def _(a=a):
+                first_keep(a).wait()
+                first_arrival(a, 1 - core).wait_recv()
+
+            @pl.when(core != home)
+            def _(a=a):
+                for i in range(2):
+                    first_arrival(a, i).wait_recv()
+
+            for i in range(2):
+                expert_x(a, i).start()
+                expert_y(a, i).start()
+
+    def expert_relay(c):
+        for a in chunks[c]:
+            for i in range(2):
+                expert_hop(a, x_dev, i, 2 + i, x_dev).wait_recv()
+            expert_relay_y(a).start()
+            for i in range(2):
+                expert_hop(a, y_dev, i, 4 + i, y_dev).wait_recv()
+            expert_relay_x(a).start()
+
+    def expert_finish(c):
+        for a in chunks[c]:
+            expert_hop(a, diag, 0, 6, y_dev).wait_recv()
+            expert_hop(a, diag, 1, 7, x_dev).wait_recv()
+            first_far(a).wait_send()
+
+            @pl.when(core != home)
+            def _(a=a):
+                first_across(a).wait_send()
+
+            for i in range(2):
+                expert_x(a, i).wait_send()
+                expert_y(a, i).wait_send()
+            expert_relay_y(a).wait_send()
+            expert_relay_x(a).wait_send()
+
+    peers = [(x_dev, z), (y_dev, z), (across, z), (across, far)]
+    peers += [(dp, (z + j) % 4) for j in (1, 2, 3)]
+    start_kernel(None, [(device, None) for device in peers], len(peers))
+    for p in range(2):
+        for j in (1, 2, 3):
+            along_z(p, jnp.where(z < 2, 4 - j, j)).start()
+        keep_own(p).start()
+    for p in range(2):
+        keep_own(p).wait()
+        to_x(p, 0).start()
+        to_y(p, 0).start()
+        to_core(p, 0, 0).start()
+
+    def block_rows(b):
+        return pl.ds(pl.multiple_of(b * ROW_BLOCK, ROW_BLOCK), ROW_BLOCK)
+
+    def arrange(b, carry):
+        rows = block_rows(b)
+        perm = hot_matrix(place_row[...] == b * ROW_BLOCK + iota((ROW_BLOCK, tok), 0))
+        hid = dot(perm, hidden[...])
+        hid_s[rows, :] = hid.astype(BF16)
+        act_one[rows, :] = normed(hid, gain_one)
+        dy_s[rows, :] = dot(perm, upstream[...]).astype(BF16)
+        small_s[rows, :] = dot(perm, small[...])
+        return carry
+
+    lax.fori_loop(0, blocks, arrange, 0)
+
+    for p in range(2):
+
+        def from_z(j, carry, p=p):
+            z_arrival(p, j).wait_recv()
+            to_x(p, j).start()
+            to_y(p, j).start()
+            to_core(p, 0, j).start()
+            return carry
+
+        lax.fori_loop(1, 4, from_z, 0)
+    for p in range(2):
+
+        def from_sides(back, carry, p=p):
+            remote(
+                shard(p, 1, back), shard(p, 1, back), a_send.at[p, 3 + back], a_recv.at[p, 3 + back],
+                (x_dev, z),
+            ).wait_recv()
+            relay_y(p, back).start()
+            to_core(p, 1, back).start()
+            remote(
+                shard(p, 2, back), shard(p, 2, back), a_send.at[p, 7 + back], a_recv.at[p, 7 + back],
+                (y_dev, z),
+            ).wait_recv()
+            relay_x(p, back).start()
+            to_core(p, 2, back).start()
+            return carry
+
+        lax.fori_loop(0, 4, from_sides, 0)
+    for c in range(len(chunks)):
+        expert_first(c)
+    for p in range(2):
+
+        def from_diag(back, carry, p=p):
+            remote(
+                shard(p, 3, back, 0), shard(p, 3, back, 0), a_send.at[p, 11 + back],
+                a_recv.at[p, 11 + back], (y_dev, z),
+            ).wait_recv()
+            remote(
+                shard(p, 3, back, 1), shard(p, 3, back, 1), a_send.at[p, 15 + back],
+                a_recv.at[p, 15 + back], (x_dev, z),
+            ).wait_recv()
+            to_core(p, 3, back).start()
+            return carry
+
+        lax.fori_loop(0, 4, from_diag, 0)
+    core_columns = (across, x_dev + across - dp, y_dev + across - dp, diag + across - dp)
+
+    def from_core(p):
+        def body(back, carry):
+            for kind in range(4):
+                view = packs[p][1].at[core_columns[kind] * 4 + (z + 4 - back) % 4]
+                sem = 19 + 4 * kind + back
+                remote(view, view, a_send.at[p, sem], a_recv.at[p, sem], (across, z)).wait_recv()
+            return carry
+
+        lax.fori_loop(0, 4, body, 0)
+
+    width = MODEL_WIDTH
+    total = g_qkv.shape[0]
+
+    def lay_rows(i, carry, gathered, targets):
+        pair = [gathered[2 * i + n, :a_rows, :].astype(F32) for n in range(2)]
+        both = jnp.concatenate(pair, axis=0).astype(BF16)
+        rows = pl.ds(pl.multiple_of(i * 2 * a_rows, 16), 2 * a_rows)
+        start = 0
+        for target in targets:
+            target[rows, :] = both[:, start : start + target.shape[1]]
+            start += target.shape[1]
+        return carry
+
+    def lay_ups(i, carry, gathered, target):
+        group = 16 // b_rows
+        pieces = [
+            gathered[group * i + n, a_rows : a_rows + b_rows, : target.shape[1]].astype(F32)
+            for n in range(group)
+        ]
+        rows = pl.ds(pl.multiple_of(i * 16, 16), 16)
+        target[rows, :] = jnp.concatenate(pieces, axis=0).astype(BF16)
+        return carry
+
+    def lay(gathered, targets, ups):
+        lax.fori_loop(
+            0, total // 2, functools.partial(lay_rows, gathered=gathered, targets=targets), 0
+        )
+        lax.fori_loop(
+            0, total * b_rows // 16, functools.partial(lay_ups, gathered=gathered, target=ups), 0
+        )
+
+    def flush(first, last):
+        return [
+            pltpu.make_async_copy(kept[i], outs[i], out_sems.at[i]) for i in range(first, last)
+        ]
+
+    from_core(0)
+    lay(g_qkv, (w_qkv, a_qkv), b_qkv)
+
+    def projection(b, carry):
+        rows = block_rows(b)
+        low_qkv[rows, :], query[rows, :], key[rows, :], value[rows, :] = project(
+            act_one[rows, :], mask[rows, :], cosine[rows, :], sine[rows, :], w_qkv, a_qkv, b_qkv
+        )
+
+        @pl.when(b == 1)
+        def _():
+            expert_spread(0)
+
+        return carry
+
+    lax.fori_loop(0, blocks, projection, 0)
+    from_core(1)
+    lay(g_out, (w_out, a_out), b_out)
+    for copy in flush(0, 14):
+        copy.start()
+    lse[...] = jnp.zeros_like(lse)
+
+    def attention(pair, carry):
+        cols = pl.ds(pl.multiple_of(pair * LANES, LANES), LANES)
+        attention_fwd_pair(
+            pair, query.at[:, cols], key.at[:, cols], value.at[:, cols], starts,
+            attn_low.at[:, cols], lse,
+        )
+
+        @pl.when(pair == 0)
+        def _():
+            expert_spread(1)
+
+        @pl.when(pair == 1)
+        def _():
+            expert_relay(0)
+
+        @pl.when(pair == 3)
+        def _():
+            expert_spread(2)
+
+        @pl.when(pair == 5)
+        def _():
+            expert_relay(1)
+
+        return carry
+
+    lax.fori_loop(0, HEAD_COUNT // 2, attention, 0)
+    for copy in flush(14, 16):
+        copy.start()
+
+    def after(b, carry):
+        rows = block_rows(b)
+        low_out[rows, :], resid[rows, :], act_two[rows, :], gate[rows, :] = post_attn(
+            kinds, attn_low[rows, :], hid_s[rows, :], mask[rows, :], small_s[rows, :],
+            w_out, a_out, b_out, router, gain_two,
+        )
+        return carry
+
+    lax.fori_loop(0, blocks, after, 0)
+    for copy in flush(16, 20):
+        copy.start()
+    expert_relay(2)
+    for c in range(len(chunks)):
+        expert_finish(c)
+
+    def attn_sent(n, carry):
+        for p in range(2):
+            to_x(p, n).wait_send()
+            to_y(p, n).wait_send()
+            relay_x(p, n).wait_send()
+            relay_y(p, n).wait_send()
+            for kind in range(4):
+                to_core(p, kind, n).wait_send()
+        return carry
+
+    lax.fori_loop(0, 4, attn_sent, 0)
+    for p in range(2):
+        for j in (1, 2, 3):
+            along_z(p, j).wait_send()
+    for copy in flush(0, 20):
+        copy.wait()
+
+
+def pair_attention_bwd_body(
+    query, key, value, dout, attended, lse, starts, cosine, sine, ga_gu, gb_gu, ga_dn, gb_dn,
+    d_query, d_key, d_value, own_ga_gu, own_gb_gu, own_ga_dn, own_gb_dn,
+    kacc, vacc, r_ga_gu, r_gb_gu, r_ga_dn, r_gb_dn, send_sems, recv_sems,
+):
+    dp, z = lax.axis_index("dp"), lax.axis_index("expert")
+    core, spot, half = dp % 2, dp // 2, z // 2
+    own = z % 2 + 2 * core
+    far = (z + 2) % 4
+    at_home = core == half
+    away = 1 - (core * half + (1 - core) * (1 - half))
+    slot = 2 * spot + away
+    groups = (
+        (ga_gu, r_ga_gu, own_ga_gu), (gb_gu, r_gb_gu, own_gb_gu),
+        (ga_dn, r_ga_dn, own_ga_dn), (gb_dn, r_gb_dn, own_gb_dn),
+    )
+    owners = 8
+
+    def piece(i, d):
+        source, target, _ = groups[i]
+        count = target.shape[1]
+        return source.at[pl.ds(pl.multiple_of(d * count, 16), count)]
+
+    def push(i, d):
+        return pltpu.make_async_remote_copy(
+            src_ref=piece(i, d), dst_ref=groups[i][1].at[slot], send_sem=send_sems.at[i, d],
+            recv_sem=recv_sems.at[i, slot], device_id=(d, own), device_id_type=MESH_ID,
+        )
+
+    def keep(i):
+        return pltpu.make_async_copy(
+            piece(i, dp), groups[i][1].at[2 * spot], recv_sems.at[i, 2 * spot]
+        )
+
+    def arrival(i, s):
+        return pltpu.make_async_remote_copy(
+            src_ref=piece(i, 0), dst_ref=groups[i][1].at[s], send_sem=send_sems.at[i, 0],
+            recv_sem=recv_sems.at[i, s], device_id=(0, own), device_id_type=MESH_ID,
+        )
+
+    @pl.when(pl.program_id(0) == 0)
+    def _():
+        senders = []
+        for m in range(owners // 2):
+            device = 2 * m + half
+            senders.append(((device, z), device != dp))
+            senders.append(((device, far), None))
+        start_kernel(None, senders, owners - 1 + away)
+
+        def send(d, carry):
+            mine = at_home & (d == dp)
+
+            @pl.when(mine)
+            def _():
+                for i in range(4):
+                    keep(i).start()
+
+            @pl.when(jnp.logical_not(mine))
+            def _():
+                for i in range(4):
+                    push(i, d).start()
+
+            return carry
+
+        lax.fori_loop(0, owners, send, 0)
+
+    attention_bwd_body(
+        query, key, value, dout, attended, lse, starts, cosine, sine, d_query, d_key, d_value,
+        kacc, vacc,
+    )
+
+    @pl.when(pl.program_id(0) == pl.num_programs(0) - 1)
+    def _():
+        def finish(s, carry):
+            mine = at_home & (s == 2 * spot)
+
+            @pl.when(mine)
+            def _():
+                for i in range(4):
+                    keep(i).wait()
+
+            @pl.when(jnp.logical_not(mine))
+            def _():
+                for i in range(4):
+                    arrival(i, s).wait_recv()
+
+            @pl.when(jnp.logical_not(at_home & (s == dp)))
+            def _():
+                for i in range(4):
+                    push(i, s).wait_send()
+
+            return carry
+
+        lax.fori_loop(0, owners, finish, 0)
+        for _, target, out in groups:
+            total = target[0].astype(F32)
+            for s in range(1, owners):
+                total = total + target[s].astype(F32)
+            out[...] = total
+
+
+def pair_tail_body(
+    place_col, d_query, d_key, d_value, low_qkv, act_one, mask, a_in, b_out, gain, ga_out, gb_out,
+    d_logits, hid_hbm, resid_hbm, w_hbm, out_hbm,
+    out, grad_hidden, grad_gate, own_ga_qkv, own_gb_qkv, own_ga_out, own_gb_out,
+    hid_s, d_resid, w_qkv, out_s, high, lower, d_low_all, ga_sum, gb_sum,
+    s_ga_qkv, s_gb_qkv, s_ga_out, s_gb_out, r_ga_qkv, r_gb_qkv, r_ga_out, r_gb_out,
+    thin_out, wide_out, thin_in, wide_in, load_sems, send_sems, recv_sems, far_send, far_recv,
+):
+    dp, z = lax.axis_index("dp"), lax.axis_index("expert")
+    others, planes = 7, 3
+    tok = place_col.shape[0]
+    blocks = tok // ROW_BLOCK
+    loads = [
+        pltpu.make_async_copy(source, target, load_sems.at[i])
+        for i, (source, target) in enumerate(
+            ((w_hbm, w_qkv), (hid_hbm, hid_s), (resid_hbm, d_resid), (out_hbm, out_s))
+        )
+    ]
+    for load in loads:
+        load.start()
+    start_kernel(
+        None,
+        [(((dp + i) % 8, z), None) for i in range(1, 8)] + [((dp, (z + j) % 4), None) for j in (1, 2, 3)],
+        others + planes,
+    )
+    ga_sum[...] = jnp.zeros_like(ga_sum)
+    gb_sum[...] = jnp.zeros_like(gb_sum)
+    parts = [slice(p * MODEL_WIDTH, (p + 1) * MODEL_WIDTH) for p in range(3)]
+    d_refs = (d_query, d_key, d_value)
+
+    def block_rows(b):
+        return pl.ds(pl.multiple_of(b * ROW_BLOCK, ROW_BLOCK), ROW_BLOCK)
+
+    def sums(b, carry):
+        rows = block_rows(b)
+        low = low_qkv[rows, :]
+        d_low = jnp.zeros((ROW_BLOCK, LANES), F32)
+        for cols, ref in zip(parts, d_refs):
+            grad = ref[rows, :]
+            d_low = d_low + dot_nt(grad, b_out[:, cols])
+            gb_sum[:, cols] += dot_tn(low, grad)
+        d_low = (d_low * mask[rows, :].astype(F32)).astype(BF16)
+        d_low_all[rows, :] = d_low
+        ga_sum[...] += dot_tn(act_one[rows, :], d_low)
+        return carry
+
+    lax.fori_loop(0, blocks, sums, 0)
+    s_ga_qkv[...] = ga_sum[...].astype(BF16)
+    s_gb_qkv[...] = gb_sum[...].astype(BF16)
+    s_ga_out[...] = ga_out[...].astype(BF16)
+    s_gb_out[...] = gb_out[...].astype(BF16)
+    groups = (
+        (s_ga_qkv, r_ga_qkv), (s_gb_qkv, r_gb_qkv), (s_ga_out, r_ga_out), (s_gb_out, r_gb_out),
+    )
+
+    def share(i, d):
+        count = groups[i][1].shape[1]
+        return groups[i][0].at[pl.ds(pl.multiple_of(d * count, 16), count)]
+
+    def near(i, n):
+        goal = (dp + n + 1) % 8
+        return pltpu.make_async_remote_copy(
+            src_ref=share(i, goal), dst_ref=groups[i][1].at[n], send_sem=send_sems.at[i, n],
+            recv_sem=recv_sems.at[i, n], device_id=(goal, z), device_id_type=MESH_ID,
+        )
+
+    def send_near(n, carry):
+        for i in range(4):
+            near(i, n).start()
+        return carry
+
+    lax.fori_loop(0, others, send_near, 0)
+
+    for load in loads[:3]:
+        load.wait()
+
+    def back(b, carry):
+        rows = block_rows(b)
+        d_act = dot_nt(d_low_all[rows, :], a_in[...])
+        for cols, ref in zip(parts, d_refs):
+            d_act = d_act + dot_nt(ref[rows, :], w_qkv[:, cols])
+        hid = hid_s[rows, :].astype(F32)
+        scale = lax.rsqrt(jnp.mean(hid * hid, axis=-1, keepdims=True) + EPSILON)
+        weighted = d_act * gain[...]
+        grad_hid = d_resid[rows, :] + (
+            scale * weighted
+            - hid * (scale * scale * scale) * jnp.mean(hid * weighted, axis=-1, keepdims=True)
+        )
+        top = grad_hid.astype(BF16)
+        high[rows, :] = top
+        lower[rows, :] = (grad_hid - top.astype(F32)).astype(BF16)
+        return carry
+
+    lax.fori_loop(0, blocks, back, 0)
+
+    def near_done(n, carry):
+        for i in range(4):
+            near(i, n).wait_recv()
+        return carry
+
+    lax.fori_loop(0, others, near_done, 0)
+    totals = []
+    for i in range(4):
+        total = share(i, dp)[...].astype(F32)
+        for n in range(others):
+            total = total + groups[i][1][n].astype(F32)
+        totals.append(total)
+    a_qkv, b_qkv, a_o, b_o = totals
+    a_count, b_count = a_qkv.shape[0] // 4, b_qkv.shape[0] // 4
+    for p in range(4):
+        a_rows, b_rows = slice(p * a_count, (p + 1) * a_count), slice(p * b_count, (p + 1) * b_count)
+        thin_out[p, :a_count, :LANES] = a_qkv[a_rows].astype(BF16)
+        thin_out[p, :a_count, LANES:] = a_o[a_rows].astype(BF16)
+        thin_out[p, a_count:, :] = jnp.zeros((thin_out.shape[1] - a_count, 2 * LANES), BF16)
+        wide_out[p] = jnp.concatenate(
+            [b_qkv[b_rows, cols] for cols in parts] + [b_o[b_rows]], axis=0
+        ).astype(BF16)
+
+    def far(i, j):
+        goal = (z + j + 1) % 4
+        source, target = ((thin_out, thin_in), (wide_out, wide_in))[i]
+        return pltpu.make_async_remote_copy(
+            src_ref=source.at[goal], dst_ref=target.at[j], send_sem=far_send.at[i, j],
+            recv_sem=far_recv.at[i, j], device_id=(dp, goal), device_id_type=MESH_ID,
+        )
+
+    for j in range(planes):
+        for i in range(2):
+            far(i, j).start()
+    loads[3].wait()
+
+    def to_rows(b, carry):
+        rows = block_rows(b)
+        perm = hot_matrix(place_col[rows, :] == iota((ROW_BLOCK, tok), 1))
+        out[rows, :] = dot(perm, out_s[...]).astype(BF16)
+        grad_hidden[rows, :] = dot(perm, high[...]) + dot(perm, lower[...])
+        top, mid, last = split_three(d_logits[...])
+        grad_gate[rows, :] = dot(perm, top) + (dot(perm, mid) + dot(perm, last))
+        return carry
+
+    lax.fori_loop(0, blocks, to_rows, 0)
+    for j in range(planes):
+        for i in range(2):
+            far(i, j).wait_recv()
+    thin = thin_out[z].astype(F32)
+    wide = wide_out[z].astype(F32)
+    for j in range(planes):
+        thin = thin + thin_in[j].astype(F32)
+        wide = wide + wide_in[j].astype(F32)
+    own_ga_qkv[...] = thin[:a_count, :LANES]
+    own_ga_out[...] = thin[:a_count, LANES:]
+    for p, cols in enumerate(parts):
+        own_gb_qkv[:, cols] = wide[p * b_count : (p + 1) * b_count]
+    own_gb_out[...] = wide[3 * b_count : 4 * b_count]
+
+    def sent(n, carry):
+        for i in range(4):
+            near(i, n).wait_send()
+        return carry
+
+    lax.fori_loop(0, others, sent, 0)
+    for j in range(planes):
+        for i in range(2):
+            far(i, j).wait_send()
+
+
+def split_three(values):
+    top = values.astype(BF16)
+    rest = values - top.astype(F32)
+    mid = rest.astype(BF16)
+    return top, mid, (rest - mid.astype(F32)).astype(BF16)
+
+
+def post_attn_body(
+    kinds, attn_low, hid_s, mask, small_s, w_out, a_out, b_out, router, gain,
+    low_out, resid, act_two, gate,
+):
+    low_out[...], resid[...], act_two[...], gate[...] = post_attn(
+        kinds, attn_low[...], hid_s[...], mask[...], small_s[...], w_out, a_out, b_out, router, gain
+    )
+
+
+def post_attn(kinds, attn, hid, mask, sm, w_out, a_out, b_out, router, gain):
+    low = (dot(attn, a_out[...]) * mask.astype(F32)).astype(BF16)
+    res = hid.astype(F32) + (dot(attn, w_out[...]) + dot(low, b_out[...]))
+    act = normed(res, gain)
+    carry = sm + (pltpu.roll(sm, LANES - 16, 1) + pltpu.roll(sm, LANES - 32, 1))
+    logits = dot(act, router[...])
+    lane = iota(logits.shape, 1)
+    routed = jnp.where(lane < kinds, logits + carry, -1e30)
+    top = jnp.max(routed, axis=1, keepdims=True)
+    expo = jnp.exp(routed - top)
+    prob = expo / jnp.sum(expo, axis=1, keepdims=True)
+    return low, res, act, jnp.where(lane < kinds, prob, logits)
 
 
 def start_kernel(send_to, hear_from, count):
@@ -828,34 +1551,11 @@
     paired = True
 
     def __init__(self, dp, ex):
-        self.axes = ("dp", "expert")
-        self.dp, self.ex = dp, ex
-        self.h = lax.axis_index("dp") & 1
-        self.z = lax.axis_index("expert")
-        self.own = (self.z & 1) + 2 * self.h
-        self.local = (self.z >> 1) == self.h
-        self.groups = [[2 * m + h for m in range(dp // 2)] for h in range(2)]
-
-    def send(self, values, target):
-        pairs = []
-        for d in range(self.dp):
-            for z in range(self.ex):
-                goal = target(d, z)
-                if goal is not None:
-                    pairs.append((d * self.ex + z, goal[0] * self.ex + goal[1]))
-        return lax.ppermute(values, self.axes, pairs)
-
-    def gather(self, shard):
-        near = self.send(shard, lambda d, z: (d, z ^ 2) if (z >> 1) == (d & 1) else None)
-        cross = self.send(shard, lambda d, z: (d ^ 1, z ^ 2) if (z >> 1) != (d & 1) else None)
-        over = self.send(shard, lambda d, z: (d ^ 1, z) if (z >> 1) != (d & 1) else None)
-        mine = jnp.where(self.local, shard, near)
-        other = jnp.where(self.local, over, cross)
-        both = jnp.stack([jnp.where(self.h == 0, mine, other), jnp.where(self.h == 0, other, mine)])
-        return lax.all_gather(both, "dp", axis=0, tiled=True, axis_index_groups=self.groups)
+        self.ex = ex
 
     def expert_ids(self):
-        return self.own ^ jnp.arange(self.ex, dtype=jnp.int32)
+        own = lax.axis_index("expert") % 2 + 2 * (lax.axis_index("dp") % 2)
+        return own ^ jnp.arange(self.ex, dtype=jnp.int32)
 
 
 class AxisPlan:
@@ -920,32 +1620,20 @@
     plan = (PairPlan if (dp_size, expert_count) == (8, 4) else AxisPlan)(dp_size, expert_count)
 
     a_rows, b_rows = query_key_weight.shape[0], adapter_out_query.shape[0]
-    own_a = jnp.concatenate(
-        [query_key_weight, output_weight, adapter_in_query, adapter_in_output], axis=1
-    )
-    own_b = jnp.concatenate([adapter_out_query, adapter_out_output], axis=1)
-    pad_rows = -(a_rows + b_rows) % 8
-    own_attn = jnp.concatenate(
-        [
-            own_a,
-            jnp.pad(own_b, ((0, pad_rows), (0, own_a.shape[1] - own_b.shape[1]))),
-        ],
-        axis=0,
-    )
-    attn_all = lax.all_gather(own_attn, ("dp", "expert"), axis=0)
-    in_rows = attn_all[:, :a_rows]
-    out_rows = attn_all[:, a_rows : a_rows + b_rows]
-    w_qkv = in_rows[:, :, : 3 * width].reshape(width, 3 * width)
-    w_out = in_rows[:, :, 3 * width : 4 * width].reshape(width, width)
-    a_qkv = in_rows[:, :, 4 * width : 4 * width + LANES].reshape(width, LANES)
-    a_out = in_rows[:, :, 4 * width + LANES :].reshape(width, LANES)
-    b_qkv = out_rows[:, :, : 3 * width].reshape(LANES, 3 * width)
-    b_out = out_rows[:, :, 3 * width : 4 * width].reshape(LANES, width)
-
-    gu_rows, up_rows, dn_rows = gate_upward_weight.shape[1], adapter_out_gate.shape[1], down_weight.shape[1]
-    wide = plan.gather(jnp.concatenate([gate_upward_weight[0], adapter_out_gate[0]], axis=0))
-    mid = plan.gather(jnp.concatenate([down_weight[0], adapter_out_down[0]], axis=0))
-    thin = plan.gather(jnp.concatenate([adapter_in_gate[0], adapter_in_down[0]], axis=0))
+    gu_rows, up_rows, dn_rows = (
+        gate_upward_weight.shape[1], adapter_out_gate.shape[1], down_weight.shape[1],
+    )
+    pad_rows = -(a_rows + b_rows) % 16
+
+    def pack(weight, adapter_in, adapter_out):
+        lower = jnp.pad(adapter_out, ((0, pad_rows), (0, LANES)))
+        return jnp.concatenate([jnp.concatenate([weight, adapter_in], axis=1), lower], axis=0)
+
+    own_qkv = pack(query_key_weight, adapter_in_query, adapter_out_query)
+    own_out = pack(output_weight, adapter_in_output, adapter_out_output)
+    own_wide = jnp.concatenate([gate_upward_weight[0], adapter_out_gate[0]], axis=0)
+    own_mid = jnp.concatenate([down_weight[0], adapter_out_down[0]], axis=0)
+    own_thin = jnp.concatenate([adapter_in_gate[0], adapter_in_down[0]], axis=0)
 
     place = token_stream_place[0]
     ends = jnp.cumsum(sequence_length[0])
@@ -980,41 +1668,87 @@
     const_value = constant_value.astype(F32)
 
     full = whole
-    hid_s, dy_s, small_s, act_one, low_qkv, query, key, value = call(
-        proj_in_body,
-        (blocks,),
-        [full((1, tok)), full((tok, width)), full((tok, width)), full((tok, LANES)),
-         row_spec(LANES), row_spec(LANES), row_spec(LANES), full((1, width)),
-         full((width, 3 * width)), full((width, LANES)), full((LANES, 3 * width))],
-        [row_spec(width), row_spec(width), row_spec(LANES), row_spec(width), row_spec(LANES),
-         row_spec(width), row_spec(width), row_spec(width)],
-        [sds((tok, width), BF16), sds((tok, width), BF16), sds((tok, LANES), F32),
-         sds((tok, width), BF16), sds((tok, LANES), BF16), sds((tok, width), BF16),
-         sds((tok, width), BF16), sds((tok, width), BF16)],
-        name="proj_in",
-    )(place[None, :], hidden_input, output_gradient, small, cosine, sine, mask, gain_one,
-      w_qkv, a_qkv, b_qkv)
-
+    hbm = pl.BlockSpec(memory_space=pl.ANY)
+    vmem = pl.BlockSpec(memory_space=pltpu.VMEM)
     pairs = HEAD_COUNT // 2
-    attn_low, lse = call(
-        attention_fwd_body,
-        (pairs,),
-        [col_spec(tok)] * 3 + [full((tok, 1))],
-        [col_spec(tok), col_spec(tok)],
-        [sds((tok, width), BF16), sds((tok, width), F32)],
-        name="attention_fwd",
-    )(query, key, value, starts)
-
-    low_out, resid, act_two, gate = call(
-        functools.partial(post_attn_body, kinds),
-        (blocks,),
-        [row_spec(width), row_spec(width), row_spec(LANES), row_spec(LANES), full((width, width)),
-         full((width, LANES)), full((LANES, width)), full((width, LANES)), full((1, width))],
-        [row_spec(LANES), row_spec(width), row_spec(width), row_spec(LANES)],
-        [sds((tok, LANES), BF16), sds((tok, width), F32), sds((tok, width), BF16),
-         sds((tok, LANES), F32)],
-        name="post_attn",
-    )(attn_low, hid_s, mask, small_s, w_out, a_out, b_out, router, gain_two)
+    if plan.paired:
+        shapes = [
+            sds((tok, width), BF16), sds((tok, width), BF16), sds((tok, LANES), F32),
+            sds((tok, width), BF16), sds((tok, LANES), BF16), sds((tok, width), BF16),
+            sds((tok, width), BF16), sds((tok, width), BF16), sds((width, 3 * width), BF16),
+            sds((width, LANES), BF16), sds((LANES, 3 * width), BF16), sds((width, width), BF16),
+            sds((width, LANES), BF16), sds((LANES, width), BF16), sds((tok, width), BF16),
+            sds((tok, LANES), F32), sds((tok, LANES), BF16), sds((tok, width), F32),
+            sds((tok, width), BF16), sds((tok, LANES), F32),
+        ]
+        (
+            hid_s, dy_s, small_s, act_one, low_qkv, query, key, value, w_qkv, a_qkv, b_qkv,
+            w_out, a_out, b_out, attn_low, lse, low_out, resid, act_two, gate, wide, mid, thin,
+        ) = pl.pallas_call(
+            functools.partial(pair_front_body, kinds, a_rows, b_rows),
+            in_specs=[vmem] * 11 + [hbm] * 5,
+            out_specs=[hbm] * 23,
+            out_shape=shapes
+            + [sds((dp_size,) + w.shape, BF16) for w in (own_wide, own_mid, own_thin)],
+            scratch_shapes=[pltpu.VMEM(s.shape, s.dtype) for s in shapes]
+            + [
+                pltpu.VMEM((devices,) + own_qkv.shape, BF16),
+                pltpu.VMEM((devices,) + own_out.shape, BF16),
+                pltpu.SemaphoreType.DMA((2, 35)), pltpu.SemaphoreType.DMA((2, 35)),
+                pltpu.SemaphoreType.DMA((4, 8)), pltpu.SemaphoreType.DMA((4, 8)),
+                pltpu.SemaphoreType.DMA((20,)), pltpu.SemaphoreType.DMA((2,)),
+            ],
+            compiler_params=pltpu.CompilerParams(
+                vmem_limit_bytes=VMEM_BYTES, collective_id=4, has_side_effects=True
+            ),
+            name="pair_front",
+        )(place[None, :], hidden_input, output_gradient, small, cosine, sine, mask, starts,
+          gain_one, gain_two, router, own_qkv, own_out, own_wide, own_mid, own_thin)
+    else:
+        all_qkv = lax.all_gather(own_qkv, ("dp", "expert"), axis=0)
+        all_out = lax.all_gather(own_out, ("dp", "expert"), axis=0)
+        upper = slice(a_rows, a_rows + b_rows)
+        w_qkv = all_qkv[:, :a_rows, : 3 * width].reshape(width, 3 * width)
+        a_qkv = all_qkv[:, :a_rows, 3 * width :].reshape(width, LANES)
+        b_qkv = all_qkv[:, upper, : 3 * width].reshape(LANES, 3 * width)
+        w_out = all_out[:, :a_rows, :width].reshape(width, width)
+        a_out = all_out[:, :a_rows, width:].reshape(width, LANES)
+        b_out = all_out[:, upper, :width].reshape(LANES, width)
+        wide, mid, thin = (plan.gather(w) for w in (own_wide, own_mid, own_thin))
+        hid_s, dy_s, small_s, act_one, low_qkv, query, key, value = call(
+            proj_in_body,
+            (blocks,),
+            [full((1, tok)), full((tok, width)), full((tok, width)), full((tok, LANES)),
+             row_spec(LANES), row_spec(LANES), row_spec(LANES), full((1, width)),
+             full((width, 3 * width)), full((width, LANES)), full((LANES, 3 * width))],
+            [row_spec(width), row_spec(width), row_spec(LANES), row_spec(width), row_spec(LANES),
+             row_spec(width), row_spec(width), row_spec(width)],
+            [sds((tok, width), BF16), sds((tok, width), BF16), sds((tok, LANES), F32),
+             sds((tok, width), BF16), sds((tok, LANES), BF16), sds((tok, width), BF16),
+             sds((tok, width), BF16), sds((tok, width), BF16)],
+            name="proj_in",
+        )(place[None, :], hidden_input, output_gradient, small, cosine, sine, mask, gain_one,
+          w_qkv, a_qkv, b_qkv)
+
+        attn_low, lse = call(
+            attention_fwd_body,
+            (pairs,),
+            [col_spec(tok)] * 3 + [full((tok, 1))],
+            [col_spec(tok), full((tok, LANES))],
+            [sds((tok, width), BF16), sds((tok, LANES), F32)],
+            name="attention_fwd",
+        )(query, key, value, starts)
+
+        low_out, resid, act_two, gate = call(
+            functools.partial(post_attn_body, kinds),
+            (blocks,),
+            [row_spec(width), row_spec(width), row_spec(LANES), row_spec(LANES), full((width, width)),
+             full((width, LANES)), full((LANES, width)), full((width, LANES)), full((1, width))],
+            [row_spec(LANES), row_spec(width), row_spec(width), row_spec(LANES)],
+            [sds((tok, LANES), BF16), sds((tok, width), F32), sds((tok, width), BF16),
+             sds((tok, LANES), F32)],
+            name="post_attn",
+        )(attn_low, hid_s, mask, small_s, w_out, a_out, b_out, router, gain_two)
 
     eids = plan.expert_ids()
     smem = pl.BlockSpec(memory_space=pltpu.SMEM)
@@ -1038,8 +1772,6 @@
         pltpu.VMEM((cap, width), F32), pltpu.VMEM((cap, width), F32),
         pltpu.VMEM((cap, LANES), F32), pltpu.VMEM((cap, LANES), F32),
     ]
-    hbm = pl.BlockSpec(memory_space=pl.ANY)
-    vmem = pl.BlockSpec(memory_space=pltpu.VMEM)
     if plan.paired:
         returned, ga_gu, gb_gu, ga_dn, gb_dn = pl.pallas_call(
             pair_ffn_body,
@@ -1109,8 +1841,8 @@
         d_query, d_key, d_value, *expert_owned = pl.pallas_call(
             pair_attention_bwd_body,
             grid=(pairs,),
-            in_specs=[col_spec(tok)] * 6
-            + [full((tok, 1)), full((tok, LANES)), full((tok, LANES))]
+            in_specs=[col_spec(tok)] * 5
+            + [full((tok, LANES)), full((tok, 1)), full((tok, LANES)), full((tok, LANES))]
             + [hbm] * 4,
             out_specs=[col_spec(tok)] * 3 + [full(s.shape) for s in own_shapes],
             out_shape=[sds((tok, width), BF16)] * 3 + own_shapes,
@@ -1170,7 +1902,8 @@
     d_query, d_key, d_value = call(
         attention_bwd_body,
         (pairs,),
-        [col_spec(tok)] * 6 + [full((tok, 1)), full((tok, LANES)), full((tok, LANES))],
+        [col_spec(tok)] * 5
+        + [full((tok, LANES)), full((tok, 1)), full((tok, LANES)), full((tok, LANES))],
         [col_spec(tok)] * 3,
         [sds((tok, width), BF16)] * 3,
         scratch=[pltpu.VMEM((tok, LANES), F32), pltpu.VMEM((tok, LANES), F32)],

time: 524 us -> 455 us (0.87)
  Pallas kernels: 331 us -> 414 us
  waiting for transfers between devices: 78.3 us -> 0 us
  starting transfers between devices: 27.1 us -> 0 us
  blocking collectives: 16.4 us -> 0 us
  between operations: 14.7 us -> 1.5 us
  local copies, waits for them, and re-layouts: 34 us -> 21.7 us
    pallas_call x3 -> x1, Pallas kernels: 64.7 us -> 149 us  [shards(): pl.pallas_call(functools.partial(pair_front_body, kinds, a_rows, b_rows),...]
    ppermute x9 -> x0, waiting for transfers between devices: 77 us -> none  [send(): return lax.ppermute(values, self.axes, pairs)]
    ppermute x9 -> x0, starting transfers between devices: 27 us -> none  [send(): return lax.ppermute(values, self.axes, pairs)]
    all_gather x1 -> x0, blocking collectives: 16.4 us -> none  [gather(): lax.all_gather(both, 'dp', axis=0, tiled=True, axis_index_groups=self.gro...]
    slice x5 -> x0, local copies, waits for them, and re-layouts: 10.8 us -> none  [the longest x1 4.06 us: shards(): w_qkv = in_rows[:, :, :3 * width].reshape(width, 3 * width)]
    unnamed x60 -> x72, local copies, waits for them, and re-layouts: 12.6 us -> 12.7 us
  transfers between devices with their start and end apart: 12 -> 0, of which waited for: 5 -> 0; matrix products, arithmetic and copies ran while one was open for 7% -> 0% of each run, Pallas kernels for 15% -> 0%
where the time goes in v4:
time: 455 us; the launch traced here: 451 us
  Pallas kernels  414 us (91%)
  local copies, waits for them, and re-layouts  21.7 us (5%)
  other arithmetic  13.6 us (3%)
    pallas_call x1, Pallas kernels, shards(): pl.pallas_call(functools.partial(pair_front_body, kinds, a_rows, b_rows),...  149 us
    pallas_call x1, Pallas kernels, shards(): pl.pallas_call(pair_ffn_body, in_specs=[hbm] * 4, out_specs=[hbm] + [vmem...  118 us
    pallas_call x1, Pallas kernels, shards(): pl.pallas_call(pair_attention_bwd_body, grid=(pairs,), in_specs=[col_spec...  53.3 us
    pallas_call x1, Pallas kernels, shards(): pl.pallas_call(pair_tail_body, in_specs=[vmem] * 13 + [hbm] * 4, out_spec...  48.3 us
    pallas_call x1, Pallas kernels, shards(): call(functools.partial(combine_body, expert_count, kinds), (blocks,), [sm...  32.3 us
    pallas_call x1, Pallas kernels, shards(): call(functools.partial(dispatch_body, expert_count), (expert_count,), [sm...  13.4 us
    unnamed x72, local copies, waits for them, and re-layouts  12.7 us

profile of v4, /device:TPU:1, one launch (start us, length us, event | category | flops | bytes accessed | tf_op | source)
XLA Modules:
  0.0 450.9 jit_solution(7680253701325584548)
XLA Ops:
  1.2 0.8 reduce-window.4
  2.1 0.7 fusion.5
  2.8 0.8 select_reduce_fusion
  3.5 2.4 fusion.1
  5.9 2.2 pad_maximum_fusion.1
  8.1 1.0 compare_convert_fusion.mask
  10.2 4.8 %concatenate.33.small = bf16[1280,128]{1,0:T(8,128)(2,1)} concatenate(bf16[1280,8]{1,0:T(8,128)(2,1)S(1)} %copy.64, bf16[1280,8]{1,0:T(8,128)(2,1)S(1)} %broadcast_in_dim.66, bf16[1280,8]{1,0:T(8,128)(2,1)S(1)} %get-tuple-element.158, bf16[1280,8]{1,0:T(8,128)(2,1)S(1)} %broadcast_in_dim.66, bf16[1280,8]{1,0:T(8,128)(2,1)S(1)} %get-tuple-element.157, ...), dimensions={1} | concatenate | bytes 655360 | tf_op jit(solution)/shard_map/concatenate | solution.py:1656
  15.0 1.1 reduce_sum.33.starts
  16.7 0.8 maximum_maximum_fusion.router
  18.7 1.0 pad_maximum_fusion.own_wide
  19.7 0.8 pad_maximum_fusion.3.own_mid
  20.5 0.7 fusion.2.own_qkv
  22.4 148.5 %pair_front.1 = (bf16[1280,768]{1,0:T(8,128)(2,1)}, bf16[1280,768]{1,0:T(8,128)(2,1)}, f32[1280,128]{1,0:T(8,128)}, bf16[1280,768]{1,0:T(8,128)(2,1)}, bf16[1280...) custom-call(s32[1,1280]{1,0:T(1,128)} %place_row.1, ...), custom_call_target="tpu_custom_call" | custom-call | tf_op jit(solution)/shard_map/pair_front/pallas_call | solution.py:1687
  171.0 13.4 %dispatch.1 = (f32[1280,128]{1,0:T(8,128)}, bf16[4,416,1664]{2,1,0:T(8,128)(2,1)}) custom-call(s32[4]{0:T(128)} %iota_xor_fusion.eids, f32[1280,128]{1,0:T(8,128)} %get-tuple-element.68.small_s, f32[1280,128]{1,0:T(8,128)} %get-tuple-element.67.gate, bf16[1280,768]{1,0:T(8,128)(2,1)} %get-tuple-element.65.act_two, bf16[1280,768]{1,0:T(8,128)(2,1)} %get-tuple-element.66.dy_s, ...), custom_call_target="tpu_custom_call" | custom-call | tf_op jit(solution)/shard_map/dispatch/pallas_call | solution.py:1756
  184.4 118.3 %pair_ffn.1 = (bf16[4,416,1536]{2,1,0:T(8,128)(2,1)}, bf16[768,128]{1,0:T(8,128)(2,1)}, bf16[128,4096]{1,0:T(8,128)(2,1)}, bf16[2048,128]{1,0:T(8,128)(2,1)}, bf16[128,768]{1,0:T(8,128)(2,1)}) custom-call(bf16[4,416,1664]{2,1,0:T(8,128)(2,1)} %get-tuple-element.72.sent, bf16[8,112,4096]{2,1,0:T(8,128)(2,1)} %get-tuple-element.73.wide, ...), custom_call_target="tpu_custom_call" | custom-call | tf_op jit(solution)/shard_map/pair_ffn/pallas_call | solution.py:1776
  303.3 32.3 %combine.1 = (bf16[1280,768]{1,0:T(8,128)(2,1)}, f32[1280,768]{1,0:T(8,128)}, bf16[1280,768]{1,0:T(8,128)(2,1)}, f32[1280,128]{1,0:T(8,128)}, f32[768,128]{1,0:T(8,128)}, /*index=5*/f32[128,768]{1,0:T(8,128)}) custom-call(s32[4]{0:T(128)} %iota_xor_fusion.eids, f32[1280,768]{1,0:T(8,128)} %get-tuple-element.64.resid, ...), custom_call_target="tpu_custom_call" | custom-call | tf_op jit(solution)/shard_map/combine/pallas_call | solution.py:1820
  335.6 53.3 %pair_attention_bwd.1 = (bf16[1280,768]{1,0:T(8,128)(2,1)}, bf16[1280,768]{1,0:T(8,128)(2,1)}, bf16[1280,768]{1,0:T(8,128)(2,1)}, f32[96,128]{1,0:T(8,128)}, f32...) custom-call(bf16[1280,768]{1,0:T(8,128)(2,1)} %get-tuple-element.61.query, ...), custom_call_target="tpu_custom_call" | custom-call | tf_op jit(solution)/shard_map/pair_attention_bwd/pallas_call | solution.py:1841
  388.9 1.1 copy.71.place_col
  390.0 48.3 %pair_tail.1 = (bf16[1280,768]{1,0:T(8,128)(2,1)}, f32[1280,768]{1,0:T(8,128)}, f32[1280,128]{1,0:T(8,128)}, f32[24,128]{1,0:T(8,128)}, f32[4,2304]{1,0:T(4,128)}, /*index=5*/f32[24,128]{1,0:T(8,128)}, f32[4,768]{1,0:T(4,128)}) custom-call(s32[1280,1]{1,0:T(8,128)} %copy.71.place_col, bf16[1280,768]{1,0:T(8,128)(2,1)} %get-tuple-element.86.d_query, ...), custom_call_target="tpu_custom_call" | custom-call | tf_op jit(solution)/shard_map/pair_tail/pallas_call | solution.py:1859
  438.3 1.9 copy.72
  440.2 3.1 copy.83
  443.4 1.9 copy.84
  448.4 0.7 copy.90
  449.1 0.7 copy.91
  (89 shorter events, 9.0 us)
Async XLA Ops:
  10.1 6.0 %copy-start.17 = (bf16[768,8]{0,1:T(8,128)(2,1)S(1)}, bf16[768,8]{0,1:T(8,128)(2,1)}, u32[]{:S(2)}) copy-start(bf16[768,8]{0,1:T(8,128)(2,1)} %param.38) | copy-start | bytes 36868
  10.2 6.1 %copy-start.22 = (bf16[768,4]{0,1:T(4,128)(2,1)S(1)}, bf16[768,4]{0,1:T(4,128)(2,1)}, u32[]{:S(2)}) copy-start(bf16[768,4]{0,1:T(4,128)(2,1)} %param.39) | copy-start | bytes 18436
  10.2 7.3 %copy-start.27 = (bf16[768]{0:T(1024)(128)(2,1)S(1)}, bf16[768]{0:T(1024)(128)(2,1)}, u32[]{:S(2)}) copy-start(bf16[768]{0:T(1024)(128)(2,1)} %param.30) | copy-start | bytes 4612
  10.2 7.9 %copy-start.28 = (bf16[768]{0:T(1024)(128)(2,1)S(1)}, bf16[768]{0:T(1024)(128)(2,1)}, u32[]{:S(2)}) copy-start(bf16[768]{0:T(1024)(128)(2,1)} %param.37) | copy-start | bytes 4612
  10.2 8.5 %copy-start.1 = (bf16[1,96,4096]{2,1,0:T(8,128)(2,1)S(1)}, bf16[1,96,4096]{2,1,0:T(8,128)(2,1)}, u32[]{:S(2)}) copy-start(bf16[1,96,4096]{2,1,0:T(8,128)(2,1)} %param.41) | copy-start | bytes 2359300
  10.2 8.5 %copy-start.5 = (bf16[1,16,4096]{2,1,0:T(8,128)(2,1)S(1)}, bf16[1,16,4096]{2,1,0:T(8,128)(2,1)}, u32[]{:S(2)}) copy-start(bf16[1,16,4096]{2,1,0:T(8,128)(2,1)} %param.44) | copy-start | bytes 393220
  15.0 4.7 %copy-start.2 = (bf16[1,256,768]{2,1,0:T(8,128)(2,1)S(1)}, bf16[1,256,768]{2,1,0:T(8,128)(2,1)}, u32[]{:S(2)}) copy-start(bf16[1,256,768]{2,1,0:T(8,128)(2,1)} %param.42) | copy-start | bytes 1179652
  15.0 4.7 %copy-start.13 = (bf16[1,16,768]{2,1,0:T(8,128)(2,1)S(1)}, bf16[1,16,768]{2,1,0:T(8,128)(2,1)}, u32[]{:S(2)}) copy-start(bf16[1,16,768]{2,1,0:T(8,128)(2,1)} %param.46) | copy-start | bytes 73732
  16.1 4.4 copy-start.7
  16.1 4.4 copy-start.16
  16.1 4.4 copy-start.23
  16.1 5.0 %copy-start.8 = (bf16[1,256,128]{2,1,0:T(8,128)(2,1)S(1)}, bf16[1,256,128]{2,1,0:T(8,128)(2,1)}, u32[]{:S(2)}) copy-start(bf16[1,256,128]{2,1,0:T(8,128)(2,1)} %param.45) | copy-start | bytes 196612
  16.1 5.0 %copy-start.14 = (bf16[1,96,128]{2,1,0:T(8,128)(2,1)S(1)}, bf16[1,96,128]{2,1,0:T(8,128)(2,1)}, u32[]{:S(2)}) copy-start(bf16[1,96,128]{2,1,0:T(8,128)(2,1)} %param.43) | copy-start | bytes 73732
  16.3 5.5 %copy-start.11 = (bf16[24,768]{1,0:T(8,128)(2,1)S(1)}, bf16[24,768]{1,0:T(8,128)(2,1)}, u32[]{:S(2)}) copy-start(bf16[24,768]{1,0:T(8,128)(2,1)} %param.32) | copy-start | bytes 110596
  16.3 5.5 %copy-start.24 = (bf16[4,768]{1,0:T(4,128)(2,1)S(1)}, bf16[4,768]{1,0:T(4,128)(2,1)}, u32[]{:S(2)}) copy-start(bf16[4,768]{1,0:T(4,128)(2,1)} %param.36) | copy-start | bytes 18436
  16.3 5.5 %copy-start.25 = (bf16[24,128]{1,0:T(8,128)(2,1)S(1)}, bf16[24,128]{1,0:T(8,128)(2,1)}, u32[]{:S(2)}) copy-start(bf16[24,128]{1,0:T(8,128)(2,1)} %param.35) | copy-start | bytes 18436
  184.4 118.3 %copy-start.26 = (bf16[2,768]{1,0:T(2,128)(2,1)S(1)}, bf16[2,768]{1,0:T(2,128)(2,1)}, u32[]{:S(2)}) copy-start(bf16[2,768]{1,0:T(2,128)(2,1)} %param.40) | copy-start | bytes 9220
  335.6 53.3 %copy-start.15 = (s32[1,1280]{1,0:T(1,128)S(1)}, s32[1,1280]{1,0:T(1,128)}, u32[]{:S(2)}) copy-start(s32[1,1280]{1,0:T(1,128)} %place_row.1) | copy-start | bytes 15364
  443.3 3.2 copy-start.19
  443.4 3.8 copy-start.18
  443.4 4.4 copy-start.10
  443.4 5.0 %copy-start.3 = (f32[16,4096]{1,0:T(8,128)S(1)}, f32[16,4096]{1,0:T(8,128)}, u32[]{:S(2)}) copy-start(f32[16,4096]{1,0:T(8,128)} %get-tuple-element.108) | copy-start | bytes 786436
  443.4 5.7 %copy-start.6 = (f32[256,128]{1,0:T(8,128)S(1)}, f32[256,128]{1,0:T(8,128)}, u32[]{:S(2)}) copy-start(f32[256,128]{1,0:T(8,128)} %get-tuple-element.109) | copy-start | bytes 393220
  443.4 6.4 %copy-start.9 = (f32[16,768]{1,0:T(8,128)S(1)}, f32[16,768]{1,0:T(8,128)}, u32[]{:S(2)}) copy-start(f32[16,768]{1,0:T(8,128)} %get-tuple-element.110) | copy-start | bytes 147460
  (5 other events, 12.5 us)
